TPU v7x, 32 devices: a whole 2x2x4 slice. The times are simulated.
32 devices in a mesh: groups: 2 (over y), sector: 4 (over z), block: 2 (over x), rep: 2 (over core).
Axes of the slice: x: 2, y: 2, z: 4, core: 2. Of those that a mesh axis runs over, the one named last changes fastest.
Arguments:
- corner: bfloat16 [8, 512, 4096], P(('groups', 'sector'), 'block', 'rep'), parts along dimension 0, may hold values from -6 to 6
- site: bfloat16 [16, 512, 128], P('groups'), parts along dimension 0, may hold values from -0.03125 to 0.03125
- projector: bfloat16 [8, 128, 128], P(('groups', 'sector')), parts along dimension 0, may hold values from -0.5 to 0.5
- cotangent: bfloat16 [8, 512, 128], P(('groups', 'sector'), 'block'), parts along dimension 0, may hold values from -6 to 6
- sector_dim: int32 [8], P(('groups', 'sector')), parts along dimension 0, may hold values from 32 to 128, as said below
- pair_dest: int32 [1024], P(('groups', 'sector', 'rep')), parts along dimension 0, may hold values from 0 to 3
- pair_sub: int32 [1024], P(('groups', 'sector', 'rep')), parts along dimension 0, may hold values from 0 to 3
- pair_site: int32 [1024], P(('groups', 'sector', 'rep')), parts along dimension 0, may hold values from 0 to 7
Outputs:
- corner_new: bfloat16 [8, 512, 128], P(('groups', 'sector'), 'block'), parts along dimension 0
- corner_grad: bfloat16 [8, 512, 4096], P(('groups', 'sector'), 'block', 'rep'), parts along dimension 0
- site_grad: float32 [16, 512, 128], P('groups', 'sector'), parts along dimension 0
There are 2 independent parts, one for each index of `groups`. A program takes and returns all parts, laid end to end along the dimension named above; each array names one. Nothing has to cross between parts.
Inputs may be any that keep to these rules, and one draw needn't show every extreme that they name: `sector_dim`: one sector in every draw keeps all 128 states.
All inputs are finite; a program needn't handle non-finite values.
Results may differ from a plain program's by a relative error of at most 0.008.
Values may be sent and summed in bfloat16 or wider, within the bound.
No kernel may reach another device: no remote copies, remote signals or barrier semaphores. Data moves between devices by JAX's collectives and lax.ppermute only.
A program may use at most 64 MiB of HBM per device.

v0:
```python
import jax
import jax.numpy as jnp
from jax import lax
from jax.sharding import PartitionSpec as P


def per_device(corner, site, projector, cotangent, sector_dim, pair_dest, pair_sub, pair_site):
    highest = lax.Precision.HIGHEST
    owners = lax.axis_size("sector")
    row_count = corner.shape[1]
    sub_width = site.shape[1]
    site_blocks = site.shape[0]
    chi_width = site.shape[2]
    local_subs = corner.shape[2] // sub_width
    combos = local_subs * site_blocks
    dest_hot = (pair_dest[:, None] == jnp.arange(owners, dtype=jnp.int32)[None, :]).astype(
        jnp.float32
    )
    combo_index = pair_sub * site_blocks + pair_site
    combo_hot = (combo_index[:, None] == jnp.arange(combos, dtype=jnp.int32)[None, :]).astype(
        jnp.float32
    )
    counts = jnp.dot(dest_hot.T, combo_hot, precision=highest, preferred_element_type=jnp.float32)
    slices = corner[0].reshape(row_count, local_subs, sub_width)
    products = jnp.einsum("rki,gic->kgrc", slices, site, preferred_element_type=jnp.float32)
    products = products.reshape(combos, row_count, chi_width)
    partial_value = jnp.einsum("bq,qrc->brc", counts, products, precision=highest)
    live_cols = (jnp.arange(chi_width, dtype=jnp.int32) < sector_dim[0]).astype(jnp.bfloat16)
    summed = lax.psum(partial_value, "rep")
    arrived = lax.all_to_all(
        summed.astype(jnp.bfloat16), "sector", split_axis=0, concat_axis=0, tiled=True
    )
    enlarged = jnp.sum(arrived.astype(jnp.float32), axis=0).astype(jnp.bfloat16)
    projected = jnp.dot(enlarged, projector[0], preferred_element_type=jnp.float32)
    projected = (projected * live_cols.astype(jnp.float32)).astype(jnp.bfloat16)
    corner_new = projected[None]
    masked = cotangent[0] * live_cols
    grad_enlarged = jnp.dot(masked, projector[0].T, preferred_element_type=jnp.float32).astype(
        jnp.bfloat16
    )
    shared = lax.all_gather(grad_enlarged[None], "sector", axis=0, tiled=True)
    pulled = jnp.einsum(
        "bq,brc->qrc", counts, shared.astype(jnp.float32), precision=highest
    ).astype(jnp.bfloat16)
    pulled = pulled.reshape(local_subs, site_blocks, row_count, chi_width)
    grad_cols = jnp.einsum("kgrc,gic->rki", pulled, site, preferred_element_type=jnp.float32)
    corner_grad = grad_cols.astype(jnp.bfloat16).reshape(1, row_count, local_subs * sub_width)
    site_part = jnp.einsum("rki,kgrc->gic", slices, pulled, preferred_element_type=jnp.float32)
    site_rows = lax.psum_scatter(site_part, "sector", scatter_dimension=1, tiled=True)
    site_grad = lax.psum(site_rows, ("block", "rep"))
    return (corner_new, corner_grad, site_grad)


def solution(mesh):
    in_specs = (
        P(("groups", "sector"), "block", "rep"),
        P("groups", None, None),
        P(("groups", "sector"), None, None),
        P(("groups", "sector"), "block", None),
        P(("groups", "sector")),
        P(("groups", "sector", "rep")),
        P(("groups", "sector", "rep")),
        P(("groups", "sector", "rep")),
    )
    out_specs = (
        P(("groups", "sector"), "block", None),
        P(("groups", "sector"), "block", "rep"),
        P("groups", "sector", None),
    )
    return jax.shard_map(
        per_device, mesh=mesh, in_specs=in_specs, out_specs=out_specs, check_vma=False
    )
```

profile of v0, /device:TPU:0, one launch (start us, length us, event | category | flops | bytes accessed | tf_op | source)
XLA Modules:
  0.0 126.7 jit_solution(693063030216031139)
XLA Ops:
  7.2 0.0 copy-start
  7.2 0.0 copy-start.3
  7.2 0.0 copy-start.4
  7.2 0.0 copy-start.5
  7.2 0.0 copy-start.6
  7.2 0.0 copy-start.7
  7.2 0.0 reduce-scatter.2.cloned.1.call-start
  7.3 1.9 %reshape_squeeze.3 = bf16[256,4,512]{2,1,0:T(4,128)(2,1)S(1)} reshape(bf16[1,256,2048]{2,1,0:T(8,128)(2,1)} %param.8) | data formatting | bytes 2097152 | tf_op jit(solution)/shard_map/reshape;squeeze | solution.py:24
  9.9 0.0 copy-done.3
  9.9 0.0 copy-done.4
  9.9 0.2 convolution_convert_fusion
  10.1 15.6 %all-gather = bf16[1024,128]{1,0:T(8,128)(2,1)S(1)} all-gather(bf16[256,128]{1,0:T(8,128)(2,1)S(1)} %convolution_convert_fusion), channel_id=2, replica_groups=mesh['groups'=2,'sector'=4,'block'=2,'rep'=2] {'sector'}, dimensions={0}, use_global_device_ids=true | all-gather | bytes 327680 | tf_op jit(solution)/shard_map/all_gather | solution.py:41
  25.7 0.0 copy-done.5
  25.7 0.0 copy-done.6
  25.7 0.0 copy-done.7
  25.7 0.2 convolution_bitcast_fusion.1
  26.0 2.7 %convert_bitcast_fusion = bf16[4,8,256,128]{3,1,0,2:T(8,128)(2,1)S(1)} fusion(f32[4,32,1]{1,0,2:T(4,128)S(1)} %convolution_bitcast_fusion.1, bf16[4,256,128]{2,1,0:T(8,128)(2,1)S(1)} %bitcast.53), kind=kOutput, calls=%fused_computation.8 | convolution fusion | flops 51380224 | bytes 2359808 | tf_op jit(solution)/shard_map/bq,brc->qrc/dot_general | solution.py:42
  28.7 0.0 copy-start.1
  28.7 1.3 %copy-done.1 = bf16[4,8,256,128]{3,1,0,2:T(8,128)(2,1)} copy-done((bf16[4,8,256,128]{3,1,0,2:T(8,128)(2,1)}, bf16[4,8,256,128]{3,1,0,2:T(8,128)(2,1)S(1)}, u32[]{:S(2)}) %copy-start.1) | copy-done | bytes 2097176
  30.0 3.0 %fusion.6 = f32[8,512,128]{1,2,0:T(8,128)} fusion(bf16[4,8,256,128]{3,1,0,2:T(8,128)(2,1)S(1)} %convert_bitcast_fusion, bf16[256,4,512]{2,1,0:T(4,128)(2,1)S(1)} %reshape_squeeze.3), kind=kOutput, calls=%fused_computation.9 | convolution fusion | flops 1073741824 | bytes 5242880 | tf_op jit(solution)/shard_map/rki,kgrc->gic/dot_general | solution.py:48
  33.0 0.0 reduce-scatter.2.cloned.1.call-update
  33.0 0.0 copy-done
  33.1 3.2 %convolution_bitcast_fusion = f32[4,8,256,128]{2,3,0,1:T(8,128)} fusion(bf16[8,512,128]{2,1,0:T(8,128)(2,1)S(1)} %copy-done, bf16[256,4,512]{2,1,0:T(4,128)(2,1)S(1)} %reshape_squeeze.3), kind=kOutput, calls=%fused_computation.2 | convolution fusion | flops 1073741824 | bytes 6291456 | tf_op jit(solution)/shard_map/rki,gic->kgrc/dot_general | solution.py:25
  36.3 5.4 %copy.42 = f32[4,8,256,128]{3,2,1,0:T(8,128)} copy(f32[4,8,256,128]{2,3,0,1:T(8,128)} %convolution_bitcast_fusion) | data formatting | bytes 8388608 | tf_op jit(solution)/shard_map/rki,gic->kgrc/transpose | solution.py:25
  41.7 7.2 %fusion = f32[4,256,128]{2,0,1:T(4,128)} fusion(f32[4,32,1]{1,0,2:T(4,128)S(1)} %convolution_bitcast_fusion.1, f32[32,256,128]{2,1,0:T(8,128)} %bitcast.51), kind=kOutput, calls=%fused_computation | convolution fusion | flops 50331648 | bytes 4719104 | tf_op jit(solution)/shard_map/bq,qrc->brc/dot_general | solution.py:27
  48.9 0.0 copy-start.2
  48.9 5.7 %all-reduce.4 = bf16[4,256,128]{2,0,1:T(4,128)(2,1)S(1)} all-reduce(f32[4,256,128]{2,0,1:T(4,128)} %fusion), channel_id=1, replica_groups=mesh['groups'=2,'sector'=4,'block'=2,'rep'=2] {'rep'}, use_global_device_ids=true, to_apply=%region_0.0 | all-reduce | flops 131072 | bytes 786432 | tf_op jit(solution)/shard_map/psum | solution.py:29
  54.6 0.7 copy.44
  55.3 5.2 %all-to-all-start = ((bf16[4,256,128]{2,1,0:T(8,128)(2,1)}), bf16[4,256,128]{2,1,0:T(8,128)(2,1)S(1)}, u32[]{:S(2)}, u32[]{:S(2)}) async-start(bf16[4,256,128]{2,1,0:T(8,128)(2,1)} %copy.44), calls=%async_computation | async-start | bytes 524288 | tf_op jit(solution)/shard_map/all_to_all | solution.py:30
  60.5 0.0 all-reduce.3.cloned.1.call-start
  60.5 22.3 %reduce-scatter.2.cloned.1.call-done = f32[8,128,128]{1,2,0:T(8,128)} async-done(((f32[8,512,128]{1,2,0:T(8,128)}), f32[8,128,128]{1,2,0:T(8,128)}) %reduce-scatter.2.cloned.1.call-update) | async-done | bytes 524304 | tf_op jit(solution)/shard_map/reduce_scatter | solution.py:49
  82.8 0.0 all-reduce.3.cloned.1.call-update
  82.8 0.0 copy-done.2
  82.8 2.3 %fusion.11 = bf16[256,4,512]{2,0,1:T(8,128)(2,1)} fusion(bf16[4,8,256,128]{3,1,0,2:T(8,128)(2,1)S(1)} %copy-done.2, bf16[8,512,128]{2,1,0:T(8,128)(2,1)S(1)} %copy-done), kind=kOutput, calls=%fused_computation.10 | convolution fusion | flops 1074266112 | bytes 4194304 | tf_op jit(solution)/shard_map/kgrc,gic->rki/dot_general | solution.py:46
  85.1 1.5 %copy.47 = bf16[256,4,512]{0,2,1:T(8,128)(2,1)S(1)} copy(bf16[256,4,512]{2,0,1:T(8,128)(2,1)} %fusion.11) | data formatting | bytes 2097152 | tf_op jit(solution)/shard_map/convert_element_type | solution.py:47
  86.6 1.4 %copy.50 = bf16[1,256,2048]{2,1,0:T(8,128)(2,1)} copy(bf16[1,256,2048]{1,2,0:T(8,128)(2,1)S(1)} %bitcast.52) | data formatting | bytes 2097152
  88.0 0.0 all-to-all-done
  88.0 0.8 fusion.15
  88.8 29.0 %all-reduce.3.cloned.1.call-done = f32[8,128,128]{1,2,0:T(8,128)} async-done(((f32[8,128,128]{1,2,0:T(8,128)}), f32[8,128,128]{1,2,0:T(8,128)}) %all-reduce.3.cloned.1.call-update) | async-done | bytes 524304 | tf_op jit(solution)/shard_map/psum | solution.py:50
  117.8 2.0 %copy.51 = f32[8,128,128]{2,1,0:T(8,128)} copy(f32[8,128,128]{1,2,0:T(8,128)} %all-reduce.3.cloned.1.call-done) | data formatting | bytes 1048576
  (4 shorter events, 0.1 us)
Async XLA Ops:
  7.2 25.9 %copy-start = (bf16[8,512,128]{2,1,0:T(8,128)(2,1)S(1)}, bf16[8,512,128]{2,1,0:T(8,128)(2,1)}, u32[]{:S(2)}) copy-start(bf16[8,512,128]{2,1,0:T(8,128)(2,1)} %param.9) | copy-start | bytes 3145732
  7.2 2.7 %copy-start.3 = (bf16[1,128,128]{2,1,0:T(8,128)(2,1)S(1)}, bf16[1,128,128]{2,1,0:T(8,128)(2,1)}, u32[]{:S(2)}) copy-start(bf16[1,128,128]{2,1,0:T(8,128)(2,1)} %param.10) | copy-start | bytes 98308
  7.2 2.7 %copy-start.4 = (bf16[1,256,128]{2,1,0:T(8,128)(2,1)S(1)}, bf16[1,256,128]{2,1,0:T(8,128)(2,1)}, u32[]{:S(2)}) copy-start(bf16[1,256,128]{2,1,0:T(8,128)(2,1)} %param.11) | copy-start | bytes 196612
  7.2 18.5 %copy-start.5 = (s32[64]{0:T(128)S(1)}, s32[64]{0:T(128)}, u32[]{:S(2)}) copy-start(s32[64]{0:T(128)} %param.15) | copy-start | bytes 772
  7.2 18.5 %copy-start.6 = (s32[64]{0:T(128)S(1)}, s32[64]{0:T(128)}, u32[]{:S(2)}) copy-start(s32[64]{0:T(128)} %param.14) | copy-start | bytes 772
  7.2 18.5 %copy-start.7 = (s32[64]{0:T(128)S(1)}, s32[64]{0:T(128)}, u32[]{:S(2)}) copy-start(s32[64]{0:T(128)} %param.13) | copy-start | bytes 772
  7.2 75.6 %reduce-scatter.2.cloned.1.call-start = ((), (), s32[]{:S(2)}) async-start(), calls=%async_computation.2 | async-start | bytes 2621440 | tf_op jit(solution)/shard_map/reduce_scatter | solution.py:49
  28.7 1.4 %copy-start.1 = (bf16[4,8,256,128]{3,1,0,2:T(8,128)(2,1)}, bf16[4,8,256,128]{3,1,0,2:T(8,128)(2,1)S(1)}, u32[]{:S(2)}) copy-start(bf16[4,8,256,128]{3,1,0,2:T(8,128)(2,1)S(1)} %convert_bitcast_fusion) | copy-start | bytes 6291460
  48.9 34.0 %copy-start.2 = (bf16[4,8,256,128]{3,1,0,2:T(8,128)(2,1)S(1)}, bf16[4,8,256,128]{3,1,0,2:T(8,128)(2,1)}, u32[]{:S(2)}) copy-start(bf16[4,8,256,128]{3,1,0,2:T(8,128)(2,1)} %copy-done.1) | copy-start | bytes 6291460
  55.3 32.7 %all-to-all-start = ((bf16[4,256,128]{2,1,0:T(8,128)(2,1)}), bf16[4,256,128]{2,1,0:T(8,128)(2,1)S(1)}, u32[]{:S(2)}, u32[]{:S(2)}) async-start(bf16[4,256,128]{2,1,0:T(8,128)(2,1)} %copy.44), calls=%async_computation | async-start | bytes 524288 | tf_op jit(solution)/shard_map/all_to_all | solution.py:30
  60.5 57.3 %all-reduce.3.cloned.1.call-start = ((), (), s32[]{:S(2)}) async-start(), calls=%async_computation.3 | async-start | bytes 1048576 | tf_op jit(solution)/shard_map/psum | solution.py:50
Sparse Core Ops, SparseCore 0:
  33.2 49.5 reduce-scatter.1
  85.3 32.5 all-reduce.2
where the time goes:
time: 127 us
  waiting for transfers between devices  51.3 us (40%)
  blocking collectives  21.3 us (17%)
  matrix products  19.6 us (15%)
  between operations  14.8 us (12%)
  local copies, waits for them, and re-layouts  14.3 us (11%)
  starting transfers between devices  5.22 us (4%)
    psum x1, waiting for transfers between devices, per_device(): site_grad = lax.psum(site_rows, ('block', 'rep'))  29 us
    reduce_scatter x1, waiting for transfers between devices, per_device(): lax.psum_scatter(site_part, 'sector', scatter_dimension=1, tiled=True)  22.3 us
    all_gather x1, blocking collectives, per_device(): shared = lax.all_gather(grad_enlarged[None], 'sector', axis=0, tiled=True)  15.6 us
    dot_general x1, matrix products, per_device(): jnp.einsum('bq,qrc->brc', counts, products, precision=highest)  7.2 us
    psum x1, blocking collectives, per_device(): summed = lax.psum(partial_value, 'rep')  5.72 us
    transpose x1, local copies, waits for them, and re-layouts, per_device(): jnp.einsum('rki,gic->kgrc', slices, site, preferred_element_type=jnp.floa...  5.36 us
    all_to_all x1, starting transfers between devices, per_device(): lax.all_to_all(summed.astype(jnp.bfloat16), 'sector', split_axis=0, conca...  5.18 us
    unnamed x18, local copies, waits for them, and re-layouts  4.84 us
  transfers between devices with their start and end apart: 3, of which 2 were waited for; matrix products, arithmetic and copies ran while one was open for 18% of the time, Pallas kernels for 0%

commit v1 on v0

v1 whole, which is shorter than its diff:
```python
import functools
import jax
import jax.numpy as jnp
from jax import lax
from jax.experimental import pallas as pl
from jax.experimental.pallas import tpu as pltpu
from jax.sharding import PartitionSpec as P

F32 = jnp.float32
BF16 = jnp.bfloat16
NT = (((1,), (1,)), ((), ()))
VMEM = pl.BlockSpec(memory_space=pltpu.VMEM)
LIMIT = 40 * 1024 * 1024


def swap(value, axis, bit):
    size = lax.axis_size(axis)
    return lax.ppermute(value, axis, [(place, place ^ bit) for place in range(size)])


def total(*terms):
    acc = terms[0].astype(F32)
    for term in terms[1:]:
        acc = acc + term.astype(F32)
    return acc


def call(kernel, outs, args, scratch=(), flops=0):
    moved = sum(a.size * a.dtype.itemsize for a in args) + sum(
        a.size * a.dtype.itemsize for a in outs
    )
    return pl.pallas_call(
        kernel,
        out_shape=list(outs),
        in_specs=[VMEM] * len(args),
        out_specs=[VMEM] * len(outs),
        scratch_shapes=list(scratch),
        compiler_params=pltpu.CompilerParams(vmem_limit_bytes=LIMIT),
        cost_estimate=pl.CostEstimate(flops=flops, bytes_accessed=moved, transcendentals=0),
    )(*args)


def count_of(table, index, height, width):
    row = table[pl.ds(index, 1), :]
    wide = jnp.concatenate([row] * (width // row.shape[1]), axis=1)
    return jnp.broadcast_to(wide, (height, width))


def forward_kernel(owners, subs, blocks, x_ref, y_ref, site_ref, table_ref, *outs):
    rows, chi = outs[0].shape
    width = site_ref.shape[1]
    stacked = jnp.concatenate(
        [ref[:, sub * width : (sub + 1) * width] for ref in (x_ref, y_ref) for sub in range(subs)],
        axis=0,
    )
    accs = [jnp.zeros((rows, chi), F32) for _ in range(owners)]
    for block in range(0, blocks, 2):
        pair = jnp.concatenate([site_ref[block], site_ref[block + 1]], axis=1)
        product = jnp.dot(stacked, pair, preferred_element_type=F32)
        for sub in range(2 * subs):
            for offset in range(2):
                piece = product[sub * rows : (sub + 1) * rows, offset * chi : (offset + 1) * chi]
                for owner in range(owners):
                    index = (owner * 2 * subs + sub) * blocks + block + offset
                    accs[owner] = accs[owner] + piece * count_of(table_ref, index, rows, chi)
    for owner in range(owners):
        outs[owner][...] = accs[owner].astype(outs[owner].dtype)


def pulled_of(grads, table_ref, owners, subs, blocks, sub, block):
    value = None
    for owner in range(owners):
        index = (owner * 2 * subs + sub) * blocks + block
        term = grads[owner] * count_of(table_ref, index, *grads[owner].shape)
        value = term if value is None else value + term
    return value.astype(BF16)


def site_kernel(
    owners, subs, blocks, mine, place_ref, x_ref, y_ref, table_ref, *refs
):
    grads = [ref[...].astype(F32) for ref in refs[:owners]]
    acc, outs = refs[-1], refs[owners:-1]
    chi = grads[0].shape[0]
    width = acc.shape[1]
    for sub in range(2 * subs):
        source = x_ref if sub < subs else y_ref
        low = (sub % subs) * width
        left = jnp.concatenate(
            [
                pulled_of_dyn(grads, table_ref, owners, subs, blocks, sub, place_ref[0] + at)
                for at in range(mine)
            ],
            axis=0,
        )
        product = jnp.dot(left, source[:, low : low + width], preferred_element_type=F32)
        if sub == 0:
            acc[...] = product
        else:
            acc[...] += product
    if len(outs) == 1:
        outs[0][...] = acc[...]
        return
    half = mine // 2
    chunk = width // owners
    sends, kept, crossing, staying = outs[: owners - 1], outs[owners - 1], outs[-2], outs[-1]
    share = crossing.shape[1]
    for rel in range(owners):
        lanes = pl.ds(pl.multiple_of(place_ref[1 + rel] * chunk, chunk), chunk)
        out = kept if rel == 0 else sends[rel - 1]
        out[...] = acc[: half * chi, lanes].astype(out.dtype)
        for out, first in ((crossing, place_ref[owners + 2]), (staying, place_ref[owners + 1])):
            rows = pl.ds(pl.multiple_of(half * chi + first * share, share), share)
            out[rel] = acc[rows, lanes].astype(out.dtype)


def pulled_of_dyn(grads, table_ref, owners, subs, blocks, sub, block):
    value = None
    for owner in range(owners):
        index = (owner * 2 * subs + sub) * blocks + block
        term = grads[owner] * count_of(table_ref, index, *grads[owner].shape)
        value = term if value is None else value + term
    return value.astype(BF16)


def corner_kernel(owners, subs, blocks, site_ref, table_ref, *refs):
    grads = [ref[...].astype(F32).T for ref in refs[:owners]]
    out = refs[owners]
    rows = grads[0].shape[0]
    width = site_ref.shape[1]
    wide = jnp.concatenate([site_ref[block] for block in range(blocks)], axis=1)
    for sub in range(subs):
        left = jnp.concatenate(
            [pulled_of(grads, table_ref, owners, subs, blocks, sub, block) for block in range(blocks)],
            axis=1,
        )
        value = lax.dot_general(left, wide, NT, preferred_element_type=F32)
        out[:, sub * width : (sub + 1) * width] = value.astype(out.dtype)


def per_device(corner, site, projector, cotangent, sector_dim, pair_dest, pair_sub, pair_site):
    owners = lax.axis_size("sector")
    sides = lax.axis_size("block")
    me, side, rep = lax.axis_index("sector"), lax.axis_index("block"), lax.axis_index("rep")
    blocks, width, chi = site.shape
    rows = corner.shape[1]
    subs = corner.shape[2] // width
    direct = owners <= 4 and sides == 2
    flat = corner[0]

    other = swap(flat, "rep", 1)
    pairs = jnp.stack([pair_dest, pair_sub, pair_site])
    far = swap(pairs, "rep", 1)

    live = (jnp.arange(chi, dtype=jnp.int32) < sector_dim[0]).astype(BF16)
    grad = lax.dot_general(
        projector[0], cotangent[0] * live, NT, preferred_element_type=F32
    ).astype(BF16)
    if direct:
        grads = [grad] + [swap(grad, "sector", bit) for bit in range(1, owners)]
    else:
        shared = lax.all_gather(grad, "sector", axis=0)
        grads = [shared[owner] for owner in range(owners)]

    def rows_of(lists, first):
        dest = lists[0] ^ me if direct else lists[0]
        return (dest * 2 * subs + first + lists[1]) * blocks + lists[2]

    index = jnp.concatenate([rows_of(pairs, 0), rows_of(far, subs)])
    hits = (
        jnp.arange(owners * 2 * subs * blocks, dtype=jnp.int32)[:, None] == index[None, :]
    ).astype(BF16)
    table = jnp.dot(hits, jnp.ones((index.shape[0], 128), BF16), preferred_element_type=F32)

    part = rows // 2
    mine_x = lax.dynamic_slice_in_dim(flat, rep * part, part, 0)
    other_x = lax.dynamic_slice_in_dim(other, rep * part, part, 0)
    partials = call(
        functools.partial(forward_kernel, owners, subs, blocks),
        [jax.ShapeDtypeStruct((part, chi), BF16)] * owners,
        [mine_x, other_x, site, table],
        flops=4 * subs * part * width * chi * blocks,
    )
    if direct:
        arrived = [partials[0]] + [
            swap(partials[bit], "sector", bit) for bit in range(1, owners)
        ]
    else:
        arrived = list(
            lax.all_to_all(jnp.stack(partials), "sector", split_axis=0, concat_axis=0, tiled=True)
        )
    enlarged = total(*arrived).astype(BF16)
    projected = jnp.dot(enlarged, projector[0], preferred_element_type=F32)
    projected = (projected * live.astype(F32)).astype(BF16)

    mine = blocks // 2
    half = mine // 2
    place = jnp.stack(
        [rep * mine] + [me ^ rel for rel in range(owners)] + [side, 1 - side]
    ).astype(jnp.int32)
    if direct:
        chunk = width // owners
        share = half * chi // sides
        outs = [jax.ShapeDtypeStruct((half * chi, chunk), BF16)] * owners
        outs += [jax.ShapeDtypeStruct((owners, share, chunk), BF16)] * 2
    else:
        outs = [jax.ShapeDtypeStruct((mine * chi, width), F32)]
    args = [place, flat, other, table] + grads
    pieces = pl.pallas_call(
        functools.partial(site_kernel, owners, subs, blocks, mine),
        out_shape=outs,
        in_specs=[pl.BlockSpec(memory_space=pltpu.SMEM)] + [VMEM] * (len(args) - 1),
        out_specs=[VMEM] * len(outs),
        scratch_shapes=[pltpu.VMEM((mine * chi, width), F32)],
        compiler_params=pltpu.CompilerParams(vmem_limit_bytes=LIMIT),
        cost_estimate=pl.CostEstimate(
            flops=4 * subs * rows * width * chi * mine, bytes_accessed=1 << 22, transcendentals=0
        ),
    )(*args)
    if direct:
        crossing, staying = pieces[owners], pieces[owners + 1]
        crossed = swap(crossing, "block", 1)
        first = [pieces[owners - 1]] + [
            swap(pieces[bit - 1], "sector", bit) for bit in range(owners - 1, 0, -1)
        ]
        merged = total(staying, crossed).astype(BF16)
        second = [merged[0]] + [swap(merged[bit], "sector", bit) for bit in range(owners - 1, 0, -1)]
        upper = total(*first).astype(BF16)
        upper = total(upper, swap(upper, "block", 1)).astype(BF16)
        lower = total(*second).astype(BF16)
        beside = swap(lower, "block", 1)
        lower = jnp.where(
            side == 0, jnp.concatenate([lower, beside]), jnp.concatenate([beside, lower])
        )
        own = jnp.concatenate([upper, lower, projected], axis=0)
        there = swap(own, "rep", 1)
        both = jnp.where(rep == 0, jnp.stack([own, there]), jnp.stack([there, own]))
        site_grad = both[:, : mine * chi].reshape(blocks, chi, chunk).swapaxes(1, 2).astype(F32)
        corner_new = both[:, mine * chi :].reshape(1, rows, chi)
    else:
        term = pieces[0].astype(BF16).reshape(mine, chi, width)
        term = lax.psum_scatter(term, "sector", scatter_dimension=2, tiled=True)
        term = lax.psum(term, "block")
        gathered = lax.all_gather(term, "rep", axis=0, tiled=True)
        site_grad = gathered.swapaxes(1, 2).astype(F32)
        corner_new = lax.all_gather(projected, "rep", axis=0, tiled=True)[None]

    corner_grad = call(
        functools.partial(corner_kernel, owners, subs, blocks),
        [jax.ShapeDtypeStruct((rows, subs * width), BF16)],
        [site, table] + grads,
        flops=2 * subs * rows * width * chi * blocks,
    )[0][None]
    return (corner_new, corner_grad, site_grad)


def solution(mesh):
    in_specs = (
        P(("groups", "sector"), "block", "rep"),
        P("groups", None, None),
        P(("groups", "sector"), None, None),
        P(("groups", "sector"), "block", None),
        P(("groups", "sector")),
        P(("groups", "sector", "rep")),
        P(("groups", "sector", "rep")),
        P(("groups", "sector", "rep")),
    )
    out_specs = (
        P(("groups", "sector"), "block", None),
        P(("groups", "sector"), "block", "rep"),
        P("groups", "sector", None),
    )
    return jax.shard_map(
        per_device, mesh=mesh, in_specs=in_specs, out_specs=out_specs, check_vma=False
    )
```

time: 127 us -> 47.2 us (0.37)
  waiting for transfers between devices: 51.3 us -> 9.02 us
  blocking collectives: 21.3 us -> 0 us
  starting transfers between devices: 5.22 us -> 24.6 us
  matrix products: 19.6 us -> 1.29 us
  between operations: 14.8 us -> 1.49 us
  local copies, waits for them, and re-layouts: 14.3 us -> 3.69 us
  Pallas kernels: 0 us -> 6.48 us
    psum x1 -> x0, waiting for transfers between devices: 29 us -> none  [per_device(): site_grad = lax.psum(site_rows, ('block', 'rep'))]
    ppermute x0 -> x18, starting transfers between devices: none -> 24.6 us  [swap(): lax.ppermute(value, axis, [(place, place ^ bit) for place in range(size)])]
    reduce_scatter x1 -> x0, waiting for transfers between devices: 22.3 us -> none  [per_device(): lax.psum_scatter(site_part, 'sector', scatter_dimension=1, tiled=True)]
    dot_general x8 -> x3, matrix products: 19.6 us -> 1.29 us  [the longest x1 1 us: per_device(): lax.dot_general(projector[0], cotangent[0] * live, NT, preferred_element_...]
    all_gather x1 -> x0, blocking collectives: 15.6 us -> none  [per_device(): shared = lax.all_gather(grad_enlarged[None], 'sector', axis=0, tiled=True)]
    ppermute x0 -> x18, waiting for transfers between devices: none -> 9.02 us  [swap(): lax.ppermute(value, axis, [(place, place ^ bit) for place in range(size)])]
    pallas_call x0 -> x3, Pallas kernels: none -> 6.48 us  [the longest x2 4.41 us: call(): pl.pallas_call(kernel, out_shape=list(outs), in_specs=[VMEM] * len(args),...]
    psum x1 -> x0, blocking collectives: 5.72 us -> none  [per_device(): summed = lax.psum(partial_value, 'rep')]
  transfers between devices with their start and end apart: 3 -> 18, of which waited for: 2 -> 4; matrix products, arithmetic and copies ran while one was open for 18% -> 4% of each run, Pallas kernels for 0% -> 14%
where the time goes in v1:
time: 47.2 us; the launch traced here: 46.9 us
  starting transfers between devices  24.6 us (52%)
  waiting for transfers between devices  9.02 us (19%)
  Pallas kernels  6.48 us (14%)
  local copies, waits for them, and re-layouts  3.69 us (8%)
  between operations  1.49 us (3%)
  matrix products  1.29 us (3%)
    ppermute x18, starting transfers between devices, swap(): lax.ppermute(value, axis, [(place, place ^ bit) for place in range(size)])  24.6 us
    ppermute x18, waiting for transfers between devices, swap(): lax.ppermute(value, axis, [(place, place ^ bit) for place in range(size)])  9.02 us
    pallas_call x2, Pallas kernels, call(): pl.pallas_call(kernel, out_shape=list(outs), in_specs=[VMEM] * len(args),...  4.41 us
    pallas_call x1, Pallas kernels, per_device(): pl.pallas_call(functools.partial(site_kernel, owners, subs, blocks, mine)...  2.08 us
    dynamic_slice x1, local copies, waits for them, and re-layouts, per_device(): mine_x = lax.dynamic_slice_in_dim(flat, rep * part, part, 0)  1.17 us
    dot_general x1, matrix products, per_device(): lax.dot_general(projector[0], cotangent[0] * live, NT, preferred_element_...  1 us
  transfers between devices with their start and end apart: 18, of which 4 were waited for; matrix products, arithmetic and copies ran while one was open for 4% of the time, Pallas kernels for 14%

profile of v1, /device:TPU:0, one launch (start us, length us, event | category | flops | bytes accessed | tf_op | source)
XLA Modules:
  0.0 46.9 jit_solution(10780291290240082907)
XLA Ops:
  0.6 0.0 copy-start
  1.3 0.1 copy-done
  1.4 1.0 %fusion.refs_0_ = bf16[128,256]{1,0:T(8,128)(2,1)S(1)} fusion(bf16[1,256,128]{2,1,0:T(8,128)(2,1)} %param.11, bf16[1,128,128]{2,1,0:T(8,128)(2,1)S(1)} %copy-done, bf16[128]{0:T(256)(128)(2,1)S(1)} %compare_convert_fusion), kind=kOutput, calls=%fused_computation.1 | convolution fusion | flops 8454144 | bytes 164096 | tf_op jit(solution)/shard_map/dot_general | solution.py:156
  2.4 3.1 %collective-permute-start.2 = (bf16[128,256]{1,0:T(8,128)(2,1)S(1)}, bf16[128,256]{1,0:T(8,128)(2,1)S(1)}, u32[]{:S(2)}, u32[]{:S(2)}) collective-permute-start(bf16[128,256]{1,0:T(8,128)(2,1)S(1)} %fusion.refs_0_), channel_id=1, source_target_pairs={{0,4},{4,0},{8,12},{12,8},{1,5},{5,1},{9,13},{13,9},{2,6},{6,2},{1... | collective-permute-start | bytes 196616 | tf_op jit(solution)/shard_map/ppermute | solution.py:18
  5.5 2.6 %collective-permute-start.3 = (bf16[128,256]{1,0:T(8,128)(2,1)S(1)}, bf16[128,256]{1,0:T(8,128)(2,1)S(1)}, u32[]{:S(2)}, u32[]{:S(2)}) collective-permute-start(bf16[128,256]{1,0:T(8,128)(2,1)S(1)} %fusion.refs_0_), channel_id=1, source_target_pairs={{0,8},{4,12},{8,0},{12,4},{1,9},{5,13},{9,1},{13,5},{2,10},{6,14},... | collective-permute-start | bytes 196616 | tf_op jit(solution)/shard_map/ppermute | solution.py:18
  8.1 0.0 collective-permute-start.4
  8.1 0.0 copy-start.3
  8.1 0.0 copy-start.4
  8.1 0.0 copy-start.5
  8.1 0.6 %copy-done.3 = s32[64]{0:T(128)S(1)} copy-done((s32[64]{0:T(128)S(1)}, s32[64]{0:T(128)}, u32[]{:S(2)}) %copy-start.3) | copy-done | bytes 280
  8.8 0.0 copy-done.4
  8.8 0.0 copy-done.5
  8.8 0.1 collective-permute-start.1
  8.9 0.5 %collective-permute-start = (bf16[256,2048]{1,0:T(8,128)(2,1)}, bf16[256,2048]{1,0:T(8,128)(2,1)S(1)}, u32[]{:S(2)}, u32[]{:S(2)}) collective-permute-start(bf16[256,2048]{1,0:T(8,128)(2,1)} %bitcast.47), channel_id=1, source_target_pairs={{0,1},{1,0},{2,3},{3,2},{4,5},{5,4},{6,7},{7,6},{8,9},{9,8},{10,11... | collective-permute-start | bytes 3145736 | tf_op jit(solution)/shard_map/ppermute | solution.py:18
  9.4 0.0 copy-start.2
  9.4 1.2 %dynamic-slice_bitcast_fusion.x_ref = bf16[128,2048]{1,0:T(8,128)(2,1)S(1)} fusion(bf16[1,256,2048]{2,1,0:T(8,128)(2,1)} %param.8, s32[]{:T(128)S(6)} %select_n.23), kind=kLoop, calls=%fused_computation.4 | loop fusion | bytes 1048580 | tf_op jit(solution)/shard_map/dynamic_slice | solution.py:176
  10.6 0.1 stack.57.place_ref
  10.7 0.0 collective-permute-done.1
  10.7 0.1 pad_add_fusion.1
  10.8 0.2 fusion.2.table_ref
  10.9 1.0 %collective-permute-done.y_ref = bf16[256,2048]{1,0:T(8,128)(2,1)S(1)} collective-permute-done((bf16[256,2048]{1,0:T(8,128)(2,1)}, bf16[256,2048]{1,0:T(8,128)(2,1)S(1)}, u32[]{:S(2)}, u32[]{:S(2)}) %collective-permute-start) | collective-permute-done | bytes 1048608 | tf_op jit(solution)/shard_map/ppermute | solution.py:18
  11.9 0.0 copy-done.2
  11.9 0.0 copy-start.1
  11.9 2.0 %shard_map.104 = (bf16[128,128]{1,0:T(8,128)(2,1)S(1)}, bf16[128,128]{1,0:T(8,128)(2,1)S(1)}, bf16[128,128]{1,0:T(8,128)(2,1)S(1)}, bf16[128,128]{1,0:T(8,128)(2,1)S(1)}) custom-call(bf16[128,2048]{1,0:T(8,128)(2,1)S(1)} %dynamic-slice_bitcast_fusion.x_ref, bf16[128,2048]{1,0:T(8,128)(2,1)S(1)} %constant_dynamic-slice_fusion.y_ref, ...), custom_call_target="tpu_custom_call" | custom-call | flops 1073741824 | bytes 2359296 | tf_op jit(solution)/shard_map/pallas_call | solution.py:32
  13.9 1.0 %collective-permute-start.14 = (bf16[128,128]{1,0:T(8,128)(2,1)S(1)}, bf16[128,128]{1,0:T(8,128)(2,1)S(1)}, u32[]{:S(2)}, u32[]{:S(2)}) collective-permute-start(bf16[128,128]{1,0:T(8,128)(2,1)S(1)} %get-tuple-element.20), channel_id=1, source_target_pairs={{0,4},{4,0},{8,12},{12,8},{1,5},{5,1},{9,13},{13,9},{2,6},{6,2},{1... | collective-permute-start | bytes 98312 | tf_op jit(solution)/shard_map/ppermute | solution.py:18
  14.9 3.5 %collective-permute-start.15 = (bf16[128,128]{1,0:T(8,128)(2,1)S(1)}, bf16[128,128]{1,0:T(8,128)(2,1)S(1)}, u32[]{:S(2)}, u32[]{:S(2)}) collective-permute-start(bf16[128,128]{1,0:T(8,128)(2,1)S(1)} %get-tuple-element.21), channel_id=1, source_target_pairs={{0,8},{4,12},{8,0},{12,4},{1,9},{5,13},{9,1},{13,5},{2,10},{6,14},... | collective-permute-start | bytes 98312 | tf_op jit(solution)/shard_map/ppermute | solution.py:18
  18.4 0.0 collective-permute-done.2.refs_1_
  18.4 0.0 collective-permute-start.16
  18.4 0.0 collective-permute-done.3.refs_2_
  18.4 0.0 collective-permute-done.4.refs_3_
  18.4 0.0 copy-done.1
  18.4 2.1 %shard_map.103 = (bf16[256,128]{1,0:T(8,128)(2,1)S(1)}, bf16[256,128]{1,0:T(8,128)(2,1)S(1)}, bf16[256,128]{1,0:T(8,128)(2,1)S(1)}, bf16[256,128]{1,0:T(8,128)(2...) custom-call(s32[7]{0:T(128)S(1)} %stack.57.place_ref, bf16[256,2048]{1,0:T(8,128)(2,1)S(1)} %bitcast.48, ...), custom_call_target="tpu_custom_call" | custom-call | flops 1073741824 | bytes 4194304 | tf_op jit(solution)/shard_map/pallas_call | solution.py:209
  20.5 3.9 %collective-permute-start.5 = (bf16[256,128]{1,0:T(8,128)(2,1)S(1)}, bf16[256,128]{1,0:T(8,128)(2,1)S(1)}, u32[]{:S(2)}, u32[]{:S(2)}) collective-permute-start(bf16[256,128]{1,0:T(8,128)(2,1)S(1)} %get-tuple-element.14), channel_id=1, source_target_pairs={{0,12},{4,8},{8,4},{12,0},{1,13},{5,9},{9,5},{13,1},{2,14},{6,10},... | collective-permute-start | bytes 196616 | tf_op jit(solution)/shard_map/ppermute | solution.py:18
  24.4 0.0 collective-permute-start.6
  24.4 0.0 collective-permute-done.14
  24.4 0.6 %collective-permute-start.7 = (bf16[256,128]{1,0:T(8,128)(2,1)S(1)}, bf16[256,128]{1,0:T(8,128)(2,1)S(1)}, u32[]{:S(2)}, u32[]{:S(2)}) collective-permute-start(bf16[256,128]{1,0:T(8,128)(2,1)S(1)} %get-tuple-element.16), channel_id=1, source_target_pairs={{0,4},{4,0},{8,12},{12,8},{1,5},{5,1},{9,13},{13,9},{2,6},{6,2},{1... | collective-permute-start | bytes 196616 | tf_op jit(solution)/shard_map/ppermute | solution.py:18
  25.0 0.0 collective-permute-done.15
  25.0 1.6 %collective-permute-start.9 = (bf16[4,128,128]{2,1,0:T(8,128)(2,1)S(1)}, bf16[4,128,128]{2,1,0:T(8,128)(2,1)S(1)}, u32[]{:S(2)}, u32[]{:S(2)}) collective-permute-start(bf16[4,128,128]{2,1,0:T(8,128)(2,1)S(1)} %get-tuple-element.18), channel_id=1, source_target_pairs={{0,2},{2,0},{1,3},{3,1},{4,6},{6,4},{5,7},{7,5},{8,10},{10,8},{9,1... | collective-permute-start | bytes 393224 | tf_op jit(solution)/shard_map/ppermute | solution.py:18
  26.6 0.0 collective-permute-done.16
  26.6 0.1 fusion.1
  26.8 3.2 %collective-permute-done.9 = bf16[4,128,128]{2,1,0:T(8,128)(2,1)S(1)} collective-permute-done((bf16[4,128,128]{2,1,0:T(8,128)(2,1)S(1)}, bf16[4,128,128]{2,1,0:T(8,128)(2,1)S(1)}, u32[]{:S(2)}, u32[]{:S(2)}) %collective-permute-start.9) | collective-permute-done | bytes 131104 | tf_op jit(solution)/shard_map/ppermute | solution.py:18
  30.0 3.8 %collective-permute-start.10 = (bf16[128,128]{1,0:T(8,128)(2,1)S(1)}, bf16[128,128]{1,0:T(8,128)(2,1)S(1)}, u32[]{:S(2)}, u32[]{:S(2)}) collective-permute-start(bf16[128,128]{1,0:T(8,128)(2,1)S(1)} %get-tuple-element.25), channel_id=1, source_target_pairs={{0,12},{4,8},{8,4},{12,0},{1,13},{5,9},{9,5},{13,1},{2,14},{6,10},... | collective-permute-start | bytes 98312 | tf_op jit(solution)/shard_map/ppermute | solution.py:18
  33.8 0.0 collective-permute-start.11
  33.8 0.0 collective-permute-done.5
  33.8 0.6 %collective-permute-start.12 = (bf16[128,128]{1,0:T(8,128)(2,1)S(1)}, bf16[128,128]{1,0:T(8,128)(2,1)S(1)}, u32[]{:S(2)}, u32[]{:S(2)}) collective-permute-start(bf16[128,128]{1,0:T(8,128)(2,1)S(1)} %get-tuple-element.26), channel_id=1, source_target_pairs={{0,4},{4,0},{8,12},{12,8},{1,5},{5,1},{9,13},{13,9},{2,6},{6,2},{1... | collective-permute-start | bytes 98312 | tf_op jit(solution)/shard_map/ppermute | solution.py:18
  34.5 0.0 collective-permute-done.6
  34.5 0.0 collective-permute-done.7
  34.5 1.7 %collective-permute-start.8 = (bf16[256,128]{1,0:T(8,128)(2,1)S(1)}, bf16[256,128]{1,0:T(8,128)(2,1)S(1)}, u32[]{:S(2)}, u32[]{:S(2)}) collective-permute-start(bf16[256,128]{1,0:T(8,128)(2,1)S(1)} %add_convert_fusion.2), channel_id=1, source_target_pairs={{0,2},{2,0},{1,3},{3,1},{4,6},{6,4},{5,7},{7,5},{8,10},{10,8},{9,1... | collective-permute-start | bytes 196616 | tf_op jit(solution)/shard_map/ppermute | solution.py:18
  36.2 0.0 collective-permute-done.10
  36.2 2.4 %collective-permute-done.11 = bf16[128,128]{1,0:T(8,128)(2,1)S(1)} collective-permute-done((bf16[128,128]{1,0:T(8,128)(2,1)S(1)}, bf16[128,128]{1,0:T(8,128)(2,1)S(1)}, u32[]{:S(2)}, u32[]{:S(2)}) %collective-permute-start.11) | collective-permute-done | bytes 32800 | tf_op jit(solution)/shard_map/ppermute | solution.py:18
  38.7 0.0 collective-permute-done.12
  38.7 1.5 %collective-permute-start.13 = (bf16[128,128]{1,0:T(8,128)(2,1)S(1)}, bf16[128,128]{1,0:T(8,128)(2,1)S(1)}, u32[]{:S(2)}, u32[]{:S(2)}) collective-permute-start(bf16[128,128]{1,0:T(8,128)(2,1)S(1)} %fusion.5), channel_id=1, source_target_pairs={{0,2},{2,0},{1,3},{3,1},{4,6},{6,4},{5,7},{7,5},{8,10},{10,8},{9,1... | collective-permute-start | bytes 98312 | tf_op jit(solution)/shard_map/ppermute | solution.py:18
  40.2 0.0 collective-permute-done.8
  40.3 2.4 %collective-permute-done.13 = bf16[128,128]{1,0:T(8,128)(2,1)S(1)} collective-permute-done((bf16[128,128]{1,0:T(8,128)(2,1)S(1)}, bf16[128,128]{1,0:T(8,128)(2,1)S(1)}, u32[]{:S(2)}, u32[]{:S(2)}) %collective-permute-start.13) | collective-permute-done | bytes 32800 | tf_op jit(solution)/shard_map/ppermute | solution.py:18
  42.7 0.1 collective-permute-start.17
  42.8 2.5 %shard_map.105 = bf16[256,2048]{1,0:T(8,128)(2,1)} custom-call(bf16[8,512,128]{2,1,0:T(8,128)(2,1)S(1)} %copy-done.2, f32[256,128]{1,0:T(8,128)S(1)} %fusion.2.table_ref, bf16[128,256]{1,0:T(8,128)(2,1)S(1)} %fusion.refs_0_, bf16[128,256]{1,0:T(8,128)(2,1)S(1)} %collective-permute-done.2.refs_1_, bf16[128,256]{1,0:T(8,128)(2,1)S(1)} %collective-permute-done.3.refs_2_, ...), custom_call_target="tpu_custom_call" | custom-call | flops 1073741824 | bytes 2490368 | tf_op jit(solution)/shard_map/pallas_call | solution.py:32
  45.3 0.0 collective-permute-done.17
  45.3 0.6 %slice.40 = bf16[2,128,128]{2,1,0:T(8,128)(2,1)} slice(bf16[2,640,128]{2,1,0:T(8,128)(2,1)S(1)} %maximum_select_fusion), slice={[0:2], [512:640], [0:128]} | slice | bytes 131072 | tf_op jit(solution)/shard_map/slice | solution.py:239
  46.0 0.9 %copy.12 = f32[8,128,128]{1,2,0:T(8,128)} copy(bf16[8,128,128]{2,1,0:T(8,128)(2,1)S(1)} %bitcast.49) | data formatting | bytes 786432 | tf_op jit(solution)/shard_map/convert_element_type | solution.py:238
  (15 shorter events, 0.3 us)
Async XLA Ops:
  0.6 0.8 %copy-start = (bf16[1,128,128]{2,1,0:T(8,128)(2,1)S(1)}, bf16[1,128,128]{2,1,0:T(8,128)(2,1)}, u32[]{:S(2)}) copy-start(bf16[1,128,128]{2,1,0:T(8,128)(2,1)} %param.10) | copy-start | bytes 98308
  2.4 16.0 %collective-permute-start.2 = (bf16[128,256]{1,0:T(8,128)(2,1)S(1)}, bf16[128,256]{1,0:T(8,128)(2,1)S(1)}, u32[]{:S(2)}, u32[]{:S(2)}) collective-permute-start(bf16[128,256]{1,0:T(8,128)(2,1)S(1)} %fusion.refs_0_), channel_id=1, source_target_pairs={{0,4},{4,0},{8,12},{12,8},{1,5},{5,1},{9,13},{13,9},{2,6},{6,2},{1... | collective-permute-start | bytes 196616 | tf_op jit(solution)/shard_map/ppermute | solution.py:18
  5.5 12.9 %collective-permute-start.3 = (bf16[128,256]{1,0:T(8,128)(2,1)S(1)}, bf16[128,256]{1,0:T(8,128)(2,1)S(1)}, u32[]{:S(2)}, u32[]{:S(2)}) collective-permute-start(bf16[128,256]{1,0:T(8,128)(2,1)S(1)} %fusion.refs_0_), channel_id=1, source_target_pairs={{0,8},{4,12},{8,0},{12,4},{1,9},{5,13},{9,1},{13,5},{2,10},{6,14},... | collective-permute-start | bytes 196616 | tf_op jit(solution)/shard_map/ppermute | solution.py:18
  8.1 10.3 %collective-permute-start.4 = (bf16[128,256]{1,0:T(8,128)(2,1)S(1)}, bf16[128,256]{1,0:T(8,128)(2,1)S(1)}, u32[]{:S(2)}, u32[]{:S(2)}) collective-permute-start(bf16[128,256]{1,0:T(8,128)(2,1)S(1)} %fusion.refs_0_), channel_id=1, source_target_pairs={{0,12},{4,8},{8,4},{12,0},{1,13},{5,9},{9,5},{13,1},{2,14},{6,10},... | collective-permute-start | bytes 196616 | tf_op jit(solution)/shard_map/ppermute | solution.py:18
  8.1 0.7 %copy-start.3 = (s32[64]{0:T(128)S(1)}, s32[64]{0:T(128)}, u32[]{:S(2)}) copy-start(s32[64]{0:T(128)} %param.15) | copy-start | bytes 772
  8.1 0.7 %copy-start.4 = (s32[64]{0:T(128)S(1)}, s32[64]{0:T(128)}, u32[]{:S(2)}) copy-start(s32[64]{0:T(128)} %param.14) | copy-start | bytes 772
  8.1 0.7 %copy-start.5 = (s32[64]{0:T(128)S(1)}, s32[64]{0:T(128)}, u32[]{:S(2)}) copy-start(s32[64]{0:T(128)} %param.13) | copy-start | bytes 772
  8.8 1.9 %collective-permute-start.1 = (s32[3,64]{1,0:T(4,128)S(1)}, s32[3,64]{1,0:T(4,128)S(1)}, u32[]{:S(2)}, u32[]{:S(2)}) collective-permute-start(s32[3,64]{1,0:T(4,128)S(1)} %pad_add_fusion), channel_id=1, source_target_pairs={{0,1},{1,0},{2,3},{3,2},{4,5},{5,4},{6,7},{7,6},{8,9},{9,8},{10,11... | collective-permute-start | bytes 2312 | tf_op jit(solution)/shard_map/ppermute | solution.py:18
  8.9 3.0 %collective-permute-start = (bf16[256,2048]{1,0:T(8,128)(2,1)}, bf16[256,2048]{1,0:T(8,128)(2,1)S(1)}, u32[]{:S(2)}, u32[]{:S(2)}) collective-permute-start(bf16[256,2048]{1,0:T(8,128)(2,1)} %bitcast.47), channel_id=1, source_target_pairs={{0,1},{1,0},{2,3},{3,2},{4,5},{5,4},{6,7},{7,6},{8,9},{9,8},{10,11... | collective-permute-start | bytes 3145736 | tf_op jit(solution)/shard_map/ppermute | solution.py:18
  9.4 2.5 %copy-start.2 = (bf16[8,512,128]{2,1,0:T(8,128)(2,1)S(1)}, bf16[8,512,128]{2,1,0:T(8,128)(2,1)}, u32[]{:S(2)}) copy-start(bf16[8,512,128]{2,1,0:T(8,128)(2,1)} %site_ref.3) | copy-start | bytes 3145732
  11.9 6.5 %copy-start.1 = (bf16[1,256,2048]{2,1,0:T(8,128)(2,1)S(1)}, bf16[1,256,2048]{2,1,0:T(8,128)(2,1)}, u32[]{:S(2)}) copy-start(bf16[1,256,2048]{2,1,0:T(8,128)(2,1)} %param.8) | copy-start | bytes 3145732
  13.9 10.5 %collective-permute-start.14 = (bf16[128,128]{1,0:T(8,128)(2,1)S(1)}, bf16[128,128]{1,0:T(8,128)(2,1)S(1)}, u32[]{:S(2)}, u32[]{:S(2)}) collective-permute-start(bf16[128,128]{1,0:T(8,128)(2,1)S(1)} %get-tuple-element.20), channel_id=1, source_target_pairs={{0,4},{4,0},{8,12},{12,8},{1,5},{5,1},{9,13},{13,9},{2,6},{6,2},{1... | collective-permute-start | bytes 98312 | tf_op jit(solution)/shard_map/ppermute | solution.py:18
  14.9 10.1 %collective-permute-start.15 = (bf16[128,128]{1,0:T(8,128)(2,1)S(1)}, bf16[128,128]{1,0:T(8,128)(2,1)S(1)}, u32[]{:S(2)}, u32[]{:S(2)}) collective-permute-start(bf16[128,128]{1,0:T(8,128)(2,1)S(1)} %get-tuple-element.21), channel_id=1, source_target_pairs={{0,8},{4,12},{8,0},{12,4},{1,9},{5,13},{9,1},{13,5},{2,10},{6,14},... | collective-permute-start | bytes 98312 | tf_op jit(solution)/shard_map/ppermute | solution.py:18
  18.4 8.3 %collective-permute-start.16 = (bf16[128,128]{1,0:T(8,128)(2,1)S(1)}, bf16[128,128]{1,0:T(8,128)(2,1)S(1)}, u32[]{:S(2)}, u32[]{:S(2)}) collective-permute-start(bf16[128,128]{1,0:T(8,128)(2,1)S(1)} %get-tuple-element.22), channel_id=1, source_target_pairs={{0,12},{4,8},{8,4},{12,0},{1,13},{5,9},{9,5},{13,1},{2,14},{6,10},... | collective-permute-start | bytes 98312 | tf_op jit(solution)/shard_map/ppermute | solution.py:18
  20.5 13.4 %collective-permute-start.5 = (bf16[256,128]{1,0:T(8,128)(2,1)S(1)}, bf16[256,128]{1,0:T(8,128)(2,1)S(1)}, u32[]{:S(2)}, u32[]{:S(2)}) collective-permute-start(bf16[256,128]{1,0:T(8,128)(2,1)S(1)} %get-tuple-element.14), channel_id=1, source_target_pairs={{0,12},{4,8},{8,4},{12,0},{1,13},{5,9},{9,5},{13,1},{2,14},{6,10},... | collective-permute-start | bytes 196616 | tf_op jit(solution)/shard_map/ppermute | solution.py:18
  24.4 10.1 %collective-permute-start.6 = (bf16[256,128]{1,0:T(8,128)(2,1)S(1)}, bf16[256,128]{1,0:T(8,128)(2,1)S(1)}, u32[]{:S(2)}, u32[]{:S(2)}) collective-permute-start(bf16[256,128]{1,0:T(8,128)(2,1)S(1)} %get-tuple-element.15), channel_id=1, source_target_pairs={{0,8},{4,12},{8,0},{12,4},{1,9},{5,13},{9,1},{13,5},{2,10},{6,14},... | collective-permute-start | bytes 196616 | tf_op jit(solution)/shard_map/ppermute | solution.py:18
  24.4 10.1 %collective-permute-start.7 = (bf16[256,128]{1,0:T(8,128)(2,1)S(1)}, bf16[256,128]{1,0:T(8,128)(2,1)S(1)}, u32[]{:S(2)}, u32[]{:S(2)}) collective-permute-start(bf16[256,128]{1,0:T(8,128)(2,1)S(1)} %get-tuple-element.16), channel_id=1, source_target_pairs={{0,4},{4,0},{8,12},{12,8},{1,5},{5,1},{9,13},{13,9},{2,6},{6,2},{1... | collective-permute-start | bytes 196616 | tf_op jit(solution)/shard_map/ppermute | solution.py:18
  25.0 5.0 %collective-permute-start.9 = (bf16[4,128,128]{2,1,0:T(8,128)(2,1)S(1)}, bf16[4,128,128]{2,1,0:T(8,128)(2,1)S(1)}, u32[]{:S(2)}, u32[]{:S(2)}) collective-permute-start(bf16[4,128,128]{2,1,0:T(8,128)(2,1)S(1)} %get-tuple-element.18), channel_id=1, source_target_pairs={{0,2},{2,0},{1,3},{3,1},{4,6},{6,4},{5,7},{7,5},{8,10},{10,8},{9,1... | collective-permute-start | bytes 393224 | tf_op jit(solution)/shard_map/ppermute | solution.py:18
  30.0 6.2 %collective-permute-start.10 = (bf16[128,128]{1,0:T(8,128)(2,1)S(1)}, bf16[128,128]{1,0:T(8,128)(2,1)S(1)}, u32[]{:S(2)}, u32[]{:S(2)}) collective-permute-start(bf16[128,128]{1,0:T(8,128)(2,1)S(1)} %get-tuple-element.25), channel_id=1, source_target_pairs={{0,12},{4,8},{8,4},{12,0},{1,13},{5,9},{9,5},{13,1},{2,14},{6,10},... | collective-permute-start | bytes 98312 | tf_op jit(solution)/shard_map/ppermute | solution.py:18
  33.8 4.8 %collective-permute-start.11 = (bf16[128,128]{1,0:T(8,128)(2,1)S(1)}, bf16[128,128]{1,0:T(8,128)(2,1)S(1)}, u32[]{:S(2)}, u32[]{:S(2)}) collective-permute-start(bf16[128,128]{1,0:T(8,128)(2,1)S(1)} %get-tuple-element.27), channel_id=1, source_target_pairs={{0,8},{4,12},{8,0},{12,4},{1,9},{5,13},{9,1},{13,5},{2,10},{6,14},... | collective-permute-start | bytes 98312 | tf_op jit(solution)/shard_map/ppermute | solution.py:18
  33.8 4.8 %collective-permute-start.12 = (bf16[128,128]{1,0:T(8,128)(2,1)S(1)}, bf16[128,128]{1,0:T(8,128)(2,1)S(1)}, u32[]{:S(2)}, u32[]{:S(2)}) collective-permute-start(bf16[128,128]{1,0:T(8,128)(2,1)S(1)} %get-tuple-element.26), channel_id=1, source_target_pairs={{0,4},{4,0},{8,12},{12,8},{1,5},{5,1},{9,13},{13,9},{2,6},{6,2},{1... | collective-permute-start | bytes 98312 | tf_op jit(solution)/shard_map/ppermute | solution.py:18
  34.5 5.7 %collective-permute-start.8 = (bf16[256,128]{1,0:T(8,128)(2,1)S(1)}, bf16[256,128]{1,0:T(8,128)(2,1)S(1)}, u32[]{:S(2)}, u32[]{:S(2)}) collective-permute-start(bf16[256,128]{1,0:T(8,128)(2,1)S(1)} %add_convert_fusion.2), channel_id=1, source_target_pairs={{0,2},{2,0},{1,3},{3,1},{4,6},{6,4},{5,7},{7,5},{8,10},{10,8},{9,1... | collective-permute-start | bytes 196616 | tf_op jit(solution)/shard_map/ppermute | solution.py:18
  38.7 4.0 %collective-permute-start.13 = (bf16[128,128]{1,0:T(8,128)(2,1)S(1)}, bf16[128,128]{1,0:T(8,128)(2,1)S(1)}, u32[]{:S(2)}, u32[]{:S(2)}) collective-permute-start(bf16[128,128]{1,0:T(8,128)(2,1)S(1)} %fusion.5), channel_id=1, source_target_pairs={{0,2},{2,0},{1,3},{3,1},{4,6},{6,4},{5,7},{7,5},{8,10},{10,8},{9,1... | collective-permute-start | bytes 98312 | tf_op jit(solution)/shard_map/ppermute | solution.py:18
  42.7 2.5 %collective-permute-start.17 = (bf16[640,128]{1,0:T(8,128)(2,1)S(1)}, bf16[640,128]{1,0:T(8,128)(2,1)S(1)}, u32[]{:S(2)}, u32[]{:S(2)}) collective-permute-start(bf16[640,128]{1,0:T(8,128)(2,1)S(1)} %get-tuple-element.24), channel_id=1, source_target_pairs={{0,1},{1,0},{2,3},{3,2},{4,5},{5,4},{6,7},{7,6},{8,9},{9,8},{10,11... | collective-permute-start | bytes 491528 | tf_op jit(solution)/shard_map/ppermute | solution.py:18

commit v2 on v1

v2 whole, which is shorter than its diff:
```python
import functools
import jax
import jax.numpy as jnp
from jax import lax
from jax.experimental import pallas as pl
from jax.experimental.pallas import tpu as pltpu
from jax.sharding import PartitionSpec as P

F32 = jnp.float32
BF16 = jnp.bfloat16
NT = (((1,), (1,)), ((), ()))
LIMIT = 24 * 1024 * 1024


def swap(value, axis, bit):
    size = lax.axis_size(axis)
    return lax.ppermute(value, axis, [(place, place ^ bit) for place in range(size)])


def total(*terms):
    acc = terms[0].astype(F32)
    for term in terms[1:]:
        acc = acc + term.astype(F32)
    return acc


def call(kernel, outs, args, scratch=(), flops=0, far=0):
    moved = sum(a.size * a.dtype.itemsize for a in args) + sum(
        a.size * a.dtype.itemsize for a in outs
    )
    scalars = pl.BlockSpec(memory_space=pltpu.SMEM)
    vectors = pl.BlockSpec(memory_space=pltpu.VMEM)
    return pl.pallas_call(
        kernel,
        out_shape=list(outs),
        in_specs=[pl.BlockSpec(memory_space=pltpu.HBM)] * far
        + [scalars if a.ndim == 1 else vectors for a in args[far:]],
        out_specs=[vectors] * len(outs),
        scratch_shapes=list(scratch),
        compiler_params=pltpu.CompilerParams(vmem_limit_bytes=LIMIT),
        cost_estimate=pl.CostEstimate(flops=flops, bytes_accessed=moved, transcendentals=0),
    )(*[pltpu.with_memory_space_constraint(a, pltpu.HBM) for a in args[:far]], *args[far:])


def start_all(arrived, *pairs):
    copies = [
        pltpu.make_async_copy(source, target, arrived.at[at])
        for at, (source, target) in enumerate(pairs)
    ]
    for copy in copies:
        copy.start()
    return copies


def count_table(pairs_ref, table_ref):
    places, lanes = table_ref.shape
    pairs = pairs_ref.shape[1]
    hits = lax.broadcasted_iota(jnp.int32, (places, pairs), 0) == pairs_ref[...]
    table_ref[...] = jnp.dot(
        jnp.where(hits, 1.0, 0.0).astype(BF16),
        jnp.ones((pairs, lanes), BF16),
        preferred_element_type=F32,
    )


def count_of(table_ref, index, height, width):
    row = table_ref[pl.ds(index, 1), :]
    wide = jnp.concatenate([row] * (width // row.shape[1]), axis=1)
    return jnp.broadcast_to(wide, (height, width))


def grad_kernel(
    owners, subs, blocks, projector_hbm, cotangent_hbm, dest_hbm, sub_hbm, site_hbm, dim_ref,
    out_ref, live_ref, combo_ref, projector_ref, cotangent_ref, lists_ref, arrived
):
    copies = start_all(
        arrived,
        (cotangent_hbm, cotangent_ref),
        (projector_hbm, projector_ref),
        (dest_hbm, lists_ref.at[0]),
        (sub_hbm, lists_ref.at[1]),
        (site_hbm, lists_ref.at[2]),
    )
    for copy in copies:
        copy.wait()
    combo_ref[...] = (lists_ref[0] * subs + lists_ref[1]) * blocks + lists_ref[2]
    lane = lax.broadcasted_iota(jnp.int32, projector_ref.shape, 1)
    live = jnp.where(lane < dim_ref[0], 1.0, 0.0)
    live_ref[...] = live[: live_ref.shape[0]]
    out_ref[...] = lax.dot_general(
        (projector_ref[...].astype(F32) * live).astype(BF16),
        cotangent_ref[...],
        NT,
        preferred_element_type=F32,
    ).astype(out_ref.dtype)


def forward_kernel(owners, subs, blocks, x_hbm, site_hbm, place_ref, own_ref, far_ref, y_ref, *refs):
    outs, (x_ref, site_ref, table_ref, arrived) = refs[:owners], refs[owners:]
    rows, chi = outs[0].shape
    width = site_ref.shape[1]
    step = 2
    copies = start_all(
        arrived,
        *[
            (site_hbm.at[block : block + step], site_ref.at[block : block + step])
            for block in range(0, blocks, step)
        ],
        (x_hbm, x_ref),
    )
    places = table_ref.shape[0] // 2
    count_table(own_ref, table_ref.at[:places])
    count_table(far_ref, table_ref.at[places:])
    mine = pl.ds(pl.multiple_of(place_ref[owners + 3], rows), rows)
    copies[0].wait()
    copies[-1].wait()
    stacked = jnp.concatenate(
        [ref[mine, sub * width : (sub + 1) * width] for ref in (x_ref, y_ref) for sub in range(subs)],
        axis=0,
    )
    accs = [jnp.zeros((rows, chi), F32) for _ in range(owners)]
    for block in range(0, blocks, step):
        if block:
            copies[block // step].wait()
        pair = jnp.concatenate([site_ref[block + offset] for offset in range(step)], axis=1)
        product = jnp.dot(stacked, pair, preferred_element_type=F32)
        for sub in range(2 * subs):
            for offset in range(step):
                piece = product[sub * rows : (sub + 1) * rows, offset * chi : (offset + 1) * chi]
                for owner in range(owners):
                    index = place_of(owners, subs, blocks, owner, sub, block + offset)
                    accs[owner] = accs[owner] + piece * count_of(table_ref, index, rows, chi)
    for owner in range(owners):
        outs[owner][...] = accs[owner].astype(outs[owner].dtype)


def place_of(owners, subs, blocks, owner, sub, block):
    return ((sub // subs * owners + owner) * subs + sub % subs) * blocks + block


def pulled_of(grads, table_ref, owners, subs, blocks, sub, block):
    value = None
    for owner, grad in enumerate(grads):
        index = place_of(owners, subs, blocks, owner, sub, block)
        term = grad * count_of(table_ref, index, *grad.shape)
        value = term if value is None else value + term
    return value.astype(BF16)


def site_kernel(owners, subs, blocks, taken, first, place_ref, table_ref, x_ref, y_ref, *refs):
    partials, refs = refs[:owners], refs[owners:]
    grads = [ref[...].astype(F32) for ref in refs[:owners]]
    outs, acc = refs[owners:-1], refs[-1]
    chi = grads[0].shape[0]
    width = acc.shape[1]
    for sub in range(2 * subs):
        source = x_ref if sub < subs else y_ref
        low = (sub % subs) * width
        left = [
            pulled_of(grads, table_ref, owners, subs, blocks, sub, place_ref[0] + at)
            for at in range(taken)
        ]
        product = jnp.dot(
            jnp.concatenate(left, axis=0), source[:, low : low + width], preferred_element_type=F32
        )
        if sub == 0:
            acc[...] = product
        else:
            acc[...] += product
    if len(outs) == 1:
        outs[0][...] = acc[...]
        return
    chunk = width // owners
    straight = first * chi
    crossing, staying = outs[owners:]
    share = crossing.shape[1]
    for rel in range(owners):
        lanes = pl.ds(pl.multiple_of(place_ref[1 + rel] * chunk, chunk), chunk)
        outs[rel][:straight] = acc[:straight, lanes].astype(outs[rel].dtype)
        outs[rel][straight:] = partials[rel][...].astype(outs[rel].dtype)
        for out, slot in ((crossing, 1), (staying, 0)):
            rows = pl.ds(pl.multiple_of(straight + place_ref[1 + owners + slot] * share, share), share)
            out[rel] = acc[rows, lanes].astype(out.dtype)


def corner_kernel(owners, subs, blocks, site_ref, table_ref, *refs):
    grads = [ref[...].astype(F32).T for ref in refs[:owners]]
    out = refs[owners]
    width = site_ref.shape[1]
    wide = jnp.concatenate([site_ref[block] for block in range(blocks)], axis=1)
    for sub in range(subs):
        left = jnp.concatenate(
            [pulled_of(grads, table_ref, owners, subs, blocks, sub, block) for block in range(blocks)],
            axis=1,
        )
        value = lax.dot_general(left, wide, NT, preferred_element_type=F32)
        out[:, sub * width : (sub + 1) * width] = value.astype(out.dtype)


def per_device(corner, site, projector, cotangent, sector_dim, pair_dest, pair_sub, pair_site):
    owners = lax.axis_size("sector")
    sides = lax.axis_size("block")
    me, side, rep = lax.axis_index("sector"), lax.axis_index("block"), lax.axis_index("rep")
    blocks, width, chi = site.shape
    rows = corner.shape[1]
    subs = corner.shape[2] // width
    pairs = pair_dest.shape[0]
    direct = owners * chi == width and sides == 2
    flat = corner[0]
    mine = blocks // 2
    first = mine // 4
    part = rows // 2
    chunk = width // owners
    places = owners * subs * blocks
    shape = jax.ShapeDtypeStruct
    place = jnp.stack(
        [rep * mine]
        + [me ^ rel for rel in range(owners)]
        + [side, 1 - side, rep * part, (1 - rep) * part]
    ).astype(jnp.int32)

    other = swap(flat, "rep", 1)
    def placed(value):
        if direct:
            stride = subs * blocks
            value = (value // stride ^ me) * stride + value % stride
        return value

    sizes = (owners, subs, blocks)
    lists = [value.reshape(1, pairs) for value in (pair_dest, pair_sub, pair_site)]
    grad, live, combo = call(
        functools.partial(grad_kernel, *sizes),
        [shape((chi, rows), BF16), shape((8, chi), F32), shape((1, pairs), jnp.int32)],
        [projector[0], cotangent[0], *lists, sector_dim],
        [
            pltpu.VMEM((chi, chi), BF16),
            pltpu.VMEM((rows, chi), BF16),
            pltpu.VMEM((3, 1, pairs), jnp.int32),
            pltpu.SemaphoreType.DMA((5,)),
        ],
        far=5,
    )
    far = swap(combo, "rep", 1)
    if direct:
        grads = [grad] + [swap(grad, "sector", bit) for bit in range(1, owners)]
    else:
        shared = lax.all_gather(grad, "sector", axis=0)
        grads = [shared[owner] for owner in range(owners)]

    *partials, near, blocks_near, table = call(
        functools.partial(forward_kernel, *sizes),
        [shape((part, chi), BF16)] * owners
        + [shape(flat.shape, BF16), shape(site.shape, BF16), shape((2 * places, 128), F32)],
        [flat, site, place, placed(combo), placed(far), other],
        [pltpu.SemaphoreType.DMA((1 + blocks // 2,))],
        flops=4 * subs * rows * width * chi * blocks,
        far=2,
    )

    def project(enlarged):
        value = jnp.dot(enlarged.astype(BF16), projector[0], preferred_element_type=F32)
        return (value * live[:1]).astype(BF16)

    def corner_term(after):
        args = lax.optimization_barrier(((blocks_near, table, *grads), after))[0]
        return call(
            functools.partial(corner_kernel, *sizes),
            [shape((rows, subs * width), BF16)],
            list(args),
            flops=2 * subs * rows * width * chi * owners,
        )[0][None]

    if direct:
        share = (mine - first) * chi // sides
        height = first * chi + part
        outs = [shape((height, chunk), F32)] + [shape((height, chunk), BF16)] * (owners - 1)
        outs += [shape((owners, share, chunk), BF16), shape((owners, share, chunk), F32)]
    else:
        outs = [shape((mine * chi, width), F32)]
    pieces = call(
        functools.partial(site_kernel, *sizes, mine, first),
        outs,
        [place, table, near, other, *partials, *grads],
        [pltpu.VMEM((mine * chi, width), F32)],
        flops=4 * subs * rows * width * chi * mine,
    )
    if direct:
        bits = range(owners - 1, 0, -1)
        straight = first * chi
        crossed = swap(pieces[owners], "block", 1)
        direct_sums = [pieces[0]] + [swap(pieces[bit], "sector", bit) for bit in bits]
        merged = total(pieces[owners + 1], crossed)
        sent = merged.astype(BF16)
        shared_sums = [merged[0]] + [swap(sent[bit], "sector", bit) for bit in bits]
        upper = total(*direct_sums)
        projected = project(upper[straight:])
        upper = upper[:straight]
        corner_grad = corner_term(upper)
        lower = total(*shared_sums)
        both = jnp.concatenate([upper, lower]).astype(BF16)
        both, corner_grad = lax.optimization_barrier((both, corner_grad))
        beside = swap(both, "block", 1)
        upper = total(upper, beside[:straight]).astype(BF16)
        lower, under = both[straight:], beside[straight:]
        own = jnp.concatenate(
            [upper, jnp.where(side == 0, lower, under), jnp.where(side == 0, under, lower)]
        )
        projected = [projected, swap(projected, "rep", 1)]
        there = swap(own, "rep", 1)

        def ordered(pair):
            return jnp.where(rep == 0, jnp.stack(pair), jnp.stack(pair[::-1]))

        corner_new = ordered(projected).reshape(1, rows, chi)
        site_grad = ordered([own, there]).reshape(blocks, chi, chunk).swapaxes(1, 2).astype(F32)
    else:
        term = pieces[0].astype(BF16).reshape(mine, chi, width)
        term = lax.psum_scatter(term, "sector", scatter_dimension=2, tiled=True)
        term = lax.psum(term, "block")
        site_grad = lax.all_gather(term, "rep", axis=0, tiled=True).swapaxes(1, 2).astype(F32)
        arrived = lax.all_to_all(
            jnp.stack(partials), "sector", split_axis=0, concat_axis=0, tiled=True
        )
        projected = project(jnp.sum(arrived.astype(F32), axis=0))
        corner_new = lax.all_gather(projected, "rep", axis=0, tiled=True)[None]
        corner_grad = corner_term(term)
    return (corner_new, corner_grad, site_grad)


def solution(mesh):
    in_specs = (
        P(("groups", "sector"), "block", "rep"),
        P("groups", None, None),
        P(("groups", "sector"), None, None),
        P(("groups", "sector"), "block", None),
        P(("groups", "sector")),
        P(("groups", "sector", "rep")),
        P(("groups", "sector", "rep")),
        P(("groups", "sector", "rep")),
    )
    out_specs = (
        P(("groups", "sector"), "block", None),
        P(("groups", "sector"), "block", "rep"),
        P("groups", "sector", None),
    )
    return jax.shard_map(
        per_device, mesh=mesh, in_specs=in_specs, out_specs=out_specs, check_vma=False
    )
```

time: 47.2 us -> 41.1 us (0.87)
  starting transfers between devices: 24.6 us -> 17.1 us
  Pallas kernels: 6.48 us -> 10.6 us
  local copies, waits for them, and re-layouts: 3.69 us -> 1.19 us
  matrix products: 1.29 us -> 0.13 us
  other arithmetic: 0.31 us -> 0.87 us
    ppermute x18 -> x15, starting transfers between devices: 24.6 us -> 17.1 us  [swap(): lax.ppermute(value, axis, [(place, place ^ bit) for place in range(size)])]
    pallas_call x3 -> x4, Pallas kernels: 6.48 us -> 10.6 us  [call(): pl.pallas_call(kernel, out_shape=list(outs), in_specs=[pl.BlockSpec(memor...]
    dynamic_slice x2 -> x0, local copies, waits for them, and re-layouts: 1.2 us -> none  [the longest x1 1.17 us: per_device(): mine_x = lax.dynamic_slice_in_dim(flat, rep * part, part, 0)]
    dot_general x3 -> x1, matrix products: 1.29 us -> 0.13 us  [project(): jnp.dot(enlarged.astype(BF16), projector[0], preferred_element_type=F32)]
    unnamed x12 -> x2, local copies, waits for them, and re-layouts: 0.8 us -> 0.14 us
    slice x2 -> x1, local copies, waits for them, and re-layouts: 0.65 us -> 0.01 us  [per_device(): upper = upper[:straight]]
    select_n x2 -> x3, other arithmetic: 0.05 us -> 0.68 us  [the longest x2 0.67 us: ordered(): return jnp.where(rep == 0, jnp.stack(pair), jnp.stack(pair[::-1]))]
    ppermute x18 -> x15, waiting for transfers between devices: 9.02 us -> 9.44 us  [swap(): lax.ppermute(value, axis, [(place, place ^ bit) for place in range(size)])]
  transfers between devices with their start and end apart: 18 -> 15, of which waited for: 4 -> 6; matrix products, arithmetic and copies ran while one was open for 4% -> 3% of each run, Pallas kernels for 14% -> 21%
where the time goes in v2:
time: 41.1 us; the launch traced here: 40.8 us
  starting transfers between devices  17.1 us (42%)
  Pallas kernels  10.6 us (26%)
  waiting for transfers between devices  9.44 us (23%)
  between operations  1.45 us (4%)
  local copies, waits for them, and re-layouts  1.19 us (3%)
  other arithmetic  0.87 us (2%)
    ppermute x15, starting transfers between devices, swap(): lax.ppermute(value, axis, [(place, place ^ bit) for place in range(size)])  17.1 us
    pallas_call x4, Pallas kernels, call(): pl.pallas_call(kernel, out_shape=list(outs), in_specs=[pl.BlockSpec(memor...  10.6 us
    ppermute x15, waiting for transfers between devices, swap(): lax.ppermute(value, axis, [(place, place ^ bit) for place in range(size)])  9.44 us
    convert_element_type x1, local copies, waits for them, and re-layouts, per_device(): ordered([own, there]).reshape(blocks, chi, chunk).swapaxes(1, 2).astype(F32)  0.94 us
  transfers between devices with their start and end apart: 15, of which 6 were waited for; matrix products, arithmetic and copies ran while one was open for 3% of the time, Pallas kernels for 21%

profile of v2, /device:TPU:0, one launch (start us, length us, event | category | flops | bytes accessed | tf_op | source)
XLA Modules:
  0.0 40.8 jit_solution(17837454639052460799)
XLA Ops:
  0.6 0.5 %collective-permute-start.1 = (bf16[256,2048]{1,0:T(8,128)(2,1)}, bf16[256,2048]{1,0:T(8,128)(2,1)S(1)}, u32[]{:S(2)}, u32[]{:S(2)}) collective-permute-start(bf16[256,2048]{1,0:T(8,128)(2,1)} %bitcast.57), channel_id=1, source_target_pairs={{0,1},{1,0},{2,3},{3,2},{4,5},{5,4},{6,7},{7,6},{8,9},{9,8},{10,11... | collective-permute-start | bytes 3145736 | tf_op jit(solution)/shard_map/ppermute | solution.py:17
  1.8 1.1 %shard_map.103 = (bf16[128,256]{1,0:T(8,128)(2,1)S(1)}, f32[8,128]{1,0:T(8,128)S(1)}, s32[1,64]{1,0:T(1,128)S(1)}) custom-call(bf16[128,128]{1,0:T(8,128)(2,1)} %bitcast.49, bf16[256,128]{1,0:T(8,128)(2,1)} %bitcast.51, s32[1,64]{1,0:T(1,128)} %bitcast.54, s32[1,64]{1,0:T(1,128)} %bitcast.55, s32[1,64]{1,0:T(1,128)} %bitcast.56, s32[1]{0:T(128)S(6)} %copy.12.dim_ref), custom_call_target="tpu_custom_call" | custom-call | bytes 168964 | tf_op jit(solution)/shard_map/pallas_call | solution.py:33
  2.9 4.7 %collective-permute-start.4 = (bf16[128,256]{1,0:T(8,128)(2,1)S(1)}, bf16[128,256]{1,0:T(8,128)(2,1)S(1)}, u32[]{:S(2)}, u32[]{:S(2)}) collective-permute-start(bf16[128,256]{1,0:T(8,128)(2,1)S(1)} %get-tuple-element.45.refs_4_.refs_0_), channel_id=1, source_target_pairs={{0,12},{4,8},{8,4},{12,0},{1,13},{5,9},{9,5},{13,1},{2,14},{6,10},... | collective-permute-start | bytes 196616 | tf_op jit(solution)/shard_map/ppermute | solution.py:17
  7.5 0.0 collective-permute-start.3
  7.5 0.6 %collective-permute-start.2 = (bf16[128,256]{1,0:T(8,128)(2,1)S(1)}, bf16[128,256]{1,0:T(8,128)(2,1)S(1)}, u32[]{:S(2)}, u32[]{:S(2)}) collective-permute-start(bf16[128,256]{1,0:T(8,128)(2,1)S(1)} %get-tuple-element.45.refs_4_.refs_0_), channel_id=1, source_target_pairs={{0,4},{4,0},{8,12},{12,8},{1,5},{5,1},{9,13},{13,9},{2,6},{6,2},{1... | collective-permute-start | bytes 196616 | tf_op jit(solution)/shard_map/ppermute | solution.py:17
  8.2 0.0 collective-permute-start
  8.2 0.1 stack.67.place_ref
  8.3 1.0 %collective-permute-done = s32[1,64]{1,0:T(1,128)S(1)} collective-permute-done((s32[1,64]{1,0:T(1,128)S(1)}, s32[1,64]{1,0:T(1,128)S(1)}, u32[]{:S(2)}, u32[]{:S(2)}) %collective-permute-start) | collective-permute-done | bytes 288 | tf_op jit(solution)/shard_map/ppermute | solution.py:17
  9.3 0.0 collective-permute-done.1.y_ref
  9.3 5.0 %shard_map.104 = (bf16[128,128]{1,0:T(8,128)(2,1)S(1)}, bf16[128,128]{1,0:T(8,128)(2,1)S(1)}, bf16[128,128]{1,0:T(8,128)(2,1)S(1)}, bf16[128,128]{1,0:T(8,128)(2...) custom-call(bf16[256,2048]{1,0:T(8,128)(2,1)} %bitcast.58, ...), custom_call_target="tpu_custom_call" | custom-call | flops 2147483648 | bytes 5505572 | tf_op jit(solution)/shard_map/pallas_call | solution.py:33
  14.3 0.0 collective-permute-done.4.refs_7_.refs_3_
  14.3 0.0 collective-permute-done.3.refs_6_.refs_2_
  14.3 0.0 collective-permute-done.2.refs_5_.refs_1_
  14.3 2.1 %shard_map.105 = (f32[256,128]{1,0:T(8,128)S(1)}, bf16[256,128]{1,0:T(8,128)(2,1)S(1)}, bf16[256,128]{1,0:T(8,128)(2,1)S(1)}, bf16[256,128]{1,0:T(8,128)(2,1)S(1...) custom-call(s32[9]{0:T(128)S(1)} %stack.67.place_ref, f32[256,128]{1,0:T(8,128)S(1)} %get-tuple-element.44.table_ref, ...), custom_call_target="tpu_custom_call" | custom-call | flops 1073741824 | bytes 3538980 | tf_op jit(solution)/shard_map/pallas_call | solution.py:33
  16.5 1.7 %collective-permute-start.9 = (bf16[4,192,128]{2,1,0:T(8,128)(2,1)S(1)}, bf16[4,192,128]{2,1,0:T(8,128)(2,1)S(1)}, u32[]{:S(2)}, u32[]{:S(2)}) collective-permute-start(bf16[4,192,128]{2,1,0:T(8,128)(2,1)S(1)} %get-tuple-element.41), channel_id=1, source_target_pairs={{0,2},{2,0},{1,3},{3,1},{4,6},{6,4},{5,7},{7,5},{8,10},{10,8},{9,1... | collective-permute-start | bytes 589832 | tf_op jit(solution)/shard_map/ppermute | solution.py:17
  18.2 3.6 %collective-permute-start.5 = (bf16[256,128]{1,0:T(8,128)(2,1)S(1)}, bf16[256,128]{1,0:T(8,128)(2,1)S(1)}, u32[]{:S(2)}, u32[]{:S(2)}) collective-permute-start(bf16[256,128]{1,0:T(8,128)(2,1)S(1)} %get-tuple-element.36), channel_id=1, source_target_pairs={{0,12},{4,8},{8,4},{12,0},{1,13},{5,9},{9,5},{13,1},{2,14},{6,10},... | collective-permute-start | bytes 196616 | tf_op jit(solution)/shard_map/ppermute | solution.py:17
  21.8 0.0 collective-permute-start.6
  21.8 0.8 %collective-permute-start.7 = (bf16[256,128]{1,0:T(8,128)(2,1)S(1)}, bf16[256,128]{1,0:T(8,128)(2,1)S(1)}, u32[]{:S(2)}, u32[]{:S(2)}) collective-permute-start(bf16[256,128]{1,0:T(8,128)(2,1)S(1)} %get-tuple-element.38), channel_id=1, source_target_pairs={{0,4},{4,0},{8,12},{12,8},{1,5},{5,1},{9,13},{13,9},{2,6},{6,2},{1... | collective-permute-start | bytes 196616 | tf_op jit(solution)/shard_map/ppermute | solution.py:17
  22.6 2.5 %shard_map.106 = bf16[256,2048]{1,0:T(8,128)(2,1)} custom-call(bf16[8,512,128]{2,1,0:T(8,128)(2,1)S(1)} %get-tuple-element.43.site_ref, f32[256,128]{1,0:T(8,128)S(1)} %get-tuple-element.44.table_ref, bf16[128,256]{1,0:T(8,128)(2,1)S(1)} %get-tuple-element.45.refs_4_.refs_0_, bf16[128,256]{1,0:T(8,128)(2,1)S(1)} %collective-permute-done.2.refs_5_.refs_1_, ...), custom_call_target="tpu_custom_call" | custom-call | flops 536870912 | bytes 2490368 | tf_op jit(solution)/shard_map/pallas_call | solution.py:33
  25.0 0.0 collective-permute-done.9
  25.0 0.1 fusion.9
  25.1 3.7 %collective-permute-start.10 = (bf16[192,128]{1,0:T(8,128)(2,1)S(1)}, bf16[192,128]{1,0:T(8,128)(2,1)S(1)}, u32[]{:S(2)}, u32[]{:S(2)}) collective-permute-start(bf16[192,128]{1,0:T(8,128)(2,1)S(1)} %get-tuple-element.53), channel_id=1, source_target_pairs={{0,12},{4,8},{8,4},{12,0},{1,13},{5,9},{9,5},{13,1},{2,14},{6,10},... | collective-permute-start | bytes 147464 | tf_op jit(solution)/shard_map/ppermute | solution.py:17
  28.8 0.0 collective-permute-start.12
  28.8 0.0 collective-permute-done.5
  28.8 0.8 %collective-permute-start.11 = (bf16[192,128]{1,0:T(8,128)(2,1)S(1)}, bf16[192,128]{1,0:T(8,128)(2,1)S(1)}, u32[]{:S(2)}, u32[]{:S(2)}) collective-permute-start(bf16[192,128]{1,0:T(8,128)(2,1)S(1)} %get-tuple-element.55), channel_id=1, source_target_pairs={{0,8},{4,12},{8,0},{12,4},{1,9},{5,13},{9,1},{13,5},{2,10},{6,14},... | collective-permute-start | bytes 147464 | tf_op jit(solution)/shard_map/ppermute | solution.py:17
  29.6 0.0 collective-permute-done.6
  29.6 0.0 collective-permute-done.7
  29.6 1.5 %collective-permute-done.10 = bf16[192,128]{1,0:T(8,128)(2,1)S(1)} collective-permute-done((bf16[192,128]{1,0:T(8,128)(2,1)S(1)}, bf16[192,128]{1,0:T(8,128)(2,1)S(1)}, u32[]{:S(2)}, u32[]{:S(2)}) %collective-permute-start.10) | collective-permute-done | bytes 49184 | tf_op jit(solution)/shard_map/ppermute | solution.py:17
  31.2 1.7 %collective-permute-done.12 = bf16[192,128]{1,0:T(8,128)(2,1)S(1)} collective-permute-done((bf16[192,128]{1,0:T(8,128)(2,1)S(1)}, bf16[192,128]{1,0:T(8,128)(2,1)S(1)}, u32[]{:S(2)}, u32[]{:S(2)}) %collective-permute-start.12) | collective-permute-done | bytes 49184 | tf_op jit(solution)/shard_map/ppermute | solution.py:17
  32.9 0.9 %collective-permute-done.11 = bf16[192,128]{1,0:T(8,128)(2,1)S(1)} collective-permute-done((bf16[192,128]{1,0:T(8,128)(2,1)S(1)}, bf16[192,128]{1,0:T(8,128)(2,1)S(1)}, u32[]{:S(2)}, u32[]{:S(2)}) %collective-permute-start.11) | collective-permute-done | bytes 49184 | tf_op jit(solution)/shard_map/ppermute | solution.py:17
  33.8 0.0 copy-start
  33.8 0.6 %collective-permute-start.13 = (bf16[320,128]{1,0:T(8,128)(2,1)S(1)}, bf16[320,128]{1,0:T(8,128)(2,1)S(1)}, u32[]{:S(2)}, u32[]{:S(2)}) collective-permute-start(bf16[320,128]{1,0:T(8,128)(2,1)S(1)} %pad_maximum_fusion.1), channel_id=1, source_target_pairs={{0,2},{2,0},{1,3},{3,1},{4,6},{6,4},{5,7},{7,5},{8,10},{10,8},{9,1... | collective-permute-start | bytes 245768 | tf_op jit(solution)/shard_map/ppermute | solution.py:17
  34.4 0.1 copy-done
  34.6 0.1 fusion
  34.7 0.0 collective-permute-start.8
  34.8 3.6 %collective-permute-done.13 = bf16[320,128]{1,0:T(8,128)(2,1)S(1)} collective-permute-done((bf16[320,128]{1,0:T(8,128)(2,1)S(1)}, bf16[320,128]{1,0:T(8,128)(2,1)S(1)}, u32[]{:S(2)}, u32[]{:S(2)}) %collective-permute-start.13) | collective-permute-done | bytes 81952 | tf_op jit(solution)/shard_map/ppermute | solution.py:17
  38.4 0.1 collective-permute-start.14
  38.5 0.0 collective-permute-done.8
  38.5 0.6 %maximum_select_fusion.1 = bf16[2,128,128]{2,1,0:T(8,128)(2,1)} fusion(bf16[1,128,128]{2,1,0:T(8,128)(2,1)S(1)} %bitcast.53, bf16[1,128,128]{2,1,0:T(8,128)(2,1)S(1)} %bitcast.50, pred[]{:T(512)S(6)} %eq.11), kind=kLoop, calls=%fused_computation.13 | loop fusion | flops 98304 | bytes 131073 | tf_op jit(solution)/shard_map/jit(_where)/select_n | solution.py:312
  39.2 0.7 %collective-permute-done.14 = bf16[512,128]{1,0:T(8,128)(2,1)S(1)} collective-permute-done((bf16[512,128]{1,0:T(8,128)(2,1)S(1)}, bf16[512,128]{1,0:T(8,128)(2,1)S(1)}, u32[]{:S(2)}, u32[]{:S(2)}) %collective-permute-start.14) | collective-permute-done | bytes 131104 | tf_op jit(solution)/shard_map/ppermute | solution.py:17
  39.9 0.9 %copy.11 = f32[8,128,128]{1,2,0:T(8,128)} copy(bf16[8,128,128]{2,1,0:T(8,128)(2,1)S(1)} %bitcast.45) | data formatting | bytes 786432 | tf_op jit(solution)/shard_map/convert_element_type | solution.py:315
  (12 shorter events, 0.2 us)
Async XLA Ops:
  0.6 8.7 %collective-permute-start.1 = (bf16[256,2048]{1,0:T(8,128)(2,1)}, bf16[256,2048]{1,0:T(8,128)(2,1)S(1)}, u32[]{:S(2)}, u32[]{:S(2)}) collective-permute-start(bf16[256,2048]{1,0:T(8,128)(2,1)} %bitcast.57), channel_id=1, source_target_pairs={{0,1},{1,0},{2,3},{3,2},{4,5},{5,4},{6,7},{7,6},{8,9},{9,8},{10,11... | collective-permute-start | bytes 3145736 | tf_op jit(solution)/shard_map/ppermute | solution.py:17
  2.9 11.5 %collective-permute-start.4 = (bf16[128,256]{1,0:T(8,128)(2,1)S(1)}, bf16[128,256]{1,0:T(8,128)(2,1)S(1)}, u32[]{:S(2)}, u32[]{:S(2)}) collective-permute-start(bf16[128,256]{1,0:T(8,128)(2,1)S(1)} %get-tuple-element.45.refs_4_.refs_0_), channel_id=1, source_target_pairs={{0,12},{4,8},{8,4},{12,0},{1,13},{5,9},{9,5},{13,1},{2,14},{6,10},... | collective-permute-start | bytes 196616 | tf_op jit(solution)/shard_map/ppermute | solution.py:17
  7.5 6.8 %collective-permute-start.3 = (bf16[128,256]{1,0:T(8,128)(2,1)S(1)}, bf16[128,256]{1,0:T(8,128)(2,1)S(1)}, u32[]{:S(2)}, u32[]{:S(2)}) collective-permute-start(bf16[128,256]{1,0:T(8,128)(2,1)S(1)} %get-tuple-element.45.refs_4_.refs_0_), channel_id=1, source_target_pairs={{0,8},{4,12},{8,0},{12,4},{1,9},{5,13},{9,1},{13,5},{2,10},{6,14},... | collective-permute-start | bytes 196616 | tf_op jit(solution)/shard_map/ppermute | solution.py:17
  7.5 6.8 %collective-permute-start.2 = (bf16[128,256]{1,0:T(8,128)(2,1)S(1)}, bf16[128,256]{1,0:T(8,128)(2,1)S(1)}, u32[]{:S(2)}, u32[]{:S(2)}) collective-permute-start(bf16[128,256]{1,0:T(8,128)(2,1)S(1)} %get-tuple-element.45.refs_4_.refs_0_), channel_id=1, source_target_pairs={{0,4},{4,0},{8,12},{12,8},{1,5},{5,1},{9,13},{13,9},{2,6},{6,2},{1... | collective-permute-start | bytes 196616 | tf_op jit(solution)/shard_map/ppermute | solution.py:17
  8.2 1.1 %collective-permute-start = (s32[1,64]{1,0:T(1,128)S(1)}, s32[1,64]{1,0:T(1,128)S(1)}, u32[]{:S(2)}, u32[]{:S(2)}) collective-permute-start(s32[1,64]{1,0:T(1,128)S(1)} %get-tuple-element.27), channel_id=1, source_target_pairs={{0,1},{1,0},{2,3},{3,2},{4,5},{5,4},{6,7},{7,6},{8,9},{9,8},{10,11... | collective-permute-start | bytes 776 | tf_op jit(solution)/shard_map/ppermute | solution.py:17
  16.5 8.6 %collective-permute-start.9 = (bf16[4,192,128]{2,1,0:T(8,128)(2,1)S(1)}, bf16[4,192,128]{2,1,0:T(8,128)(2,1)S(1)}, u32[]{:S(2)}, u32[]{:S(2)}) collective-permute-start(bf16[4,192,128]{2,1,0:T(8,128)(2,1)S(1)} %get-tuple-element.41), channel_id=1, source_target_pairs={{0,2},{2,0},{1,3},{3,1},{4,6},{6,4},{5,7},{7,5},{8,10},{10,8},{9,1... | collective-permute-start | bytes 589832 | tf_op jit(solution)/shard_map/ppermute | solution.py:17
  18.2 10.6 %collective-permute-start.5 = (bf16[256,128]{1,0:T(8,128)(2,1)S(1)}, bf16[256,128]{1,0:T(8,128)(2,1)S(1)}, u32[]{:S(2)}, u32[]{:S(2)}) collective-permute-start(bf16[256,128]{1,0:T(8,128)(2,1)S(1)} %get-tuple-element.36), channel_id=1, source_target_pairs={{0,12},{4,8},{8,4},{12,0},{1,13},{5,9},{9,5},{13,1},{2,14},{6,10},... | collective-permute-start | bytes 196616 | tf_op jit(solution)/shard_map/ppermute | solution.py:17
  21.8 7.8 %collective-permute-start.6 = (bf16[256,128]{1,0:T(8,128)(2,1)S(1)}, bf16[256,128]{1,0:T(8,128)(2,1)S(1)}, u32[]{:S(2)}, u32[]{:S(2)}) collective-permute-start(bf16[256,128]{1,0:T(8,128)(2,1)S(1)} %get-tuple-element.37), channel_id=1, source_target_pairs={{0,8},{4,12},{8,0},{12,4},{1,9},{5,13},{9,1},{13,5},{2,10},{6,14},... | collective-permute-start | bytes 196616 | tf_op jit(solution)/shard_map/ppermute | solution.py:17
  21.8 7.8 %collective-permute-start.7 = (bf16[256,128]{1,0:T(8,128)(2,1)S(1)}, bf16[256,128]{1,0:T(8,128)(2,1)S(1)}, u32[]{:S(2)}, u32[]{:S(2)}) collective-permute-start(bf16[256,128]{1,0:T(8,128)(2,1)S(1)} %get-tuple-element.38), channel_id=1, source_target_pairs={{0,4},{4,0},{8,12},{12,8},{1,5},{5,1},{9,13},{13,9},{2,6},{6,2},{1... | collective-permute-start | bytes 196616 | tf_op jit(solution)/shard_map/ppermute | solution.py:17
  25.1 6.1 %collective-permute-start.10 = (bf16[192,128]{1,0:T(8,128)(2,1)S(1)}, bf16[192,128]{1,0:T(8,128)(2,1)S(1)}, u32[]{:S(2)}, u32[]{:S(2)}) collective-permute-start(bf16[192,128]{1,0:T(8,128)(2,1)S(1)} %get-tuple-element.53), channel_id=1, source_target_pairs={{0,12},{4,8},{8,4},{12,0},{1,13},{5,9},{9,5},{13,1},{2,14},{6,10},... | collective-permute-start | bytes 147464 | tf_op jit(solution)/shard_map/ppermute | solution.py:17
  28.8 4.1 %collective-permute-start.12 = (bf16[192,128]{1,0:T(8,128)(2,1)S(1)}, bf16[192,128]{1,0:T(8,128)(2,1)S(1)}, u32[]{:S(2)}, u32[]{:S(2)}) collective-permute-start(bf16[192,128]{1,0:T(8,128)(2,1)S(1)} %get-tuple-element.54), channel_id=1, source_target_pairs={{0,4},{4,0},{8,12},{12,8},{1,5},{5,1},{9,13},{13,9},{2,6},{6,2},{1... | collective-permute-start | bytes 147464 | tf_op jit(solution)/shard_map/ppermute | solution.py:17
  28.8 5.0 %collective-permute-start.11 = (bf16[192,128]{1,0:T(8,128)(2,1)S(1)}, bf16[192,128]{1,0:T(8,128)(2,1)S(1)}, u32[]{:S(2)}, u32[]{:S(2)}) collective-permute-start(bf16[192,128]{1,0:T(8,128)(2,1)S(1)} %get-tuple-element.55), channel_id=1, source_target_pairs={{0,8},{4,12},{8,0},{12,4},{1,9},{5,13},{9,1},{13,5},{2,10},{6,14},... | collective-permute-start | bytes 147464 | tf_op jit(solution)/shard_map/ppermute | solution.py:17
  33.8 0.8 %copy-start = (bf16[1,128,128]{2,1,0:T(8,128)(2,1)S(1)}, bf16[1,128,128]{2,1,0:T(8,128)(2,1)}, u32[]{:S(2)}) copy-start(bf16[1,128,128]{2,1,0:T(8,128)(2,1)} %param.10) | copy-start | bytes 98308
  33.8 4.5 %collective-permute-start.13 = (bf16[320,128]{1,0:T(8,128)(2,1)S(1)}, bf16[320,128]{1,0:T(8,128)(2,1)S(1)}, u32[]{:S(2)}, u32[]{:S(2)}) collective-permute-start(bf16[320,128]{1,0:T(8,128)(2,1)S(1)} %pad_maximum_fusion.1), channel_id=1, source_target_pairs={{0,2},{2,0},{1,3},{3,1},{4,6},{6,4},{5,7},{7,5},{8,10},{10,8},{9,1... | collective-permute-start | bytes 245768 | tf_op jit(solution)/shard_map/ppermute | solution.py:17
  34.7 3.8 %collective-permute-start.8 = (bf16[128,128]{1,0:T(8,128)(2,1)S(1)}, bf16[128,128]{1,0:T(8,128)(2,1)S(1)}, u32[]{:S(2)}, u32[]{:S(2)}) collective-permute-start(bf16[128,128]{1,0:T(8,128)(2,1)S(1)} %fusion), channel_id=1, source_target_pairs={{0,1},{1,0},{2,3},{3,2},{4,5},{5,4},{6,7},{7,6},{8,9},{9,8},{10,11... | collective-permute-start | bytes 98312 | tf_op jit(solution)/shard_map/ppermute | solution.py:17
  38.4 1.4 %collective-permute-start.14 = (bf16[512,128]{1,0:T(8,128)(2,1)S(1)}, bf16[512,128]{1,0:T(8,128)(2,1)S(1)}, u32[]{:S(2)}, u32[]{:S(2)}) collective-permute-start(bf16[512,128]{1,0:T(8,128)(2,1)S(1)} %get-tuple-element.59), channel_id=1, source_target_pairs={{0,1},{1,0},{2,3},{3,2},{4,5},{5,4},{6,7},{7,6},{8,9},{9,8},{10,11... | collective-permute-start | bytes 393224 | tf_op jit(solution)/shard_map/ppermute | solution.py:17

commit v3 on v0

v3 whole, which is shorter than its diff:
```python
import functools
import jax
import jax.numpy as jnp
from jax import lax
from jax.experimental import pallas as pl
from jax.experimental.pallas import tpu as pltpu
from jax.sharding import PartitionSpec as P

F32 = jnp.float32
BF16 = jnp.bfloat16
NT = (((1,), (1,)), ((), ()))
LIMIT = 28 * 1024 * 1024


def swap(value, axis, bit):
    size = lax.axis_size(axis)
    return lax.ppermute(value, axis, [(place, place ^ bit) for place in range(size)])


def total(*terms):
    acc = terms[0].astype(F32)
    for term in terms[1:]:
        acc = acc + term.astype(F32)
    return acc


def call(kernel, outs, args, scratch=(), flops=0, after=()):
    args = [*args, *after]
    moved = sum(a.size * a.dtype.itemsize for a in args) + sum(
        a.size * a.dtype.itemsize for a in outs
    )
    scalars = pl.BlockSpec(memory_space=pltpu.SMEM)
    vectors = pl.BlockSpec(memory_space=pltpu.VMEM)
    return pl.pallas_call(
        kernel,
        out_shape=list(outs),
        in_specs=[scalars if a.ndim == 1 else vectors for a in args[: len(args) - len(after)]]
        + [pl.BlockSpec(memory_space=pl.ANY)] * len(after),
        out_specs=[vectors] * len(outs),
        scratch_shapes=list(scratch),
        compiler_params=pltpu.CompilerParams(vmem_limit_bytes=LIMIT),
        cost_estimate=pl.CostEstimate(flops=flops if flops >> 34 else 0, bytes_accessed=moved, transcendentals=0),
    )(*args)


def count_of(table_ref, index, height, width):
    row = table_ref[pl.ds(index, 1), :]
    wide = jnp.concatenate([row] * (width // row.shape[1]), axis=1)
    return jnp.broadcast_to(wide, (height, width))


def lanes_kernel(out_ref):
    out_ref[...] = lax.broadcasted_iota(jnp.int32, out_ref.shape, 1)


def grad_kernel(dim_ref, lanes_ref, projector_ref, cotangent_ref, out_ref, live_ref):
    live = jnp.where(lanes_ref[...] < dim_ref[0], 1.0, 0.0)
    live_ref[...] = live
    masked = projector_ref[...].astype(F32) * live[:1]
    out_ref[...] = lax.dot_general(
        masked.astype(BF16), cotangent_ref[...], NT, preferred_element_type=F32
    ).astype(out_ref.dtype)


def forward_kernel(owners, subs, blocks, table_ref, x_ref, site_ref, keep_ref, send_ref, product_ref, sum_ref):
    rows, chi = keep_ref.shape[1:]
    width = site_ref.shape[1]
    step, tile = 2, 32
    rep = lax.axis_index("rep")
    stacked = jnp.concatenate(
        [
            x_ref[pl.ds(pl.multiple_of(half * rows, rows), rows), sub * width : (sub + 1) * width]
            for half in (1 - rep, rep)
            for sub in range(subs)
        ],
        axis=0,
    )
    for low in range(0, blocks, step):
        pair = jnp.concatenate(
            [site_ref[block_at(blocks, low + offset)] for offset in range(step)], axis=1
        )
        product_ref[low // step % 2] = jnp.dot(stacked, pair, preferred_element_type=F32)

        def add(at, low=low):
            for half, out_ref in ((1, keep_ref), (0, sum_ref)):
                pieces = [
                    product_ref[
                        low // step % 2,
                        pl.ds((half * subs + sub) * rows + at, tile),
                        offset * chi : (offset + 1) * chi,
                    ]
                    for sub in range(subs)
                    for offset in range(step)
                ]
                for owner in range(owners):
                    value = None
                    for sub in range(subs):
                        for offset in range(step):
                            index = (owner * subs + sub) * blocks + low + offset
                            term = pieces[sub * step + offset] * count_of(table_ref, index, tile, chi)
                            value = term if value is None else value + term
                    if low:
                        value = value + out_ref[owner, pl.ds(at, tile)]
                    out_ref[owner, pl.ds(at, tile)] = value

        if owners <= 4:
            for at in range(0, rows, tile):
                add(at)
        else:
            pl.loop(0, rows, step=tile)(lambda at: add(pl.multiple_of(at, tile)))
    send_ref[...] = sum_ref[...].astype(send_ref.dtype)


def site_kernel(
    owners, subs, blocks, taken, first, own_table, far_table, x_ref, y_ref, keep_ref, got_ref, *refs
):
    grads, outs, left_ref = refs[:owners], refs[owners:-1], refs[-1]
    chi, rows = grads[0].shape
    width = x_ref.shape[1] // subs
    cut = len(outs) > 1
    whole = [ref[...].astype(F32) for ref in grads]
    parts = [(at, whole) for at in range(first if cut else taken)]
    if cut:
        crossing, staying = outs[owners:]
        share = crossing.shape[1] // (taken - first)
        side = lax.axis_index("block")
        for slot in (1 - side, side):
            mine = pl.ds(pl.multiple_of(slot * share, share), share)
            shared = [ref[mine, :].astype(F32) for ref in grads]
            parts += [(at, shared) for at in range(first, taken)]
    tables = [own_table, far_table]
    for sub in range(2 * subs):
        low = 0
        for at, values in parts:
            height = values[0].shape[0]
            left_ref[low : low + height, sub * rows : (sub + 1) * rows] = pulled_of(
                values, tables[sub // subs], subs, blocks, sub % subs, at
            )
            low += height
    chunk = width // owners
    step = max(1, 256 // chunk) if cut else owners
    for rel in range(0, owners, step):
        columns = []
        for ref in (x_ref, y_ref):
            for sub in range(subs):
                pieces = [
                    ref[:, pl.ds(pl.multiple_of(sub * width + (lax.axis_index("sector") ^ at) * chunk, chunk), chunk)]
                    for at in range(rel, rel + step)
                ]
                columns.append(
                    jnp.concatenate(pieces, axis=1) if cut else ref[:, sub * width : (sub + 1) * width]
                )
        product = jnp.dot(
            left_ref[...], jnp.concatenate(columns, axis=0), preferred_element_type=F32
        )
        if not cut:
            outs[0][...] = product
            return
        straight, middle = first * chi, first * chi + crossing.shape[1]
        for at in range(step):
            lanes = slice(at * chunk, (at + 1) * chunk)
            out = outs[rel + at]
            partial = keep_ref[rel + at] + got_ref[rel + at].astype(F32)
            out[:straight] = product[:straight, lanes].astype(out.dtype)
            out[straight:] = partial.astype(BF16).astype(out.dtype)
            crossing[rel + at] = product[straight:middle, lanes].astype(crossing.dtype)
            staying[rel + at] = product[middle:, lanes].astype(staying.dtype)


def block_at(blocks, at):
    return lax.rem(lax.axis_index("rep") * (blocks // 2) + at, blocks)


def pulled_of(grads, table_ref, subs, blocks, sub, block):
    value = None
    for owner, grad in enumerate(grads):
        index = (owner * subs + sub) * blocks + block
        term = grad * count_of(table_ref, index, *grad.shape)
        value = term if value is None else value + term
    return value.astype(BF16)


def sum_kernel(count, *refs):
    out_ref, rest_ref = refs[-2:]
    upper, lower = total(*[ref[...] for ref in refs[:count]]), total(*[ref[...] for ref in refs[count : 2 * count]])
    straight = out_ref.shape[0] - lower.shape[0]
    out_ref[:straight] = upper[:straight].astype(out_ref.dtype)
    out_ref[straight:] = lower.astype(out_ref.dtype)
    rest_ref[...] = upper[straight:].astype(rest_ref.dtype)


def corner_kernel(owners, subs, blocks, site_ref, table_ref, *refs):
    grads = [ref[...].astype(F32).T for ref in refs[:owners]]
    out, token = refs[-2:]
    token[...] = jnp.zeros(token.shape, token.dtype)
    width = site_ref.shape[1]
    wide = jnp.concatenate(
        [site_ref[block_at(blocks, block)] for block in range(blocks)], axis=1
    )
    for sub in range(subs):
        left = jnp.concatenate(
            [pulled_of(grads, table_ref, subs, blocks, sub, block) for block in range(blocks)],
            axis=1,
        )
        value = lax.dot_general(left, wide, NT, preferred_element_type=F32)
        out[:, sub * width : (sub + 1) * width] = value.astype(out.dtype)


def per_device(corner, site, projector, cotangent, sector_dim, pair_dest, pair_sub, pair_site):
    owners = lax.axis_size("sector")
    sides = lax.axis_size("block")
    me, side, rep = lax.axis_index("sector"), lax.axis_index("block"), lax.axis_index("rep")
    blocks, width, chi = site.shape
    rows = corner.shape[1]
    subs = corner.shape[2] // width
    pairs = pair_dest.shape[0]
    direct = owners * chi == width and sides == 2 and blocks >= 8
    flat = corner[0]
    mine = blocks // 2
    first = mine // 2
    part = rows // 2
    chunk = width // owners
    places = owners * subs * blocks
    shape = jax.ShapeDtypeStruct
    other = swap(flat, "rep", 1)
    def table_of(value):
        if direct:
            stride = subs * blocks
            value = (value // stride ^ me) * stride + value % stride
        value = value // blocks * blocks + (value + rep * mine) % blocks
        hits = (jnp.arange(places, dtype=jnp.int32)[:, None] == value[None, :]).astype(BF16)
        return jnp.dot(hits, jnp.ones((pairs, 128), BF16), preferred_element_type=F32)

    sizes = (owners, subs, blocks)
    combo = (pair_dest * subs + pair_sub) * blocks + pair_site
    lanes = call(lanes_kernel, [shape((8, chi), jnp.int32)], [], flops=1 << 34)[0]
    grad, live = call(
        grad_kernel,
        [shape((chi, rows), BF16), shape((8, chi), F32)],
        [sector_dim, lanes, projector[0], cotangent[0]],
    )
    far = swap(combo, "rep", 1)
    if direct:
        grads = [grad] + [swap(grad, "sector", bit) for bit in range(1, owners)]
    else:
        shared = lax.all_gather(grad, "sector", axis=0)
        grads = [shared[owner] for owner in range(owners)]

    near, distant = table_of(combo), table_of(far)
    keep, send = call(
        functools.partial(forward_kernel, *sizes),
        [shape((owners, part, chi), F32), shape((owners, part, chi), BF16)],
        [near, flat, site],
        [
            pltpu.VMEM((2, 2 * part * subs, 2 * chi), F32),
            pltpu.VMEM((owners, part, chi), F32),
        ],
        flops=4 * subs * rows * width * chi * blocks,
    )
    got = swap(send, "rep", 1)

    def project(enlarged):
        value = jnp.dot(enlarged.astype(BF16), projector[0], preferred_element_type=F32)
        return (value * live[:1]).astype(BF16)

    def corner_term(after):
        return call(
            functools.partial(corner_kernel, *sizes),
            [shape((rows, subs * width), BF16), shape((8, chi), F32)],
            [site, near, *grads],
            flops=2 * subs * rows * width * chi * owners,
            after=[after],
        )

    if direct:
        share = (mine - first) * chi // sides
        height = first * chi + part
        outs = [shape((height, chunk), F32)] + [shape((height, chunk), BF16)] * (owners - 1)
        outs += [shape((owners, share, chunk), BF16), shape((owners, share, chunk), F32)]
    else:
        outs = [shape((mine * chi, width), F32)]
    pieces = call(
        functools.partial(site_kernel, *sizes, mine, first),
        outs,
        [near, distant, flat, other, keep, got, *grads],
        [pltpu.VMEM((mine * chi, 2 * subs * rows), BF16)],
        flops=4 * subs * rows * width * chi * mine,
    )
    if direct:
        bits = range(owners - 1, 0, -1)
        straight = first * chi
        crossed = swap(pieces[owners], "block", 1)
        direct_sums = [pieces[0]] + [swap(pieces[bit], "sector", bit) for bit in bits]
        merged = total(pieces[owners + 1], crossed)
        sent = merged.astype(BF16)
        shared_sums = [merged[0]] + [swap(sent[bit], "sector", bit) for bit in bits]
        corner_grad, token = corner_term(sent)
        both, enlarged = call(
            functools.partial(sum_kernel, owners),
            [shape((straight + share, chunk), BF16), shape((part, chunk), BF16)],
            [*direct_sums, *shared_sums],
            after=[token],
        )
        projected = project(enlarged)
        beside = swap(both, "block", 1)
        upper = total(both[:straight], beside[:straight]).astype(BF16)
        lower, under = [
            value[straight:].reshape(mine - first, chi // sides, chunk) for value in (both, beside)
        ]
        lower = jnp.where(
            side == 0,
            jnp.concatenate([lower, under], axis=1),
            jnp.concatenate([under, lower], axis=1),
        )
        own = jnp.concatenate([upper, lower.reshape(share * sides, chunk)])
        projected = [projected, swap(projected, "rep", 1)]
        there = swap(own, "rep", 1)

        def ordered(pair):
            return jnp.where(rep == 0, jnp.stack(pair), jnp.stack(pair[::-1]))

        corner_new = ordered(projected).reshape(1, rows, chi)
        site_grad = ordered([own, there]).reshape(blocks, chi, chunk).swapaxes(1, 2).astype(F32)
    else:
        term = pieces[0].astype(BF16).reshape(mine, chi, width)
        term = lax.psum_scatter(term, "sector", scatter_dimension=2, tiled=True)
        term = lax.psum(term, "block")
        site_grad = lax.all_gather(term, "rep", axis=0, tiled=True).swapaxes(1, 2).astype(F32)
        partials = (keep + got.astype(F32)).astype(BF16)
        arrived = lax.all_to_all(partials, "sector", split_axis=0, concat_axis=0, tiled=True)
        projected = project(jnp.sum(arrived.astype(F32), axis=0))
        corner_new = lax.all_gather(projected, "rep", axis=0, tiled=True)[None]
        corner_grad = corner_term(term)[0]
    return (corner_new, corner_grad[None], site_grad)


def solution(mesh):
    in_specs = (
        P(("groups", "sector"), "block", "rep"),
        P("groups", None, None),
        P(("groups", "sector"), None, None),
        P(("groups", "sector"), "block", None),
        P(("groups", "sector")),
        P(("groups", "sector", "rep")),
        P(("groups", "sector", "rep")),
        P(("groups", "sector", "rep")),
    )
    out_specs = (
        P(("groups", "sector"), "block", None),
        P(("groups", "sector"), "block", "rep"),
        P("groups", "sector", None),
    )
    return jax.shard_map(
        per_device, mesh=mesh, in_specs=in_specs, out_specs=out_specs, check_vma=False
    )
```

time: 127 us -> 37 us (0.29)
  waiting for transfers between devices: 51.3 us -> 6.47 us
  blocking collectives: 21.3 us -> 0 us
  matrix products: 19.6 us -> 0.39 us
  starting transfers between devices: 5.22 us -> 19.8 us
  between operations: 14.8 us -> 1.6 us
  local copies, waits for them, and re-layouts: 14.3 us -> 1.67 us
  Pallas kernels: 0 us -> 6.02 us
    psum x1 -> x0, waiting for transfers between devices: 29 us -> none  [per_device(): site_grad = lax.psum(site_rows, ('block', 'rep'))]
    reduce_scatter x1 -> x0, waiting for transfers between devices: 22.3 us -> none  [per_device(): lax.psum_scatter(site_part, 'sector', scatter_dimension=1, tiled=True)]
    ppermute x0 -> x16, starting transfers between devices: none -> 19.8 us  [swap(): lax.ppermute(value, axis, [(place, place ^ bit) for place in range(size)])]
    dot_general x8 -> x3, matrix products: 19.6 us -> 0.39 us  [the longest x2 0.26 us: table_of(): jnp.dot(hits, jnp.ones((pairs, 128), BF16), preferred_element_type=F32)]
    all_gather x1 -> x0, blocking collectives: 15.6 us -> none  [per_device(): shared = lax.all_gather(grad_enlarged[None], 'sector', axis=0, tiled=True)]
    ppermute x0 -> x16, waiting for transfers between devices: none -> 6.47 us  [swap(): lax.ppermute(value, axis, [(place, place ^ bit) for place in range(size)])]
    pallas_call x0 -> x6, Pallas kernels: none -> 6.02 us  [call(): pl.pallas_call(kernel, out_shape=list(outs), in_specs=[scalars if a.ndim...]
    psum x1 -> x0, blocking collectives: 5.72 us -> none  [per_device(): summed = lax.psum(partial_value, 'rep')]
  transfers between devices with their start and end apart: 3 -> 16, of which waited for: 2 -> 6; matrix products, arithmetic and copies ran while one was open for 18% -> 3% of each run, Pallas kernels for 0% -> 12%
where the time goes in v3:
time: 37 us; the launch traced here: 36.8 us
  starting transfers between devices  19.8 us (54%)
  waiting for transfers between devices  6.47 us (17%)
  Pallas kernels  6.02 us (16%)
  local copies, waits for them, and re-layouts  1.67 us (5%)
  between operations  1.6 us (4%)
  other arithmetic  0.82 us (2%)
  matrix products  0.39 us (1%)
    ppermute x16, starting transfers between devices, swap(): lax.ppermute(value, axis, [(place, place ^ bit) for place in range(size)])  19.8 us
    ppermute x16, waiting for transfers between devices, swap(): lax.ppermute(value, axis, [(place, place ^ bit) for place in range(size)])  6.47 us
    pallas_call x6, Pallas kernels, call(): pl.pallas_call(kernel, out_shape=list(outs), in_specs=[scalars if a.ndim...  6.02 us
    convert_element_type x1, local copies, waits for them, and re-layouts, per_device(): ordered([own, there]).reshape(blocks, chi, chunk).swapaxes(1, 2).astype(F32)  0.94 us
  transfers between devices with their start and end apart: 16, of which 6 were waited for; matrix products, arithmetic and copies ran while one was open for 3% of the time, Pallas kernels for 12%

profile of v3, /device:TPU:0, one launch (start us, length us, event | category | flops | bytes accessed | tf_op | source)
XLA Modules:
  0.0 36.8 jit_solution(13692586497967251735)
XLA Ops:
  0.6 0.0 copy-start.2
  0.6 0.0 copy-start.3
  0.7 0.0 copy-start
  0.7 0.0 copy-start.1
  0.7 0.5 %collective-permute-start.1 = (bf16[256,2048]{1,0:T(8,128)(2,1)}, bf16[256,2048]{1,0:T(8,128)(2,1)S(1)}, u32[]{:S(2)}, u32[]{:S(2)}) collective-permute-start(bf16[256,2048]{1,0:T(8,128)(2,1)} %bitcast.29), channel_id=1, source_target_pairs={{0,1},{1,0},{2,3},{3,2},{4,5},{5,4},{6,7},{7,6},{8,9},{9,8},{10,11... | collective-permute-start | bytes 3145736 | tf_op jit(solution)/shard_map/ppermute | solution.py:17
  2.0 0.0 copy-done.2
  2.0 0.0 copy-done.3
  2.0 0.2 shard_map.105
  2.1 4.7 %collective-permute-start.5 = (bf16[128,256]{1,0:T(8,128)(2,1)S(1)}, bf16[128,256]{1,0:T(8,128)(2,1)S(1)}, u32[]{:S(2)}, u32[]{:S(2)}) collective-permute-start(bf16[128,256]{1,0:T(8,128)(2,1)S(1)} %get-tuple-element.19.refs_0_), channel_id=1, source_target_pairs={{0,12},{4,8},{8,4},{12,0},{1,13},{5,9},{9,5},{13,1},{2,14},{6,10},... | collective-permute-start | bytes 196616 | tf_op jit(solution)/shard_map/ppermute | solution.py:17
  6.9 0.0 collective-permute-start.4
  6.9 0.6 %collective-permute-start.3 = (bf16[128,256]{1,0:T(8,128)(2,1)S(1)}, bf16[128,256]{1,0:T(8,128)(2,1)S(1)}, u32[]{:S(2)}, u32[]{:S(2)}) collective-permute-start(bf16[128,256]{1,0:T(8,128)(2,1)S(1)} %get-tuple-element.19.refs_0_), channel_id=1, source_target_pairs={{0,4},{4,0},{8,12},{12,8},{1,5},{5,1},{9,13},{13,9},{2,6},{6,2},{1... | collective-permute-start | bytes 196616 | tf_op jit(solution)/shard_map/ppermute | solution.py:17
  7.5 0.0 copy-start.4
  7.5 0.0 copy-start.5
  7.5 0.0 copy-start.6
  7.5 0.6 %copy-done.4 = s32[64]{0:T(128)S(1)} copy-done((s32[64]{0:T(128)S(1)}, s32[64]{0:T(128)}, u32[]{:S(2)}) %copy-start.4) | copy-done | bytes 280
  8.2 0.0 copy-done.5
  8.2 0.0 copy-done.6
  8.2 0.1 collective-permute-start
  8.3 0.1 fusion.1.table_ref.own_table
  8.4 0.0 copy-done
  8.4 0.0 copy-done.1
  8.4 1.9 %shard_map.103 = (f32[4,128,128]{2,1,0:T(8,128)S(1)}, bf16[4,128,128]{2,1,0:T(8,128)(2,1)S(1)}) custom-call(f32[128,128]{1,0:T(8,128)S(1)} %fusion.1.table_ref.own_table, bf16[256,2048]{1,0:T(8,128)(2,1)S(1)} %bitcast.30, bf16[8,512,128]{2,1,0:T(8,128)(2,1)S(1)} %copy-done), custom_call_target="tpu_custom_call" | custom-call | bytes 2555904 | tf_op jit(solution)/shard_map/pallas_call | solution.py:34
  10.3 0.0 collective-permute-done
  10.3 0.6 %collective-permute-start.2 = (bf16[4,128,128]{2,1,0:T(8,128)(2,1)S(1)}, bf16[4,128,128]{2,1,0:T(8,128)(2,1)S(1)}, u32[]{:S(2)}, u32[]{:S(2)}) collective-permute-start(bf16[4,128,128]{2,1,0:T(8,128)(2,1)S(1)} %get-tuple-element.18), channel_id=1, source_target_pairs={{0,1},{1,0},{2,3},{3,2},{4,5},{5,4},{6,7},{7,6},{8,9},{9,8},{10,11... | collective-permute-start | bytes 393224 | tf_op jit(solution)/shard_map/ppermute | solution.py:17
  10.9 0.1 fusion.2.far_table
  11.0 0.0 collective-permute-done.5.refs_3_
  11.1 1.8 %collective-permute-done.4.refs_2_ = bf16[128,256]{1,0:T(8,128)(2,1)S(1)} collective-permute-done((bf16[128,256]{1,0:T(8,128)(2,1)S(1)}, bf16[128,256]{1,0:T(8,128)(2,1)S(1)}, u32[]{:S(2)}, u32[]{:S(2)}) %collective-permute-start.4) | collective-permute-done | bytes 65568 | tf_op jit(solution)/shard_map/ppermute | solution.py:17
  12.8 0.0 collective-permute-done.3.refs_1_
  12.8 0.0 collective-permute-done.2.got_ref
  12.8 0.0 collective-permute-done.1.y_ref
  12.8 1.5 %shard_map.106 = (f32[384,128]{1,0:T(8,128)S(1)}, bf16[384,128]{1,0:T(8,128)(2,1)S(1)}, bf16[384,128]{1,0:T(8,128)(2,1)S(1)}, bf16[384,128]{1,0:T(8,128)(2,1)S(1...) custom-call(f32[128,128]{1,0:T(8,128)S(1)} %fusion.1.table_ref.own_table, ...), custom_call_target="tpu_custom_call" | custom-call | bytes 3768320 | tf_op jit(solution)/shard_map/pallas_call | solution.py:34
  14.4 1.5 %collective-permute-start.9 = (bf16[4,128,128]{2,1,0:T(8,128)(2,1)S(1)}, bf16[4,128,128]{2,1,0:T(8,128)(2,1)S(1)}, u32[]{:S(2)}, u32[]{:S(2)}) collective-permute-start(bf16[4,128,128]{2,1,0:T(8,128)(2,1)S(1)} %get-tuple-element.25), channel_id=1, source_target_pairs={{0,2},{2,0},{1,3},{3,1},{4,6},{6,4},{5,7},{7,5},{8,10},{10,8},{9,1... | collective-permute-start | bytes 393224 | tf_op jit(solution)/shard_map/ppermute | solution.py:17
  15.9 2.8 %collective-permute-start.6 = (bf16[384,128]{1,0:T(8,128)(2,1)S(1)}, bf16[384,128]{1,0:T(8,128)(2,1)S(1)}, u32[]{:S(2)}, u32[]{:S(2)}) collective-permute-start(bf16[384,128]{1,0:T(8,128)(2,1)S(1)} %get-tuple-element.21), channel_id=1, source_target_pairs={{0,12},{4,8},{8,4},{12,0},{1,13},{5,9},{9,5},{13,1},{2,14},{6,10},... | collective-permute-start | bytes 294920 | tf_op jit(solution)/shard_map/ppermute | solution.py:17
  18.7 0.0 collective-permute-start.7
  18.7 1.6 %collective-permute-start.8 = (bf16[384,128]{1,0:T(8,128)(2,1)S(1)}, bf16[384,128]{1,0:T(8,128)(2,1)S(1)}, u32[]{:S(2)}, u32[]{:S(2)}) collective-permute-start(bf16[384,128]{1,0:T(8,128)(2,1)S(1)} %get-tuple-element.23), channel_id=1, source_target_pairs={{0,4},{4,0},{8,12},{12,8},{1,5},{5,1},{9,13},{13,9},{2,6},{6,2},{1... | collective-permute-start | bytes 294920 | tf_op jit(solution)/shard_map/ppermute | solution.py:17
  20.3 0.0 collective-permute-done.9
  20.4 0.5 %collective-permute-start.12 = (bf16[128,128]{1,0:T(8,128)(2,1)S(1)}, bf16[128,128]{1,0:T(8,128)(2,1)S(1)}, u32[]{:S(2)}, u32[]{:S(2)}) collective-permute-start(bf16[128,128]{1,0:T(8,128)(2,1)S(1)} %get-tuple-element.37), channel_id=1, source_target_pairs={{0,4},{4,0},{8,12},{12,8},{1,5},{5,1},{9,13},{13,9},{2,6},{6,2},{1... | collective-permute-start | bytes 98312 | tf_op jit(solution)/shard_map/ppermute | solution.py:17
  20.9 2.9 %collective-permute-start.11 = (bf16[128,128]{1,0:T(8,128)(2,1)S(1)}, bf16[128,128]{1,0:T(8,128)(2,1)S(1)}, u32[]{:S(2)}, u32[]{:S(2)}) collective-permute-start(bf16[128,128]{1,0:T(8,128)(2,1)S(1)} %get-tuple-element.38), channel_id=1, source_target_pairs={{0,8},{4,12},{8,0},{12,4},{1,9},{5,13},{9,1},{13,5},{2,10},{6,14},... | collective-permute-start | bytes 98312 | tf_op jit(solution)/shard_map/ppermute | solution.py:17
  23.8 0.0 collective-permute-done.6.refs_1_
  23.8 2.5 %collective-permute-start.10 = (bf16[128,128]{1,0:T(8,128)(2,1)S(1)}, bf16[128,128]{1,0:T(8,128)(2,1)S(1)}, u32[]{:S(2)}, u32[]{:S(2)}) collective-permute-start(bf16[128,128]{1,0:T(8,128)(2,1)S(1)} %get-tuple-element.39), channel_id=1, source_target_pairs={{0,12},{4,8},{8,4},{12,0},{1,13},{5,9},{9,5},{13,1},{2,14},{6,10},... | collective-permute-start | bytes 98312 | tf_op jit(solution)/shard_map/ppermute | solution.py:17
  26.3 2.4 %shard_map.107 = (bf16[256,2048]{1,0:T(8,128)(2,1)}, f32[8,128]{1,0:T(8,128)S(1)}) custom-call(bf16[8,512,128]{2,1,0:T(8,128)(2,1)S(1)} %copy-done, f32[128,128]{1,0:T(8,128)S(1)} %fusion.1.table_ref.own_table, bf16[128,256]{1,0:T(8,128)(2,1)S(1)} %get-tuple-element.19.refs_0_, bf16[128,256]{1,0:T(8,128)(2,1)S(1)} %collective-permute-done.3.refs_1_, ...), custom_call_target="tpu_custom_call" | custom-call | bytes 2560000 | tf_op jit(solution)/shard_map/pallas_call | solution.py:34
  28.7 0.2 collective-permute-done.7.refs_2_
  28.9 0.0 collective-permute-done.8.refs_3_
  28.9 0.0 collective-permute-done.12.refs_7_
  28.9 0.4 collective-permute-done.11.refs_6_
  29.2 0.3 collective-permute-done.10.refs_5_
  29.6 0.1 shard_map.108
  29.6 1.4 %collective-permute-start.14 = (bf16[384,128]{1,0:T(8,128)(2,1)S(1)}, bf16[384,128]{1,0:T(8,128)(2,1)S(1)}, u32[]{:S(2)}, u32[]{:S(2)}) collective-permute-start(bf16[384,128]{1,0:T(8,128)(2,1)S(1)} %get-tuple-element.30), channel_id=1, source_target_pairs={{0,2},{2,0},{1,3},{3,1},{4,6},{6,4},{5,7},{7,5},{8,10},{10,8},{9,1... | collective-permute-start | bytes 294920 | tf_op jit(solution)/shard_map/ppermute | solution.py:17
  31.0 0.1 fusion
  31.2 0.1 collective-permute-start.13
  31.2 3.1 %collective-permute-done.14 = bf16[384,128]{1,0:T(8,128)(2,1)S(1)} collective-permute-done((bf16[384,128]{1,0:T(8,128)(2,1)S(1)}, bf16[384,128]{1,0:T(8,128)(2,1)S(1)}, u32[]{:S(2)}, u32[]{:S(2)}) %collective-permute-start.14) | collective-permute-done | bytes 98336 | tf_op jit(solution)/shard_map/ppermute | solution.py:17
  34.4 0.1 collective-permute-start.15
  34.5 0.0 collective-permute-done.13
  34.5 0.6 %maximum_select_fusion.1 = bf16[2,128,128]{2,1,0:T(8,128)(2,1)} fusion(bf16[1,128,128]{2,1,0:T(8,128)(2,1)S(1)} %bitcast.42, bf16[1,128,128]{2,1,0:T(8,128)(2,1)S(1)} %bitcast.38, pred[]{:T(512)S(6)} %eq.38), kind=kLoop, calls=%fused_computation.7 | loop fusion | flops 98304 | bytes 131073 | tf_op jit(solution)/shard_map/jit(_where)/select_n | solution.py:320
  35.2 0.7 %collective-permute-done.15 = bf16[512,128]{1,0:T(8,128)(2,1)S(1)} collective-permute-done((bf16[512,128]{1,0:T(8,128)(2,1)S(1)}, bf16[512,128]{1,0:T(8,128)(2,1)S(1)}, u32[]{:S(2)}, u32[]{:S(2)}) %collective-permute-start.15) | collective-permute-done | bytes 131104 | tf_op jit(solution)/shard_map/ppermute | solution.py:17
  35.9 0.9 %copy.11 = f32[8,128,128]{1,2,0:T(8,128)} copy(bf16[8,128,128]{2,1,0:T(8,128)(2,1)S(1)} %bitcast.34) | data formatting | bytes 786432 | tf_op jit(solution)/shard_map/convert_element_type | solution.py:323
  (13 shorter events, 0.2 us)
Async XLA Ops:
  0.6 1.3 %copy-start.2 = (bf16[1,128,128]{2,1,0:T(8,128)(2,1)S(1)}, bf16[1,128,128]{2,1,0:T(8,128)(2,1)}, u32[]{:S(2)}) copy-start(bf16[1,128,128]{2,1,0:T(8,128)(2,1)} %param.10) | copy-start | bytes 98308
  0.6 1.3 %copy-start.3 = (bf16[1,256,128]{2,1,0:T(8,128)(2,1)S(1)}, bf16[1,256,128]{2,1,0:T(8,128)(2,1)}, u32[]{:S(2)}) copy-start(bf16[1,256,128]{2,1,0:T(8,128)(2,1)} %param.11) | copy-start | bytes 196612
  0.7 7.8 %copy-start = (bf16[8,512,128]{2,1,0:T(8,128)(2,1)S(1)}, bf16[8,512,128]{2,1,0:T(8,128)(2,1)}, u32[]{:S(2)}) copy-start(bf16[8,512,128]{2,1,0:T(8,128)(2,1)} %site_ref.3) | copy-start | bytes 3145732
  0.7 7.8 %copy-start.1 = (bf16[1,256,2048]{2,1,0:T(8,128)(2,1)S(1)}, bf16[1,256,2048]{2,1,0:T(8,128)(2,1)}, u32[]{:S(2)}) copy-start(bf16[1,256,2048]{2,1,0:T(8,128)(2,1)} %param.8) | copy-start | bytes 3145732
  0.7 12.2 %collective-permute-start.1 = (bf16[256,2048]{1,0:T(8,128)(2,1)}, bf16[256,2048]{1,0:T(8,128)(2,1)S(1)}, u32[]{:S(2)}, u32[]{:S(2)}) collective-permute-start(bf16[256,2048]{1,0:T(8,128)(2,1)} %bitcast.29), channel_id=1, source_target_pairs={{0,1},{1,0},{2,3},{3,2},{4,5},{5,4},{6,7},{7,6},{8,9},{9,8},{10,11... | collective-permute-start | bytes 3145736 | tf_op jit(solution)/shard_map/ppermute | solution.py:17
  2.1 8.9 %collective-permute-start.5 = (bf16[128,256]{1,0:T(8,128)(2,1)S(1)}, bf16[128,256]{1,0:T(8,128)(2,1)S(1)}, u32[]{:S(2)}, u32[]{:S(2)}) collective-permute-start(bf16[128,256]{1,0:T(8,128)(2,1)S(1)} %get-tuple-element.19.refs_0_), channel_id=1, source_target_pairs={{0,12},{4,8},{8,4},{12,0},{1,13},{5,9},{9,5},{13,1},{2,14},{6,10},... | collective-permute-start | bytes 196616 | tf_op jit(solution)/shard_map/ppermute | solution.py:17
  6.9 6.0 %collective-permute-start.4 = (bf16[128,256]{1,0:T(8,128)(2,1)S(1)}, bf16[128,256]{1,0:T(8,128)(2,1)S(1)}, u32[]{:S(2)}, u32[]{:S(2)}) collective-permute-start(bf16[128,256]{1,0:T(8,128)(2,1)S(1)} %get-tuple-element.19.refs_0_), channel_id=1, source_target_pairs={{0,8},{4,12},{8,0},{12,4},{1,9},{5,13},{9,1},{13,5},{2,10},{6,14},... | collective-permute-start | bytes 196616 | tf_op jit(solution)/shard_map/ppermute | solution.py:17
  6.9 6.0 %collective-permute-start.3 = (bf16[128,256]{1,0:T(8,128)(2,1)S(1)}, bf16[128,256]{1,0:T(8,128)(2,1)S(1)}, u32[]{:S(2)}, u32[]{:S(2)}) collective-permute-start(bf16[128,256]{1,0:T(8,128)(2,1)S(1)} %get-tuple-element.19.refs_0_), channel_id=1, source_target_pairs={{0,4},{4,0},{8,12},{12,8},{1,5},{5,1},{9,13},{13,9},{2,6},{6,2},{1... | collective-permute-start | bytes 196616 | tf_op jit(solution)/shard_map/ppermute | solution.py:17
  7.5 0.7 %copy-start.4 = (s32[64]{0:T(128)S(1)}, s32[64]{0:T(128)}, u32[]{:S(2)}) copy-start(s32[64]{0:T(128)} %param.15) | copy-start | bytes 772
  7.5 0.7 %copy-start.5 = (s32[64]{0:T(128)S(1)}, s32[64]{0:T(128)}, u32[]{:S(2)}) copy-start(s32[64]{0:T(128)} %param.14) | copy-start | bytes 772
  7.5 0.7 %copy-start.6 = (s32[64]{0:T(128)S(1)}, s32[64]{0:T(128)}, u32[]{:S(2)}) copy-start(s32[64]{0:T(128)} %param.13) | copy-start | bytes 772
  8.2 2.1 %collective-permute-start = (s32[64]{0:T(128)S(1)}, s32[64]{0:T(128)S(1)}, u32[]{:S(2)}, u32[]{:S(2)}) collective-permute-start(s32[64]{0:T(128)S(1)} %get-tuple-element.34), channel_id=1, source_target_pairs={{0,1},{1,0},{2,3},{3,2},{4,5},{5,4},{6,7},{7,6},{8,9},{9,8},{10,11... | collective-permute-start | bytes 776 | tf_op jit(solution)/shard_map/ppermute | solution.py:17
  10.3 2.5 %collective-permute-start.2 = (bf16[4,128,128]{2,1,0:T(8,128)(2,1)S(1)}, bf16[4,128,128]{2,1,0:T(8,128)(2,1)S(1)}, u32[]{:S(2)}, u32[]{:S(2)}) collective-permute-start(bf16[4,128,128]{2,1,0:T(8,128)(2,1)S(1)} %get-tuple-element.18), channel_id=1, source_target_pairs={{0,1},{1,0},{2,3},{3,2},{4,5},{5,4},{6,7},{7,6},{8,9},{9,8},{10,11... | collective-permute-start | bytes 393224 | tf_op jit(solution)/shard_map/ppermute | solution.py:17
  14.4 5.9 %collective-permute-start.9 = (bf16[4,128,128]{2,1,0:T(8,128)(2,1)S(1)}, bf16[4,128,128]{2,1,0:T(8,128)(2,1)S(1)}, u32[]{:S(2)}, u32[]{:S(2)}) collective-permute-start(bf16[4,128,128]{2,1,0:T(8,128)(2,1)S(1)} %get-tuple-element.25), channel_id=1, source_target_pairs={{0,2},{2,0},{1,3},{3,1},{4,6},{6,4},{5,7},{7,5},{8,10},{10,8},{9,1... | collective-permute-start | bytes 393224 | tf_op jit(solution)/shard_map/ppermute | solution.py:17
  15.9 7.9 %collective-permute-start.6 = (bf16[384,128]{1,0:T(8,128)(2,1)S(1)}, bf16[384,128]{1,0:T(8,128)(2,1)S(1)}, u32[]{:S(2)}, u32[]{:S(2)}) collective-permute-start(bf16[384,128]{1,0:T(8,128)(2,1)S(1)} %get-tuple-element.21), channel_id=1, source_target_pairs={{0,12},{4,8},{8,4},{12,0},{1,13},{5,9},{9,5},{13,1},{2,14},{6,10},... | collective-permute-start | bytes 294920 | tf_op jit(solution)/shard_map/ppermute | solution.py:17
  18.7 10.1 %collective-permute-start.7 = (bf16[384,128]{1,0:T(8,128)(2,1)S(1)}, bf16[384,128]{1,0:T(8,128)(2,1)S(1)}, u32[]{:S(2)}, u32[]{:S(2)}) collective-permute-start(bf16[384,128]{1,0:T(8,128)(2,1)S(1)} %get-tuple-element.22), channel_id=1, source_target_pairs={{0,8},{4,12},{8,0},{12,4},{1,9},{5,13},{9,1},{13,5},{2,10},{6,14},... | collective-permute-start | bytes 294920 | tf_op jit(solution)/shard_map/ppermute | solution.py:17
  18.7 10.1 %collective-permute-start.8 = (bf16[384,128]{1,0:T(8,128)(2,1)S(1)}, bf16[384,128]{1,0:T(8,128)(2,1)S(1)}, u32[]{:S(2)}, u32[]{:S(2)}) collective-permute-start(bf16[384,128]{1,0:T(8,128)(2,1)S(1)} %get-tuple-element.23), channel_id=1, source_target_pairs={{0,4},{4,0},{8,12},{12,8},{1,5},{5,1},{9,13},{13,9},{2,6},{6,2},{1... | collective-permute-start | bytes 294920 | tf_op jit(solution)/shard_map/ppermute | solution.py:17
  20.4 8.5 %collective-permute-start.12 = (bf16[128,128]{1,0:T(8,128)(2,1)S(1)}, bf16[128,128]{1,0:T(8,128)(2,1)S(1)}, u32[]{:S(2)}, u32[]{:S(2)}) collective-permute-start(bf16[128,128]{1,0:T(8,128)(2,1)S(1)} %get-tuple-element.37), channel_id=1, source_target_pairs={{0,4},{4,0},{8,12},{12,8},{1,5},{5,1},{9,13},{13,9},{2,6},{6,2},{1... | collective-permute-start | bytes 98312 | tf_op jit(solution)/shard_map/ppermute | solution.py:17
  20.9 8.3 %collective-permute-start.11 = (bf16[128,128]{1,0:T(8,128)(2,1)S(1)}, bf16[128,128]{1,0:T(8,128)(2,1)S(1)}, u32[]{:S(2)}, u32[]{:S(2)}) collective-permute-start(bf16[128,128]{1,0:T(8,128)(2,1)S(1)} %get-tuple-element.38), channel_id=1, source_target_pairs={{0,8},{4,12},{8,0},{12,4},{1,9},{5,13},{9,1},{13,5},{2,10},{6,14},... | collective-permute-start | bytes 98312 | tf_op jit(solution)/shard_map/ppermute | solution.py:17
  23.8 5.8 %collective-permute-start.10 = (bf16[128,128]{1,0:T(8,128)(2,1)S(1)}, bf16[128,128]{1,0:T(8,128)(2,1)S(1)}, u32[]{:S(2)}, u32[]{:S(2)}) collective-permute-start(bf16[128,128]{1,0:T(8,128)(2,1)S(1)} %get-tuple-element.39), channel_id=1, source_target_pairs={{0,12},{4,8},{8,4},{12,0},{1,13},{5,9},{9,5},{13,1},{2,14},{6,10},... | collective-permute-start | bytes 98312 | tf_op jit(solution)/shard_map/ppermute | solution.py:17
  29.6 4.7 %collective-permute-start.14 = (bf16[384,128]{1,0:T(8,128)(2,1)S(1)}, bf16[384,128]{1,0:T(8,128)(2,1)S(1)}, u32[]{:S(2)}, u32[]{:S(2)}) collective-permute-start(bf16[384,128]{1,0:T(8,128)(2,1)S(1)} %get-tuple-element.30), channel_id=1, source_target_pairs={{0,2},{2,0},{1,3},{3,1},{4,6},{6,4},{5,7},{7,5},{8,10},{10,8},{9,1... | collective-permute-start | bytes 294920 | tf_op jit(solution)/shard_map/ppermute | solution.py:17
  31.2 3.3 %collective-permute-start.13 = (bf16[128,128]{1,0:T(8,128)(2,1)S(1)}, bf16[128,128]{1,0:T(8,128)(2,1)S(1)}, u32[]{:S(2)}, u32[]{:S(2)}) collective-permute-start(bf16[128,128]{1,0:T(8,128)(2,1)S(1)} %fusion), channel_id=1, source_target_pairs={{0,1},{1,0},{2,3},{3,2},{4,5},{5,4},{6,7},{7,6},{8,9},{9,8},{10,11... | collective-permute-start | bytes 98312 | tf_op jit(solution)/shard_map/ppermute | solution.py:17
  34.4 1.4 %collective-permute-start.15 = (bf16[512,128]{1,0:T(8,128)(2,1)S(1)}, bf16[512,128]{1,0:T(8,128)(2,1)S(1)}, u32[]{:S(2)}, u32[]{:S(2)}) collective-permute-start(bf16[512,128]{1,0:T(8,128)(2,1)S(1)} %get-tuple-element.36), channel_id=1, source_target_pairs={{0,1},{1,0},{2,3},{3,2},{4,5},{5,4},{6,7},{7,6},{8,9},{9,8},{10,11... | collective-permute-start | bytes 393224 | tf_op jit(solution)/shard_map/ppermute | solution.py:17

commit v4 on v3

--- a/solution.py
+++ b/solution.py
@@ -24,7 +24,7 @@
     return acc
 
 
-def call(kernel, outs, args, scratch=(), flops=0, after=()):
+def call(kernel, outs, args, scratch=(), flops=0, after=(), stores=0):
     args = [*args, *after]
     moved = sum(a.size * a.dtype.itemsize for a in args) + sum(
         a.size * a.dtype.itemsize for a in outs
@@ -36,7 +36,7 @@
         out_shape=list(outs),
         in_specs=[scalars if a.ndim == 1 else vectors for a in args[: len(args) - len(after)]]
         + [pl.BlockSpec(memory_space=pl.ANY)] * len(after),
-        out_specs=[vectors] * len(outs),
+        out_specs=[pl.BlockSpec(memory_space=pltpu.HBM)] * stores + [vectors] * (len(outs) - stores),
         scratch_shapes=list(scratch),
         compiler_params=pltpu.CompilerParams(vmem_limit_bytes=LIMIT),
         cost_estimate=pl.CostEstimate(flops=flops if flops >> 34 else 0, bytes_accessed=moved, transcendentals=0),
@@ -180,30 +180,55 @@
     return value.astype(BF16)
 
 
-def sum_kernel(count, *refs):
+def straight_kernel(*refs):
     out_ref, rest_ref = refs[-2:]
-    upper, lower = total(*[ref[...] for ref in refs[:count]]), total(*[ref[...] for ref in refs[count : 2 * count]])
-    straight = out_ref.shape[0] - lower.shape[0]
-    out_ref[:straight] = upper[:straight].astype(out_ref.dtype)
-    out_ref[straight:] = lower.astype(out_ref.dtype)
-    rest_ref[...] = upper[straight:].astype(rest_ref.dtype)
+    value = total(*[ref[...] for ref in refs[:-3]])
+    straight = out_ref.shape[0]
+    out_ref[...] = value[:straight].astype(out_ref.dtype)
+    rest_ref[...] = value[straight:].astype(rest_ref.dtype)
+
+
+def shared_kernel(*refs):
+    refs[-1][...] = total(*[ref[...] for ref in refs[:-1]]).astype(refs[-1].dtype)
+
+
+def share_kernel(parts, upper_ref, over_ref, lower_ref, under_ref, unread, out_ref):
+    side = lax.axis_index("block")
+    straight = upper_ref.shape[0]
+    out_ref[:straight] = total(upper_ref[...], over_ref[...]).astype(out_ref.dtype)
+    share = lower_ref.shape[0] // parts
+    for part in range(parts):
+        for ref, slot in ((lower_ref, side), (under_ref, 1 - side)):
+            low = pl.multiple_of(straight + (2 * part + slot) * share, share)
+            out_ref[pl.ds(low, share)] = ref[part * share : (part + 1) * share]
 
 
 def corner_kernel(owners, subs, blocks, site_ref, table_ref, *refs):
     grads = [ref[...].astype(F32).T for ref in refs[:owners]]
-    out, token = refs[-2:]
-    token[...] = jnp.zeros(token.shape, token.dtype)
+    out = refs[-1]
+    rows = grads[0].shape[0]
     width = site_ref.shape[1]
-    wide = jnp.concatenate(
-        [site_ref[block_at(blocks, block)] for block in range(blocks)], axis=1
-    )
+    wide = jnp.concatenate([site_ref[block_at(blocks, block)] for block in range(blocks)], axis=1)
+    left = jnp.concatenate(
+        [
+            jnp.concatenate(
+                [pulled_of(grads, table_ref, subs, blocks, sub, block) for block in range(blocks)],
+                axis=1,
+            )
+            for sub in range(subs)
+        ],
+        axis=0,
+    )
+    value = lax.dot_general(left, wide, NT, preferred_element_type=F32)
     for sub in range(subs):
-        left = jnp.concatenate(
-            [pulled_of(grads, table_ref, subs, blocks, sub, block) for block in range(blocks)],
-            axis=1,
-        )
-        value = lax.dot_general(left, wide, NT, preferred_element_type=F32)
-        out[:, sub * width : (sub + 1) * width] = value.astype(out.dtype)
+        out[:, sub * width : (sub + 1) * width] = value[sub * rows : (sub + 1) * rows].astype(out.dtype)
+
+
+def store_kernel(value_ref, unread, out_hbm, token_ref, stored):
+    copy = pltpu.make_async_copy(value_ref, out_hbm, stored)
+    copy.start()
+    token_ref[...] = jnp.zeros(token_ref.shape, token_ref.dtype)
+    copy.wait()
 
 
 def per_device(corner, site, projector, cotangent, sector_dim, pair_dest, pair_sub, pair_site):
@@ -266,11 +291,11 @@
     def corner_term(after):
         return call(
             functools.partial(corner_kernel, *sizes),
-            [shape((rows, subs * width), BF16), shape((8, chi), F32)],
+            [shape((rows, subs * width), BF16)],
             [site, near, *grads],
             flops=2 * subs * rows * width * chi * owners,
             after=[after],
-        )
+        )[0]
 
     if direct:
         share = (mine - first) * chi // sides
@@ -294,25 +319,31 @@
         merged = total(pieces[owners + 1], crossed)
         sent = merged.astype(BF16)
         shared_sums = [merged[0]] + [swap(sent[bit], "sector", bit) for bit in bits]
-        corner_grad, token = corner_term(sent)
-        both, enlarged = call(
-            functools.partial(sum_kernel, owners),
-            [shape((straight + share, chunk), BF16), shape((part, chunk), BF16)],
-            [*direct_sums, *shared_sums],
+        corner_grad = corner_term(sent)
+        upper, enlarged = call(
+            straight_kernel,
+            [shape((straight, chunk), BF16), shape((part, chunk), BF16)],
+            direct_sums,
+            after=[corner_grad],
+        )
+        over = swap(upper, "block", 1)
+        projected = project(enlarged)
+        lower = call(shared_kernel, [shape((share, chunk), BF16)], shared_sums)[0]
+        under = swap(lower, "block", 1)
+        corner_grad, token = call(
+            store_kernel,
+            [shape(corner_grad.shape, BF16), shape((8, chi), F32)],
+            [corner_grad],
+            [pltpu.SemaphoreType.DMA],
+            after=[lower],
+            stores=1,
+        )
+        own = call(
+            functools.partial(share_kernel, mine - first),
+            [shape((straight + share * sides, chunk), BF16)],
+            [upper, over, lower, under],
             after=[token],
-        )
-        projected = project(enlarged)
-        beside = swap(both, "block", 1)
-        upper = total(both[:straight], beside[:straight]).astype(BF16)
-        lower, under = [
-            value[straight:].reshape(mine - first, chi // sides, chunk) for value in (both, beside)
-        ]
-        lower = jnp.where(
-            side == 0,
-            jnp.concatenate([lower, under], axis=1),
-            jnp.concatenate([under, lower], axis=1),
-        )
-        own = jnp.concatenate([upper, lower.reshape(share * sides, chunk)])
+        )[0]
         projected = [projected, swap(projected, "rep", 1)]
         there = swap(own, "rep", 1)
 
@@ -330,7 +361,7 @@
         arrived = lax.all_to_all(partials, "sector", split_axis=0, concat_axis=0, tiled=True)
         projected = project(jnp.sum(arrived.astype(F32), axis=0))
         corner_new = lax.all_gather(projected, "rep", axis=0, tiled=True)[None]
-        corner_grad = corner_term(term)[0]
+        corner_grad = corner_term(term)
     return (corner_new, corner_grad[None], site_grad)
 
 

time: 37 us -> 36.2 us (0.978)
  waiting for transfers between devices: 6.47 us -> 5.08 us
  starting transfers between devices: 19.8 us -> 20.6 us
    ppermute x16 -> x17, waiting for transfers between devices: 6.47 us -> 5.08 us  [swap(): lax.ppermute(value, axis, [(place, place ^ bit) for place in range(size)])]
    ppermute x16 -> x17, starting transfers between devices: 19.8 us -> 20.6 us  [swap(): lax.ppermute(value, axis, [(place, place ^ bit) for place in range(size)])]
    pallas_call x6 -> x9, Pallas kernels: 6.02 us -> 5.98 us  [call(): pl.pallas_call(kernel, out_shape=list(outs), in_specs=[scalars if a.ndim...]
  transfers between devices with their start and end apart: 16 -> 17, of which waited for: 6 -> 4; matrix products, arithmetic and copies ran while one was open for 3% -> 3% of each run, Pallas kernels for 12% -> 12%
where the time goes in v4:
time: 36.2 us; the launch traced here: 36 us
  starting transfers between devices  20.6 us (57%)
  Pallas kernels  5.98 us (17%)
  waiting for transfers between devices  5.08 us (14%)
  local copies, waits for them, and re-layouts  1.66 us (5%)
  between operations  1.59 us (4%)
  other arithmetic  0.75 us (2%)
  matrix products  0.39 us (1%)
    ppermute x17, starting transfers between devices, swap(): lax.ppermute(value, axis, [(place, place ^ bit) for place in range(size)])  20.6 us
    pallas_call x9, Pallas kernels, call(): pl.pallas_call(kernel, out_shape=list(outs), in_specs=[scalars if a.ndim...  5.98 us
    ppermute x17, waiting for transfers between devices, swap(): lax.ppermute(value, axis, [(place, place ^ bit) for place in range(size)])  5.08 us
    convert_element_type x1, local copies, waits for them, and re-layouts, per_device(): ordered([own, there]).reshape(blocks, chi, chunk).swapaxes(1, 2).astype(F32)  0.94 us
  transfers between devices with their start and end apart: 17, of which 4 were waited for; matrix products, arithmetic and copies ran while one was open for 3% of the time, Pallas kernels for 12%

profile of v4, /device:TPU:0, one launch (start us, length us, event | category | flops | bytes accessed | tf_op | source)
XLA Modules:
  0.0 36.0 jit_solution(14528112918228572483)
XLA Ops:
  0.6 0.0 copy-start.2
  0.6 0.0 copy-start.3
  0.7 0.0 copy-start
  0.7 0.0 copy-start.1
  0.7 0.5 %collective-permute-start.1 = (bf16[256,2048]{1,0:T(8,128)(2,1)}, bf16[256,2048]{1,0:T(8,128)(2,1)S(1)}, u32[]{:S(2)}, u32[]{:S(2)}) collective-permute-start(bf16[256,2048]{1,0:T(8,128)(2,1)} %bitcast.25), channel_id=1, source_target_pairs={{0,1},{1,0},{2,3},{3,2},{4,5},{5,4},{6,7},{7,6},{8,9},{9,8},{10,11... | collective-permute-start | bytes 3145736 | tf_op jit(solution)/shard_map/ppermute | solution.py:17
  2.0 0.0 copy-done.2
  2.0 0.0 copy-done.3
  2.0 0.2 shard_map.105
  2.1 4.7 %collective-permute-start.5 = (bf16[128,256]{1,0:T(8,128)(2,1)S(1)}, bf16[128,256]{1,0:T(8,128)(2,1)S(1)}, u32[]{:S(2)}, u32[]{:S(2)}) collective-permute-start(bf16[128,256]{1,0:T(8,128)(2,1)S(1)} %get-tuple-element.19.refs_0_), channel_id=1, source_target_pairs={{0,12},{4,8},{8,4},{12,0},{1,13},{5,9},{9,5},{13,1},{2,14},{6,10},... | collective-permute-start | bytes 196616 | tf_op jit(solution)/shard_map/ppermute | solution.py:17
  6.9 0.0 collective-permute-start.4
  6.9 0.6 %collective-permute-start.3 = (bf16[128,256]{1,0:T(8,128)(2,1)S(1)}, bf16[128,256]{1,0:T(8,128)(2,1)S(1)}, u32[]{:S(2)}, u32[]{:S(2)}) collective-permute-start(bf16[128,256]{1,0:T(8,128)(2,1)S(1)} %get-tuple-element.19.refs_0_), channel_id=1, source_target_pairs={{0,4},{4,0},{8,12},{12,8},{1,5},{5,1},{9,13},{13,9},{2,6},{6,2},{1... | collective-permute-start | bytes 196616 | tf_op jit(solution)/shard_map/ppermute | solution.py:17
  7.5 0.0 copy-start.4
  7.5 0.0 copy-start.5
  7.5 0.0 copy-start.6
  7.5 0.6 %copy-done.4 = s32[64]{0:T(128)S(1)} copy-done((s32[64]{0:T(128)S(1)}, s32[64]{0:T(128)}, u32[]{:S(2)}) %copy-start.4) | copy-done | bytes 280
  8.2 0.0 copy-done.5
  8.2 0.0 copy-done.6
  8.2 0.1 collective-permute-start
  8.3 0.1 fusion.1.table_ref.own_table
  8.4 0.0 copy-done
  8.4 0.0 copy-done.1
  8.4 1.9 %shard_map.103 = (f32[4,128,128]{2,1,0:T(8,128)S(1)}, bf16[4,128,128]{2,1,0:T(8,128)(2,1)S(1)}) custom-call(f32[128,128]{1,0:T(8,128)S(1)} %fusion.1.table_ref.own_table, bf16[256,2048]{1,0:T(8,128)(2,1)S(1)} %bitcast.26, bf16[8,512,128]{2,1,0:T(8,128)(2,1)S(1)} %copy-done), custom_call_target="tpu_custom_call" | custom-call | bytes 2555904 | tf_op jit(solution)/shard_map/pallas_call | solution.py:34
  10.3 0.0 collective-permute-done
  10.3 0.6 %collective-permute-start.2 = (bf16[4,128,128]{2,1,0:T(8,128)(2,1)S(1)}, bf16[4,128,128]{2,1,0:T(8,128)(2,1)S(1)}, u32[]{:S(2)}, u32[]{:S(2)}) collective-permute-start(bf16[4,128,128]{2,1,0:T(8,128)(2,1)S(1)} %get-tuple-element.18), channel_id=1, source_target_pairs={{0,1},{1,0},{2,3},{3,2},{4,5},{5,4},{6,7},{7,6},{8,9},{9,8},{10,11... | collective-permute-start | bytes 393224 | tf_op jit(solution)/shard_map/ppermute | solution.py:17
  10.9 0.1 fusion.2.far_table
  11.0 0.0 collective-permute-done.5.refs_3_
  11.1 1.8 %collective-permute-done.4.refs_2_ = bf16[128,256]{1,0:T(8,128)(2,1)S(1)} collective-permute-done((bf16[128,256]{1,0:T(8,128)(2,1)S(1)}, bf16[128,256]{1,0:T(8,128)(2,1)S(1)}, u32[]{:S(2)}, u32[]{:S(2)}) %collective-permute-start.4) | collective-permute-done | bytes 65568 | tf_op jit(solution)/shard_map/ppermute | solution.py:17
  12.8 0.0 collective-permute-done.3.refs_1_
  12.8 0.0 collective-permute-done.2.got_ref
  12.8 0.0 collective-permute-done.1.y_ref
  12.8 1.5 %shard_map.106 = (f32[384,128]{1,0:T(8,128)S(1)}, bf16[384,128]{1,0:T(8,128)(2,1)S(1)}, bf16[384,128]{1,0:T(8,128)(2,1)S(1)}, bf16[384,128]{1,0:T(8,128)(2,1)S(1...) custom-call(f32[128,128]{1,0:T(8,128)S(1)} %fusion.1.table_ref.own_table, ...), custom_call_target="tpu_custom_call" | custom-call | bytes 3768320 | tf_op jit(solution)/shard_map/pallas_call | solution.py:34
  14.4 1.5 %collective-permute-start.9 = (bf16[4,128,128]{2,1,0:T(8,128)(2,1)S(1)}, bf16[4,128,128]{2,1,0:T(8,128)(2,1)S(1)}, u32[]{:S(2)}, u32[]{:S(2)}) collective-permute-start(bf16[4,128,128]{2,1,0:T(8,128)(2,1)S(1)} %get-tuple-element.25), channel_id=1, source_target_pairs={{0,2},{2,0},{1,3},{3,1},{4,6},{6,4},{5,7},{7,5},{8,10},{10,8},{9,1... | collective-permute-start | bytes 393224 | tf_op jit(solution)/shard_map/ppermute | solution.py:17
  15.9 2.8 %collective-permute-start.6 = (bf16[384,128]{1,0:T(8,128)(2,1)S(1)}, bf16[384,128]{1,0:T(8,128)(2,1)S(1)}, u32[]{:S(2)}, u32[]{:S(2)}) collective-permute-start(bf16[384,128]{1,0:T(8,128)(2,1)S(1)} %get-tuple-element.21), channel_id=1, source_target_pairs={{0,12},{4,8},{8,4},{12,0},{1,13},{5,9},{9,5},{13,1},{2,14},{6,10},... | collective-permute-start | bytes 294920 | tf_op jit(solution)/shard_map/ppermute | solution.py:17
  18.7 0.0 collective-permute-start.7
  18.7 1.6 %collective-permute-start.8 = (bf16[384,128]{1,0:T(8,128)(2,1)S(1)}, bf16[384,128]{1,0:T(8,128)(2,1)S(1)}, u32[]{:S(2)}, u32[]{:S(2)}) collective-permute-start(bf16[384,128]{1,0:T(8,128)(2,1)S(1)} %get-tuple-element.23), channel_id=1, source_target_pairs={{0,4},{4,0},{8,12},{12,8},{1,5},{5,1},{9,13},{13,9},{2,6},{6,2},{1... | collective-permute-start | bytes 294920 | tf_op jit(solution)/shard_map/ppermute | solution.py:17
  20.3 0.0 collective-permute-done.9
  20.4 0.5 %collective-permute-start.13 = (bf16[128,128]{1,0:T(8,128)(2,1)S(1)}, bf16[128,128]{1,0:T(8,128)(2,1)S(1)}, u32[]{:S(2)}, u32[]{:S(2)}) collective-permute-start(bf16[128,128]{1,0:T(8,128)(2,1)S(1)} %get-tuple-element.35), channel_id=1, source_target_pairs={{0,4},{4,0},{8,12},{12,8},{1,5},{5,1},{9,13},{13,9},{2,6},{6,2},{1... | collective-permute-start | bytes 98312 | tf_op jit(solution)/shard_map/ppermute | solution.py:17
  20.9 2.9 %collective-permute-start.12 = (bf16[128,128]{1,0:T(8,128)(2,1)S(1)}, bf16[128,128]{1,0:T(8,128)(2,1)S(1)}, u32[]{:S(2)}, u32[]{:S(2)}) collective-permute-start(bf16[128,128]{1,0:T(8,128)(2,1)S(1)} %get-tuple-element.36), channel_id=1, source_target_pairs={{0,8},{4,12},{8,0},{12,4},{1,9},{5,13},{9,1},{13,5},{2,10},{6,14},... | collective-permute-start | bytes 98312 | tf_op jit(solution)/shard_map/ppermute | solution.py:17
  23.8 0.0 collective-permute-done.6.refs_1_
  23.8 2.5 %collective-permute-start.11 = (bf16[128,128]{1,0:T(8,128)(2,1)S(1)}, bf16[128,128]{1,0:T(8,128)(2,1)S(1)}, u32[]{:S(2)}, u32[]{:S(2)}) collective-permute-start(bf16[128,128]{1,0:T(8,128)(2,1)S(1)} %get-tuple-element.37), channel_id=1, source_target_pairs={{0,12},{4,8},{8,4},{12,0},{1,13},{5,9},{9,5},{13,1},{2,14},{6,10},... | collective-permute-start | bytes 98312 | tf_op jit(solution)/shard_map/ppermute | solution.py:17
  26.3 1.3 %shard_map.107.refs_4_.value_ref = bf16[256,2048]{1,0:T(8,128)(2,1)S(1)} custom-call(bf16[8,512,128]{2,1,0:T(8,128)(2,1)S(1)} %copy-done, f32[128,128]{1,0:T(8,128)S(1)} %fusion.1.table_ref.own_table, bf16[128,256]{1,0:T(8,128)(2,1)S(1)} %get-tuple-element.19.refs_0_, bf16[128,256]{1,0:T(8,128)(2,1)S(1)} %collective-permute-done.3.refs_1_, ...), custom_call_target="tpu_custom_call" | custom-call | bytes 2555904 | tf_op jit(solution)/shard_map/pallas_call | solution.py:34
  27.6 1.3 %collective-permute-done.7.refs_2_ = bf16[384,128]{1,0:T(8,128)(2,1)S(1)} collective-permute-done((bf16[384,128]{1,0:T(8,128)(2,1)S(1)}, bf16[384,128]{1,0:T(8,128)(2,1)S(1)}, u32[]{:S(2)}, u32[]{:S(2)}) %collective-permute-start.7) | collective-permute-done | bytes 98336 | tf_op jit(solution)/shard_map/ppermute | solution.py:17
  28.9 0.0 collective-permute-done.8.refs_3_
  28.9 0.6 %collective-permute-start.14 = (bf16[256,128]{1,0:T(8,128)(2,1)S(1)}, bf16[256,128]{1,0:T(8,128)(2,1)S(1)}, u32[]{:S(2)}, u32[]{:S(2)}) collective-permute-start(bf16[256,128]{1,0:T(8,128)(2,1)S(1)} %get-tuple-element.29.upper_ref), channel_id=1, source_target_pairs={{0,2},{2,0},{1,3},{3,1},{4,6},{6,4},{5,7},{7,5},{8,10},{10,8},{9,1... | collective-permute-start | bytes 196616 | tf_op jit(solution)/shard_map/ppermute | solution.py:17
  29.5 0.0 collective-permute-done.13.refs_3_
  29.5 0.0 collective-permute-done.12.refs_2_
  29.5 0.0 collective-permute-done.11.refs_1_
  29.6 1.5 %collective-permute-start.15 = (bf16[128,128]{1,0:T(8,128)(2,1)S(1)}, bf16[128,128]{1,0:T(8,128)(2,1)S(1)}, u32[]{:S(2)}, u32[]{:S(2)}) collective-permute-start(bf16[128,128]{1,0:T(8,128)(2,1)S(1)} %shard_map.109.unread.lower_ref), channel_id=1, source_target_pairs={{0,2},{2,0},{1,3},{3,1},{4,6},{6,4},{5,7},{7,5},{8,10},{10,8},{9,1... | collective-permute-start | bytes 98312 | tf_op jit(solution)/shard_map/ppermute | solution.py:17
  31.1 0.1 fusion
  31.3 0.0 collective-permute-start.10
  31.3 1.0 %shard_map.110 = (bf16[256,2048]{1,0:T(8,128)(2,1)}, f32[8,128]{1,0:T(8,128)S(1)}) custom-call(bf16[256,2048]{1,0:T(8,128)(2,1)S(1)} %shard_map.107.refs_4_.value_ref, bf16[128,128]{1,0:T(8,128)(2,1)S(1)} %shard_map.109.unread.lower_ref), custom_call_target="tpu_custom_call" | custom-call | bytes 2134016 | tf_op jit(solution)/shard_map/pallas_call | solution.py:34
  32.3 1.3 %collective-permute-done.15.under_ref = bf16[128,128]{1,0:T(8,128)(2,1)S(1)} collective-permute-done((bf16[128,128]{1,0:T(8,128)(2,1)S(1)}, bf16[128,128]{1,0:T(8,128)(2,1)S(1)}, u32[]{:S(2)}, u32[]{:S(2)}) %collective-permute-start.15) | collective-permute-done | bytes 32800 | tf_op jit(solution)/shard_map/ppermute | solution.py:17
  33.6 0.0 collective-permute-done.14.over_ref
  33.6 0.1 collective-permute-start.16
  33.7 0.0 collective-permute-done.10
  33.7 0.6 %maximum_select_fusion.1 = bf16[2,128,128]{2,1,0:T(8,128)(2,1)} fusion(bf16[1,128,128]{2,1,0:T(8,128)(2,1)S(1)} %bitcast.36, bf16[1,128,128]{2,1,0:T(8,128)(2,1)S(1)} %bitcast.34, pred[]{:T(512)S(6)} %eq.35), kind=kLoop, calls=%fused_computation.5 | loop fusion | flops 98304 | bytes 131073 | tf_op jit(solution)/shard_map/jit(_where)/select_n | solution.py:351
  34.4 0.7 %collective-permute-done.16 = bf16[512,128]{1,0:T(8,128)(2,1)S(1)} collective-permute-done((bf16[512,128]{1,0:T(8,128)(2,1)S(1)}, bf16[512,128]{1,0:T(8,128)(2,1)S(1)}, u32[]{:S(2)}, u32[]{:S(2)}) %collective-permute-start.16) | collective-permute-done | bytes 131104 | tf_op jit(solution)/shard_map/ppermute | solution.py:17
  35.1 0.9 %copy.11 = f32[8,128,128]{1,2,0:T(8,128)} copy(bf16[8,128,128]{2,1,0:T(8,128)(2,1)S(1)} %bitcast.31) | data formatting | bytes 786432 | tf_op jit(solution)/shard_map/convert_element_type | solution.py:354
  (11 shorter events, 0.2 us)
Async XLA Ops:
  0.6 1.3 %copy-start.2 = (bf16[1,128,128]{2,1,0:T(8,128)(2,1)S(1)}, bf16[1,128,128]{2,1,0:T(8,128)(2,1)}, u32[]{:S(2)}) copy-start(bf16[1,128,128]{2,1,0:T(8,128)(2,1)} %param.10) | copy-start | bytes 98308
  0.6 1.3 %copy-start.3 = (bf16[1,256,128]{2,1,0:T(8,128)(2,1)S(1)}, bf16[1,256,128]{2,1,0:T(8,128)(2,1)}, u32[]{:S(2)}) copy-start(bf16[1,256,128]{2,1,0:T(8,128)(2,1)} %param.11) | copy-start | bytes 196612
  0.7 7.8 %copy-start = (bf16[8,512,128]{2,1,0:T(8,128)(2,1)S(1)}, bf16[8,512,128]{2,1,0:T(8,128)(2,1)}, u32[]{:S(2)}) copy-start(bf16[8,512,128]{2,1,0:T(8,128)(2,1)} %site_ref.3) | copy-start | bytes 3145732
  0.7 7.8 %copy-start.1 = (bf16[1,256,2048]{2,1,0:T(8,128)(2,1)S(1)}, bf16[1,256,2048]{2,1,0:T(8,128)(2,1)}, u32[]{:S(2)}) copy-start(bf16[1,256,2048]{2,1,0:T(8,128)(2,1)} %param.8) | copy-start | bytes 3145732
  0.7 12.2 %collective-permute-start.1 = (bf16[256,2048]{1,0:T(8,128)(2,1)}, bf16[256,2048]{1,0:T(8,128)(2,1)S(1)}, u32[]{:S(2)}, u32[]{:S(2)}) collective-permute-start(bf16[256,2048]{1,0:T(8,128)(2,1)} %bitcast.25), channel_id=1, source_target_pairs={{0,1},{1,0},{2,3},{3,2},{4,5},{5,4},{6,7},{7,6},{8,9},{9,8},{10,11... | collective-permute-start | bytes 3145736 | tf_op jit(solution)/shard_map/ppermute | solution.py:17
  2.1 8.9 %collective-permute-start.5 = (bf16[128,256]{1,0:T(8,128)(2,1)S(1)}, bf16[128,256]{1,0:T(8,128)(2,1)S(1)}, u32[]{:S(2)}, u32[]{:S(2)}) collective-permute-start(bf16[128,256]{1,0:T(8,128)(2,1)S(1)} %get-tuple-element.19.refs_0_), channel_id=1, source_target_pairs={{0,12},{4,8},{8,4},{12,0},{1,13},{5,9},{9,5},{13,1},{2,14},{6,10},... | collective-permute-start | bytes 196616 | tf_op jit(solution)/shard_map/ppermute | solution.py:17
  6.9 6.0 %collective-permute-start.4 = (bf16[128,256]{1,0:T(8,128)(2,1)S(1)}, bf16[128,256]{1,0:T(8,128)(2,1)S(1)}, u32[]{:S(2)}, u32[]{:S(2)}) collective-permute-start(bf16[128,256]{1,0:T(8,128)(2,1)S(1)} %get-tuple-element.19.refs_0_), channel_id=1, source_target_pairs={{0,8},{4,12},{8,0},{12,4},{1,9},{5,13},{9,1},{13,5},{2,10},{6,14},... | collective-permute-start | bytes 196616 | tf_op jit(solution)/shard_map/ppermute | solution.py:17
  6.9 6.0 %collective-permute-start.3 = (bf16[128,256]{1,0:T(8,128)(2,1)S(1)}, bf16[128,256]{1,0:T(8,128)(2,1)S(1)}, u32[]{:S(2)}, u32[]{:S(2)}) collective-permute-start(bf16[128,256]{1,0:T(8,128)(2,1)S(1)} %get-tuple-element.19.refs_0_), channel_id=1, source_target_pairs={{0,4},{4,0},{8,12},{12,8},{1,5},{5,1},{9,13},{13,9},{2,6},{6,2},{1... | collective-permute-start | bytes 196616 | tf_op jit(solution)/shard_map/ppermute | solution.py:17
  7.5 0.7 %copy-start.4 = (s32[64]{0:T(128)S(1)}, s32[64]{0:T(128)}, u32[]{:S(2)}) copy-start(s32[64]{0:T(128)} %param.15) | copy-start | bytes 772
  7.5 0.7 %copy-start.5 = (s32[64]{0:T(128)S(1)}, s32[64]{0:T(128)}, u32[]{:S(2)}) copy-start(s32[64]{0:T(128)} %param.14) | copy-start | bytes 772
  7.5 0.7 %copy-start.6 = (s32[64]{0:T(128)S(1)}, s32[64]{0:T(128)}, u32[]{:S(2)}) copy-start(s32[64]{0:T(128)} %param.13) | copy-start | bytes 772
  8.2 2.1 %collective-permute-start = (s32[64]{0:T(128)S(1)}, s32[64]{0:T(128)S(1)}, u32[]{:S(2)}, u32[]{:S(2)}) collective-permute-start(s32[64]{0:T(128)S(1)} %get-tuple-element.34), channel_id=1, source_target_pairs={{0,1},{1,0},{2,3},{3,2},{4,5},{5,4},{6,7},{7,6},{8,9},{9,8},{10,11... | collective-permute-start | bytes 776 | tf_op jit(solution)/shard_map/ppermute | solution.py:17
  10.3 2.5 %collective-permute-start.2 = (bf16[4,128,128]{2,1,0:T(8,128)(2,1)S(1)}, bf16[4,128,128]{2,1,0:T(8,128)(2,1)S(1)}, u32[]{:S(2)}, u32[]{:S(2)}) collective-permute-start(bf16[4,128,128]{2,1,0:T(8,128)(2,1)S(1)} %get-tuple-element.18), channel_id=1, source_target_pairs={{0,1},{1,0},{2,3},{3,2},{4,5},{5,4},{6,7},{7,6},{8,9},{9,8},{10,11... | collective-permute-start | bytes 393224 | tf_op jit(solution)/shard_map/ppermute | solution.py:17
  14.4 5.9 %collective-permute-start.9 = (bf16[4,128,128]{2,1,0:T(8,128)(2,1)S(1)}, bf16[4,128,128]{2,1,0:T(8,128)(2,1)S(1)}, u32[]{:S(2)}, u32[]{:S(2)}) collective-permute-start(bf16[4,128,128]{2,1,0:T(8,128)(2,1)S(1)} %get-tuple-element.25), channel_id=1, source_target_pairs={{0,2},{2,0},{1,3},{3,1},{4,6},{6,4},{5,7},{7,5},{8,10},{10,8},{9,1... | collective-permute-start | bytes 393224 | tf_op jit(solution)/shard_map/ppermute | solution.py:17
  15.9 7.9 %collective-permute-start.6 = (bf16[384,128]{1,0:T(8,128)(2,1)S(1)}, bf16[384,128]{1,0:T(8,128)(2,1)S(1)}, u32[]{:S(2)}, u32[]{:S(2)}) collective-permute-start(bf16[384,128]{1,0:T(8,128)(2,1)S(1)} %get-tuple-element.21), channel_id=1, source_target_pairs={{0,12},{4,8},{8,4},{12,0},{1,13},{5,9},{9,5},{13,1},{2,14},{6,10},... | collective-permute-start | bytes 294920 | tf_op jit(solution)/shard_map/ppermute | solution.py:17
  18.7 10.1 %collective-permute-start.7 = (bf16[384,128]{1,0:T(8,128)(2,1)S(1)}, bf16[384,128]{1,0:T(8,128)(2,1)S(1)}, u32[]{:S(2)}, u32[]{:S(2)}) collective-permute-start(bf16[384,128]{1,0:T(8,128)(2,1)S(1)} %get-tuple-element.22), channel_id=1, source_target_pairs={{0,8},{4,12},{8,0},{12,4},{1,9},{5,13},{9,1},{13,5},{2,10},{6,14},... | collective-permute-start | bytes 294920 | tf_op jit(solution)/shard_map/ppermute | solution.py:17
  18.7 10.1 %collective-permute-start.8 = (bf16[384,128]{1,0:T(8,128)(2,1)S(1)}, bf16[384,128]{1,0:T(8,128)(2,1)S(1)}, u32[]{:S(2)}, u32[]{:S(2)}) collective-permute-start(bf16[384,128]{1,0:T(8,128)(2,1)S(1)} %get-tuple-element.23), channel_id=1, source_target_pairs={{0,4},{4,0},{8,12},{12,8},{1,5},{5,1},{9,13},{13,9},{2,6},{6,2},{1... | collective-permute-start | bytes 294920 | tf_op jit(solution)/shard_map/ppermute | solution.py:17
  20.4 9.2 %collective-permute-start.13 = (bf16[128,128]{1,0:T(8,128)(2,1)S(1)}, bf16[128,128]{1,0:T(8,128)(2,1)S(1)}, u32[]{:S(2)}, u32[]{:S(2)}) collective-permute-start(bf16[128,128]{1,0:T(8,128)(2,1)S(1)} %get-tuple-element.35), channel_id=1, source_target_pairs={{0,4},{4,0},{8,12},{12,8},{1,5},{5,1},{9,13},{13,9},{2,6},{6,2},{1... | collective-permute-start | bytes 98312 | tf_op jit(solution)/shard_map/ppermute | solution.py:17
  20.9 8.7 %collective-permute-start.12 = (bf16[128,128]{1,0:T(8,128)(2,1)S(1)}, bf16[128,128]{1,0:T(8,128)(2,1)S(1)}, u32[]{:S(2)}, u32[]{:S(2)}) collective-permute-start(bf16[128,128]{1,0:T(8,128)(2,1)S(1)} %get-tuple-element.36), channel_id=1, source_target_pairs={{0,8},{4,12},{8,0},{12,4},{1,9},{5,13},{9,1},{13,5},{2,10},{6,14},... | collective-permute-start | bytes 98312 | tf_op jit(solution)/shard_map/ppermute | solution.py:17
  23.8 5.8 %collective-permute-start.11 = (bf16[128,128]{1,0:T(8,128)(2,1)S(1)}, bf16[128,128]{1,0:T(8,128)(2,1)S(1)}, u32[]{:S(2)}, u32[]{:S(2)}) collective-permute-start(bf16[128,128]{1,0:T(8,128)(2,1)S(1)} %get-tuple-element.37), channel_id=1, source_target_pairs={{0,12},{4,8},{8,4},{12,0},{1,13},{5,9},{9,5},{13,1},{2,14},{6,10},... | collective-permute-start | bytes 98312 | tf_op jit(solution)/shard_map/ppermute | solution.py:17
  28.9 4.7 %collective-permute-start.14 = (bf16[256,128]{1,0:T(8,128)(2,1)S(1)}, bf16[256,128]{1,0:T(8,128)(2,1)S(1)}, u32[]{:S(2)}, u32[]{:S(2)}) collective-permute-start(bf16[256,128]{1,0:T(8,128)(2,1)S(1)} %get-tuple-element.29.upper_ref), channel_id=1, source_target_pairs={{0,2},{2,0},{1,3},{3,1},{4,6},{6,4},{5,7},{7,5},{8,10},{10,8},{9,1... | collective-permute-start | bytes 196616 | tf_op jit(solution)/shard_map/ppermute | solution.py:17
  29.6 4.0 %collective-permute-start.15 = (bf16[128,128]{1,0:T(8,128)(2,1)S(1)}, bf16[128,128]{1,0:T(8,128)(2,1)S(1)}, u32[]{:S(2)}, u32[]{:S(2)}) collective-permute-start(bf16[128,128]{1,0:T(8,128)(2,1)S(1)} %shard_map.109.unread.lower_ref), channel_id=1, source_target_pairs={{0,2},{2,0},{1,3},{3,1},{4,6},{6,4},{5,7},{7,5},{8,10},{10,8},{9,1... | collective-permute-start | bytes 98312 | tf_op jit(solution)/shard_map/ppermute | solution.py:17
  31.3 2.5 %collective-permute-start.10 = (bf16[128,128]{1,0:T(8,128)(2,1)S(1)}, bf16[128,128]{1,0:T(8,128)(2,1)S(1)}, u32[]{:S(2)}, u32[]{:S(2)}) collective-permute-start(bf16[128,128]{1,0:T(8,128)(2,1)S(1)} %fusion), channel_id=1, source_target_pairs={{0,1},{1,0},{2,3},{3,2},{4,5},{5,4},{6,7},{7,6},{8,9},{9,8},{10,11... | collective-permute-start | bytes 98312 | tf_op jit(solution)/shard_map/ppermute | solution.py:17
  33.6 1.4 %collective-permute-start.16 = (bf16[512,128]{1,0:T(8,128)(2,1)S(1)}, bf16[512,128]{1,0:T(8,128)(2,1)S(1)}, u32[]{:S(2)}, u32[]{:S(2)}) collective-permute-start(bf16[512,128]{1,0:T(8,128)(2,1)S(1)} %shard_map.111), channel_id=1, source_target_pairs={{0,1},{1,0},{2,3},{3,2},{4,5},{5,4},{6,7},{7,6},{8,9},{9,8},{10,11... | collective-permute-start | bytes 393224 | tf_op jit(solution)/shard_map/ppermute | solution.py:17

commit v5 on v4

--- a/solution.py
+++ b/solution.py
@@ -112,7 +112,7 @@
 
 
 def site_kernel(
-    owners, subs, blocks, taken, first, own_table, far_table, x_ref, y_ref, keep_ref, got_ref, *refs
+    owners, subs, blocks, taken, first, own_table, far_table, x_ref, y_ref, *refs
 ):
     grads, outs, left_ref = refs[:owners], refs[owners:-1], refs[-1]
     chi, rows = grads[0].shape
@@ -160,9 +160,7 @@
         for at in range(step):
             lanes = slice(at * chunk, (at + 1) * chunk)
             out = outs[rel + at]
-            partial = keep_ref[rel + at] + got_ref[rel + at].astype(F32)
-            out[:straight] = product[:straight, lanes].astype(out.dtype)
-            out[straight:] = partial.astype(BF16).astype(out.dtype)
+            out[...] = product[:straight, lanes].astype(out.dtype)
             crossing[rel + at] = product[straight:middle, lanes].astype(crossing.dtype)
             staying[rel + at] = product[middle:, lanes].astype(staying.dtype)
 
@@ -180,27 +178,33 @@
     return value.astype(BF16)
 
 
-def straight_kernel(*refs):
+def ride_kernel(keep_ref, got_ref, *refs):
+    pieces, outs = refs[: len(refs) // 2], refs[len(refs) // 2 :]
+    straight = pieces[0].shape[0]
+    for at, (piece, out) in enumerate(zip(pieces, outs, strict=True)):
+        out[:straight] = piece[...]
+        out[straight:] = (keep_ref[at] + got_ref[at].astype(F32)).astype(BF16).astype(out.dtype)
+
+
+def sum_kernel(count, *refs):
     out_ref, rest_ref = refs[-2:]
-    value = total(*[ref[...] for ref in refs[:-3]])
-    straight = out_ref.shape[0]
-    out_ref[...] = value[:straight].astype(out_ref.dtype)
-    rest_ref[...] = value[straight:].astype(rest_ref.dtype)
-
-
-def shared_kernel(*refs):
-    refs[-1][...] = total(*[ref[...] for ref in refs[:-1]]).astype(refs[-1].dtype)
-
-
-def share_kernel(parts, upper_ref, over_ref, lower_ref, under_ref, unread, out_ref):
+    upper, lower = [
+        total(*[ref[...] for ref in part]) for part in (refs[:count], refs[count : 2 * count])
+    ]
+    straight = out_ref.shape[0] - lower.shape[0]
+    out_ref[:straight] = upper[:straight].astype(out_ref.dtype)
+    out_ref[straight:] = lower.astype(out_ref.dtype)
+    rest_ref[...] = upper[straight:].astype(rest_ref.dtype)
+
+
+def share_kernel(straight, parts, both_ref, beside_ref, unread, out_ref):
     side = lax.axis_index("block")
-    straight = upper_ref.shape[0]
-    out_ref[:straight] = total(upper_ref[...], over_ref[...]).astype(out_ref.dtype)
-    share = lower_ref.shape[0] // parts
+    out_ref[:straight] = total(both_ref[:straight], beside_ref[:straight]).astype(out_ref.dtype)
+    share = (both_ref.shape[0] - straight) // parts
     for part in range(parts):
-        for ref, slot in ((lower_ref, side), (under_ref, 1 - side)):
+        for ref, slot in ((both_ref, side), (beside_ref, 1 - side)):
             low = pl.multiple_of(straight + (2 * part + slot) * share, share)
-            out_ref[pl.ds(low, share)] = ref[part * share : (part + 1) * share]
+            out_ref[pl.ds(low, share)] = ref[straight + part * share : straight + (part + 1) * share]
 
 
 def corner_kernel(owners, subs, blocks, site_ref, table_ref, *refs):
@@ -242,7 +246,7 @@
     direct = owners * chi == width and sides == 2 and blocks >= 8
     flat = corner[0]
     mine = blocks // 2
-    first = mine // 2
+    first = mine // 4
     part = rows // 2
     chunk = width // owners
     places = owners * subs * blocks
@@ -299,49 +303,52 @@
 
     if direct:
         share = (mine - first) * chi // sides
-        height = first * chi + part
-        outs = [shape((height, chunk), F32)] + [shape((height, chunk), BF16)] * (owners - 1)
+        straight = first * chi
+        types = [F32] + [BF16] * (owners - 1)
+        outs = [shape((straight, chunk), kind) for kind in types]
         outs += [shape((owners, share, chunk), BF16), shape((owners, share, chunk), F32)]
     else:
         outs = [shape((mine * chi, width), F32)]
     pieces = call(
         functools.partial(site_kernel, *sizes, mine, first),
         outs,
-        [near, distant, flat, other, keep, got, *grads],
+        [near, distant, flat, other, *grads],
         [pltpu.VMEM((mine * chi, 2 * subs * rows), BF16)],
         flops=4 * subs * rows * width * chi * mine,
     )
     if direct:
         bits = range(owners - 1, 0, -1)
-        straight = first * chi
         crossed = swap(pieces[owners], "block", 1)
+        merged = total(pieces[owners + 1], crossed)
+        pieces = call(
+            ride_kernel,
+            [shape((straight + part, chunk), kind) for kind in types],
+            [keep, got, *pieces[:owners]],
+        )
         direct_sums = [pieces[0]] + [swap(pieces[bit], "sector", bit) for bit in bits]
-        merged = total(pieces[owners + 1], crossed)
         sent = merged.astype(BF16)
-        shared_sums = [merged[0]] + [swap(sent[bit], "sector", bit) for bit in bits]
+        shared_sums = [merged[0]] + [swap(sent[bit], "sector", bit) for bit in (3, 1, 2)]
         corner_grad = corner_term(sent)
-        upper, enlarged = call(
-            straight_kernel,
-            [shape((straight, chunk), BF16), shape((part, chunk), BF16)],
-            direct_sums,
+        both, enlarged = call(
+            functools.partial(sum_kernel, owners),
+            [shape((straight + share, chunk), BF16), shape((part, chunk), BF16)],
+            [*direct_sums, *shared_sums],
             after=[corner_grad],
         )
-        over = swap(upper, "block", 1)
+        beside = swap(both, "block", 1)
         projected = project(enlarged)
-        lower = call(shared_kernel, [shape((share, chunk), BF16)], shared_sums)[0]
-        under = swap(lower, "block", 1)
         corner_grad, token = call(
             store_kernel,
             [shape(corner_grad.shape, BF16), shape((8, chi), F32)],
             [corner_grad],
             [pltpu.SemaphoreType.DMA],
-            after=[lower],
+            after=[both],
             stores=1,
         )
         own = call(
-            functools.partial(share_kernel, mine - first),
+            functools.partial(share_kernel, straight, mine - first),
             [shape((straight + share * sides, chunk), BF16)],
-            [upper, over, lower, under],
+            [both, beside],
             after=[token],
         )[0]
         projected = [projected, swap(projected, "rep", 1)]

time: 36.2 us -> 35.7 us (0.986)
  starting transfers between devices: 20.6 us -> 19 us
  waiting for transfers between devices: 5.08 us -> 6.21 us
    ppermute x17 -> x16, starting transfers between devices: 20.6 us -> 19 us  [swap(): lax.ppermute(value, axis, [(place, place ^ bit) for place in range(size)])]
    ppermute x17 -> x16, waiting for transfers between devices: 5.08 us -> 6.21 us  [swap(): lax.ppermute(value, axis, [(place, place ^ bit) for place in range(size)])]
  transfers between devices with their start and end apart: 17 -> 16, of which waited for: 4 -> 6; matrix products, arithmetic and copies ran while one was open for 3% -> 3% of each run, Pallas kernels for 12% -> 17%
where the time goes in v5:
time: 35.7 us; the launch traced here: 35.6 us
  starting transfers between devices  19 us (53%)
  waiting for transfers between devices  6.21 us (17%)
  Pallas kernels  5.93 us (17%)
  local copies, waits for them, and re-layouts  1.66 us (5%)
  between operations  1.61 us (5%)
  other arithmetic  0.77 us (2%)
  matrix products  0.39 us (1%)
    ppermute x16, starting transfers between devices, swap(): lax.ppermute(value, axis, [(place, place ^ bit) for place in range(size)])  19 us
    ppermute x16, waiting for transfers between devices, swap(): lax.ppermute(value, axis, [(place, place ^ bit) for place in range(size)])  6.21 us
    pallas_call x9, Pallas kernels, call(): pl.pallas_call(kernel, out_shape=list(outs), in_specs=[scalars if a.ndim...  5.93 us
    convert_element_type x1, local copies, waits for them, and re-layouts, per_device(): ordered([own, there]).reshape(blocks, chi, chunk).swapaxes(1, 2).astype(F32)  0.94 us
  transfers between devices with their start and end apart: 16, of which 6 were waited for; matrix products, arithmetic and copies ran while one was open for 3% of the time, Pallas kernels for 17%

profile of v5, /device:TPU:0, one launch (start us, length us, event | category | flops | bytes accessed | tf_op | source)
XLA Modules:
  0.0 35.6 jit_solution(3455171955197833723)
XLA Ops:
  0.6 0.0 copy-start.2
  0.6 0.0 copy-start.3
  0.7 0.0 copy-start
  0.7 0.0 copy-start.1
  0.7 0.5 %collective-permute-start.2 = (bf16[256,2048]{1,0:T(8,128)(2,1)}, bf16[256,2048]{1,0:T(8,128)(2,1)S(1)}, u32[]{:S(2)}, u32[]{:S(2)}) collective-permute-start(bf16[256,2048]{1,0:T(8,128)(2,1)} %bitcast.25), channel_id=1, source_target_pairs={{0,1},{1,0},{2,3},{3,2},{4,5},{5,4},{6,7},{7,6},{8,9},{9,8},{10,11... | collective-permute-start | bytes 3145736 | tf_op jit(solution)/shard_map/ppermute | solution.py:17
  2.0 0.0 copy-done.2
  2.0 0.0 copy-done.3
  2.0 0.2 shard_map.105
  2.1 2.7 %collective-permute-start.3 = (bf16[128,256]{1,0:T(8,128)(2,1)S(1)}, bf16[128,256]{1,0:T(8,128)(2,1)S(1)}, u32[]{:S(2)}, u32[]{:S(2)}) collective-permute-start(bf16[128,256]{1,0:T(8,128)(2,1)S(1)} %get-tuple-element.23.refs_0_), channel_id=1, source_target_pairs={{0,4},{4,0},{8,12},{12,8},{1,5},{5,1},{9,13},{13,9},{2,6},{6,2},{1... | collective-permute-start | bytes 196616 | tf_op jit(solution)/shard_map/ppermute | solution.py:17
  4.8 2.6 %collective-permute-start.4 = (bf16[128,256]{1,0:T(8,128)(2,1)S(1)}, bf16[128,256]{1,0:T(8,128)(2,1)S(1)}, u32[]{:S(2)}, u32[]{:S(2)}) collective-permute-start(bf16[128,256]{1,0:T(8,128)(2,1)S(1)} %get-tuple-element.23.refs_0_), channel_id=1, source_target_pairs={{0,8},{4,12},{8,0},{12,4},{1,9},{5,13},{9,1},{13,5},{2,10},{6,14},... | collective-permute-start | bytes 196616 | tf_op jit(solution)/shard_map/ppermute | solution.py:17
  7.4 0.0 collective-permute-start.5
  7.4 0.0 copy-start.4
  7.4 0.0 copy-start.5
  7.4 0.0 copy-start.6
  7.4 0.6 %copy-done.4 = s32[64]{0:T(128)S(1)} copy-done((s32[64]{0:T(128)S(1)}, s32[64]{0:T(128)}, u32[]{:S(2)}) %copy-start.4) | copy-done | bytes 280
  8.1 0.0 copy-done.5
  8.1 0.0 copy-done.6
  8.1 0.1 collective-permute-start.1
  8.2 0.1 fusion.1.table_ref.own_table
  8.4 0.0 copy-done
  8.4 0.0 copy-done.1
  8.4 1.9 %shard_map.103 = (f32[4,128,128]{2,1,0:T(8,128)S(1)}, bf16[4,128,128]{2,1,0:T(8,128)(2,1)S(1)}) custom-call(f32[128,128]{1,0:T(8,128)S(1)} %fusion.1.table_ref.own_table, bf16[256,2048]{1,0:T(8,128)(2,1)S(1)} %bitcast.26, bf16[8,512,128]{2,1,0:T(8,128)(2,1)S(1)} %copy-done.1), custom_call_target="tpu_custom_call" | custom-call | bytes 2555904 | tf_op jit(solution)/shard_map/pallas_call | solution.py:34
  10.2 0.0 collective-permute-done.1
  10.3 0.6 %collective-permute-start = (bf16[4,128,128]{2,1,0:T(8,128)(2,1)S(1)}, bf16[4,128,128]{2,1,0:T(8,128)(2,1)S(1)}, u32[]{:S(2)}, u32[]{:S(2)}) collective-permute-start(bf16[4,128,128]{2,1,0:T(8,128)(2,1)S(1)} %get-tuple-element.22), channel_id=1, source_target_pairs={{0,1},{1,0},{2,3},{3,2},{4,5},{5,4},{6,7},{7,6},{8,9},{9,8},{10,11... | collective-permute-start | bytes 393224 | tf_op jit(solution)/shard_map/ppermute | solution.py:17
  10.8 0.1 fusion.2.far_table
  11.0 0.0 collective-permute-done.3.refs_1_
  11.0 1.5 %collective-permute-done.4.refs_2_ = bf16[128,256]{1,0:T(8,128)(2,1)S(1)} collective-permute-done((bf16[128,256]{1,0:T(8,128)(2,1)S(1)}, bf16[128,256]{1,0:T(8,128)(2,1)S(1)}, u32[]{:S(2)}, u32[]{:S(2)}) %collective-permute-start.4) | collective-permute-done | bytes 65568 | tf_op jit(solution)/shard_map/ppermute | solution.py:17
  12.5 1.1 %collective-permute-done.5.refs_3_ = bf16[128,256]{1,0:T(8,128)(2,1)S(1)} collective-permute-done((bf16[128,256]{1,0:T(8,128)(2,1)S(1)}, bf16[128,256]{1,0:T(8,128)(2,1)S(1)}, u32[]{:S(2)}, u32[]{:S(2)}) %collective-permute-start.5) | collective-permute-done | bytes 65568 | tf_op jit(solution)/shard_map/ppermute | solution.py:17
  13.5 0.0 collective-permute-done.2.y_ref
  13.5 1.5 %shard_map.106 = (f32[128,128]{1,0:T(8,128)S(1)}, bf16[128,128]{1,0:T(8,128)(2,1)S(1)}, bf16[128,128]{1,0:T(8,128)(2,1)S(1)}, bf16[128,128]{1,0:T(8,128)(2,1)S(1...) custom-call(f32[128,128]{1,0:T(8,128)S(1)} %fusion.1.table_ref.own_table, ...), custom_call_target="tpu_custom_call" | custom-call | bytes 3244032 | tf_op jit(solution)/shard_map/pallas_call | solution.py:34
  15.0 1.6 %collective-permute-start.9 = (bf16[4,192,128]{2,1,0:T(8,128)(2,1)S(1)}, bf16[4,192,128]{2,1,0:T(8,128)(2,1)S(1)}, u32[]{:S(2)}, u32[]{:S(2)}) collective-permute-start(bf16[4,192,128]{2,1,0:T(8,128)(2,1)S(1)} %get-tuple-element.33), channel_id=1, source_target_pairs={{0,2},{2,0},{1,3},{3,1},{4,6},{6,4},{5,7},{7,5},{8,10},{10,8},{9,1... | collective-permute-start | bytes 589832 | tf_op jit(solution)/shard_map/ppermute | solution.py:17
  16.6 0.0 collective-permute-done.got_ref
  16.6 2.3 %collective-permute-start.6 = (bf16[256,128]{1,0:T(8,128)(2,1)S(1)}, bf16[256,128]{1,0:T(8,128)(2,1)S(1)}, u32[]{:S(2)}, u32[]{:S(2)}) collective-permute-start(bf16[256,128]{1,0:T(8,128)(2,1)S(1)} %get-tuple-element.29), channel_id=1, source_target_pairs={{0,12},{4,8},{8,4},{12,0},{1,13},{5,9},{9,5},{13,1},{2,14},{6,10},... | collective-permute-start | bytes 196616 | tf_op jit(solution)/shard_map/ppermute | solution.py:17
  18.9 0.3 collective-permute-start.7
  19.3 1.8 %collective-permute-start.8 = (bf16[256,128]{1,0:T(8,128)(2,1)S(1)}, bf16[256,128]{1,0:T(8,128)(2,1)S(1)}, u32[]{:S(2)}, u32[]{:S(2)}) collective-permute-start(bf16[256,128]{1,0:T(8,128)(2,1)S(1)} %get-tuple-element.31), channel_id=1, source_target_pairs={{0,4},{4,0},{8,12},{12,8},{1,5},{5,1},{9,13},{13,9},{2,6},{6,2},{1... | collective-permute-start | bytes 196616 | tf_op jit(solution)/shard_map/ppermute | solution.py:17
  21.1 0.0 collective-permute-done.9
  21.1 0.1 fusion.16
  21.2 2.3 %collective-permute-start.10 = (bf16[192,128]{1,0:T(8,128)(2,1)S(1)}, bf16[192,128]{1,0:T(8,128)(2,1)S(1)}, u32[]{:S(2)}, u32[]{:S(2)}) collective-permute-start(bf16[192,128]{1,0:T(8,128)(2,1)S(1)} %get-tuple-element.45), channel_id=1, source_target_pairs={{0,12},{4,8},{8,4},{12,0},{1,13},{5,9},{9,5},{13,1},{2,14},{6,10},... | collective-permute-start | bytes 147464 | tf_op jit(solution)/shard_map/ppermute | solution.py:17
  23.5 0.1 collective-permute-start.11
  23.6 0.0 collective-permute-done.6.refs_1_
  23.6 2.5 %collective-permute-start.12 = (bf16[192,128]{1,0:T(8,128)(2,1)S(1)}, bf16[192,128]{1,0:T(8,128)(2,1)S(1)}, u32[]{:S(2)}, u32[]{:S(2)}) collective-permute-start(bf16[192,128]{1,0:T(8,128)(2,1)S(1)} %get-tuple-element.43), channel_id=1, source_target_pairs={{0,8},{4,12},{8,0},{12,4},{1,9},{5,13},{9,1},{13,5},{2,10},{6,14},... | collective-permute-start | bytes 147464 | tf_op jit(solution)/shard_map/ppermute | solution.py:17
  26.1 1.3 %shard_map.108.refs_8_.value_ref = bf16[256,2048]{1,0:T(8,128)(2,1)S(1)} custom-call(bf16[8,512,128]{2,1,0:T(8,128)(2,1)S(1)} %copy-done.1, f32[128,128]{1,0:T(8,128)S(1)} %fusion.1.table_ref.own_table, bf16[128,256]{1,0:T(8,128)(2,1)S(1)} %get-tuple-element.23.refs_0_, bf16[128,256]{1,0:T(8,128)(2,1)S(1)} %collective-permute-done.3.refs_1_, ...), custom_call_target="tpu_custom_call" | custom-call | bytes 2621440 | tf_op jit(solution)/shard_map/pallas_call | solution.py:34
  27.4 0.0 collective-permute-done.7.refs_2_
  27.4 0.0 collective-permute-done.8.refs_3_
  27.4 0.0 collective-permute-done.10.refs_5_
  27.4 0.6 %collective-permute-done.11.refs_6_ = bf16[192,128]{1,0:T(8,128)(2,1)S(1)} collective-permute-done((bf16[192,128]{1,0:T(8,128)(2,1)S(1)}, bf16[192,128]{1,0:T(8,128)(2,1)S(1)}, u32[]{:S(2)}, u32[]{:S(2)}) %collective-permute-start.11) | collective-permute-done | bytes 49184 | tf_op jit(solution)/shard_map/ppermute | solution.py:17
  28.0 0.6 %collective-permute-done.12.refs_7_ = bf16[192,128]{1,0:T(8,128)(2,1)S(1)} collective-permute-done((bf16[192,128]{1,0:T(8,128)(2,1)S(1)}, bf16[192,128]{1,0:T(8,128)(2,1)S(1)}, u32[]{:S(2)}, u32[]{:S(2)}) %collective-permute-start.12) | collective-permute-done | bytes 49184 | tf_op jit(solution)/shard_map/ppermute | solution.py:17
  28.6 0.1 shard_map.109
  28.6 1.6 %collective-permute-start.14 = (bf16[320,128]{1,0:T(8,128)(2,1)S(1)}, bf16[320,128]{1,0:T(8,128)(2,1)S(1)}, u32[]{:S(2)}, u32[]{:S(2)}) collective-permute-start(bf16[320,128]{1,0:T(8,128)(2,1)S(1)} %get-tuple-element.36.unread.both_ref), channel_id=1, source_target_pairs={{0,2},{2,0},{1,3},{3,1},{4,6},{6,4},{5,7},{7,5},{8,10},{10,8},{9,1... | collective-permute-start | bytes 245768 | tf_op jit(solution)/shard_map/ppermute | solution.py:17
  30.2 0.1 fusion
  30.3 0.0 collective-permute-start.13
  30.4 1.0 %shard_map.110 = (bf16[256,2048]{1,0:T(8,128)(2,1)}, f32[8,128]{1,0:T(8,128)S(1)}) custom-call(bf16[256,2048]{1,0:T(8,128)(2,1)S(1)} %shard_map.108.refs_8_.value_ref, bf16[320,128]{1,0:T(8,128)(2,1)S(1)} %get-tuple-element.36.unread.both_ref), custom_call_target="tpu_custom_call" | custom-call | bytes 2183168 | tf_op jit(solution)/shard_map/pallas_call | solution.py:34
  31.4 1.8 %collective-permute-done.14.beside_ref = bf16[320,128]{1,0:T(8,128)(2,1)S(1)} collective-permute-done((bf16[320,128]{1,0:T(8,128)(2,1)S(1)}, bf16[320,128]{1,0:T(8,128)(2,1)S(1)}, u32[]{:S(2)}, u32[]{:S(2)}) %collective-permute-start.14) | collective-permute-done | bytes 81952 | tf_op jit(solution)/shard_map/ppermute | solution.py:17
  33.2 0.1 collective-permute-start.15
  33.3 0.0 collective-permute-done.13
  33.3 0.6 %maximum_select_fusion.1 = bf16[2,128,128]{2,1,0:T(8,128)(2,1)} fusion(bf16[1,128,128]{2,1,0:T(8,128)(2,1)S(1)} %bitcast.36, bf16[1,128,128]{2,1,0:T(8,128)(2,1)S(1)} %bitcast.34, pred[]{:T(512)S(6)} %eq.35), kind=kLoop, calls=%fused_computation.5 | loop fusion | flops 98304 | bytes 131073 | tf_op jit(solution)/shard_map/jit(_where)/select_n | solution.py:358
  33.9 0.7 %collective-permute-done.15 = bf16[512,128]{1,0:T(8,128)(2,1)S(1)} collective-permute-done((bf16[512,128]{1,0:T(8,128)(2,1)S(1)}, bf16[512,128]{1,0:T(8,128)(2,1)S(1)}, u32[]{:S(2)}, u32[]{:S(2)}) %collective-permute-start.15) | collective-permute-done | bytes 131104 | tf_op jit(solution)/shard_map/ppermute | solution.py:17
  34.6 0.9 %copy.11 = f32[8,128,128]{1,2,0:T(8,128)} copy(bf16[8,128,128]{2,1,0:T(8,128)(2,1)S(1)} %bitcast.31) | data formatting | bytes 786432 | tf_op jit(solution)/shard_map/convert_element_type | solution.py:361
  (9 shorter events, 0.1 us)
Async XLA Ops:
  0.6 1.3 %copy-start.2 = (bf16[1,128,128]{2,1,0:T(8,128)(2,1)S(1)}, bf16[1,128,128]{2,1,0:T(8,128)(2,1)}, u32[]{:S(2)}) copy-start(bf16[1,128,128]{2,1,0:T(8,128)(2,1)} %param.10) | copy-start | bytes 98308
  0.6 1.3 %copy-start.3 = (bf16[1,256,128]{2,1,0:T(8,128)(2,1)S(1)}, bf16[1,256,128]{2,1,0:T(8,128)(2,1)}, u32[]{:S(2)}) copy-start(bf16[1,256,128]{2,1,0:T(8,128)(2,1)} %param.11) | copy-start | bytes 196612
  0.7 7.7 %copy-start = (bf16[1,256,2048]{2,1,0:T(8,128)(2,1)S(1)}, bf16[1,256,2048]{2,1,0:T(8,128)(2,1)}, u32[]{:S(2)}) copy-start(bf16[1,256,2048]{2,1,0:T(8,128)(2,1)} %param.8) | copy-start | bytes 3145732
  0.7 7.7 %copy-start.1 = (bf16[8,512,128]{2,1,0:T(8,128)(2,1)S(1)}, bf16[8,512,128]{2,1,0:T(8,128)(2,1)}, u32[]{:S(2)}) copy-start(bf16[8,512,128]{2,1,0:T(8,128)(2,1)} %site_ref.3) | copy-start | bytes 3145732
  0.7 12.9 %collective-permute-start.2 = (bf16[256,2048]{1,0:T(8,128)(2,1)}, bf16[256,2048]{1,0:T(8,128)(2,1)S(1)}, u32[]{:S(2)}, u32[]{:S(2)}) collective-permute-start(bf16[256,2048]{1,0:T(8,128)(2,1)} %bitcast.25), channel_id=1, source_target_pairs={{0,1},{1,0},{2,3},{3,2},{4,5},{5,4},{6,7},{7,6},{8,9},{9,8},{10,11... | collective-permute-start | bytes 3145736 | tf_op jit(solution)/shard_map/ppermute | solution.py:17
  2.1 8.8 %collective-permute-start.3 = (bf16[128,256]{1,0:T(8,128)(2,1)S(1)}, bf16[128,256]{1,0:T(8,128)(2,1)S(1)}, u32[]{:S(2)}, u32[]{:S(2)}) collective-permute-start(bf16[128,256]{1,0:T(8,128)(2,1)S(1)} %get-tuple-element.23.refs_0_), channel_id=1, source_target_pairs={{0,4},{4,0},{8,12},{12,8},{1,5},{5,1},{9,13},{13,9},{2,6},{6,2},{1... | collective-permute-start | bytes 196616 | tf_op jit(solution)/shard_map/ppermute | solution.py:17
  4.8 7.7 %collective-permute-start.4 = (bf16[128,256]{1,0:T(8,128)(2,1)S(1)}, bf16[128,256]{1,0:T(8,128)(2,1)S(1)}, u32[]{:S(2)}, u32[]{:S(2)}) collective-permute-start(bf16[128,256]{1,0:T(8,128)(2,1)S(1)} %get-tuple-element.23.refs_0_), channel_id=1, source_target_pairs={{0,8},{4,12},{8,0},{12,4},{1,9},{5,13},{9,1},{13,5},{2,10},{6,14},... | collective-permute-start | bytes 196616 | tf_op jit(solution)/shard_map/ppermute | solution.py:17
  7.4 6.1 %collective-permute-start.5 = (bf16[128,256]{1,0:T(8,128)(2,1)S(1)}, bf16[128,256]{1,0:T(8,128)(2,1)S(1)}, u32[]{:S(2)}, u32[]{:S(2)}) collective-permute-start(bf16[128,256]{1,0:T(8,128)(2,1)S(1)} %get-tuple-element.23.refs_0_), channel_id=1, source_target_pairs={{0,12},{4,8},{8,4},{12,0},{1,13},{5,9},{9,5},{13,1},{2,14},{6,10},... | collective-permute-start | bytes 196616 | tf_op jit(solution)/shard_map/ppermute | solution.py:17
  7.4 0.7 %copy-start.4 = (s32[64]{0:T(128)S(1)}, s32[64]{0:T(128)}, u32[]{:S(2)}) copy-start(s32[64]{0:T(128)} %param.15) | copy-start | bytes 772
  7.4 0.7 %copy-start.5 = (s32[64]{0:T(128)S(1)}, s32[64]{0:T(128)}, u32[]{:S(2)}) copy-start(s32[64]{0:T(128)} %param.14) | copy-start | bytes 772
  7.4 0.7 %copy-start.6 = (s32[64]{0:T(128)S(1)}, s32[64]{0:T(128)}, u32[]{:S(2)}) copy-start(s32[64]{0:T(128)} %param.13) | copy-start | bytes 772
  8.1 2.1 %collective-permute-start.1 = (s32[64]{0:T(128)S(1)}, s32[64]{0:T(128)S(1)}, u32[]{:S(2)}, u32[]{:S(2)}) collective-permute-start(s32[64]{0:T(128)S(1)} %get-tuple-element.42), channel_id=1, source_target_pairs={{0,1},{1,0},{2,3},{3,2},{4,5},{5,4},{6,7},{7,6},{8,9},{9,8},{10,11... | collective-permute-start | bytes 776 | tf_op jit(solution)/shard_map/ppermute | solution.py:17
  10.3 6.3 %collective-permute-start = (bf16[4,128,128]{2,1,0:T(8,128)(2,1)S(1)}, bf16[4,128,128]{2,1,0:T(8,128)(2,1)S(1)}, u32[]{:S(2)}, u32[]{:S(2)}) collective-permute-start(bf16[4,128,128]{2,1,0:T(8,128)(2,1)S(1)} %get-tuple-element.22), channel_id=1, source_target_pairs={{0,1},{1,0},{2,3},{3,2},{4,5},{5,4},{6,7},{7,6},{8,9},{9,8},{10,11... | collective-permute-start | bytes 393224 | tf_op jit(solution)/shard_map/ppermute | solution.py:17
  15.0 6.1 %collective-permute-start.9 = (bf16[4,192,128]{2,1,0:T(8,128)(2,1)S(1)}, bf16[4,192,128]{2,1,0:T(8,128)(2,1)S(1)}, u32[]{:S(2)}, u32[]{:S(2)}) collective-permute-start(bf16[4,192,128]{2,1,0:T(8,128)(2,1)S(1)} %get-tuple-element.33), channel_id=1, source_target_pairs={{0,2},{2,0},{1,3},{3,1},{4,6},{6,4},{5,7},{7,5},{8,10},{10,8},{9,1... | collective-permute-start | bytes 589832 | tf_op jit(solution)/shard_map/ppermute | solution.py:17
  16.6 7.0 %collective-permute-start.6 = (bf16[256,128]{1,0:T(8,128)(2,1)S(1)}, bf16[256,128]{1,0:T(8,128)(2,1)S(1)}, u32[]{:S(2)}, u32[]{:S(2)}) collective-permute-start(bf16[256,128]{1,0:T(8,128)(2,1)S(1)} %get-tuple-element.29), channel_id=1, source_target_pairs={{0,12},{4,8},{8,4},{12,0},{1,13},{5,9},{9,5},{13,1},{2,14},{6,10},... | collective-permute-start | bytes 196616 | tf_op jit(solution)/shard_map/ppermute | solution.py:17
  18.9 8.5 %collective-permute-start.7 = (bf16[256,128]{1,0:T(8,128)(2,1)S(1)}, bf16[256,128]{1,0:T(8,128)(2,1)S(1)}, u32[]{:S(2)}, u32[]{:S(2)}) collective-permute-start(bf16[256,128]{1,0:T(8,128)(2,1)S(1)} %get-tuple-element.30), channel_id=1, source_target_pairs={{0,8},{4,12},{8,0},{12,4},{1,9},{5,13},{9,1},{13,5},{2,10},{6,14},... | collective-permute-start | bytes 196616 | tf_op jit(solution)/shard_map/ppermute | solution.py:17
  19.3 8.1 %collective-permute-start.8 = (bf16[256,128]{1,0:T(8,128)(2,1)S(1)}, bf16[256,128]{1,0:T(8,128)(2,1)S(1)}, u32[]{:S(2)}, u32[]{:S(2)}) collective-permute-start(bf16[256,128]{1,0:T(8,128)(2,1)S(1)} %get-tuple-element.31), channel_id=1, source_target_pairs={{0,4},{4,0},{8,12},{12,8},{1,5},{5,1},{9,13},{13,9},{2,6},{6,2},{1... | collective-permute-start | bytes 196616 | tf_op jit(solution)/shard_map/ppermute | solution.py:17
  21.2 6.3 %collective-permute-start.10 = (bf16[192,128]{1,0:T(8,128)(2,1)S(1)}, bf16[192,128]{1,0:T(8,128)(2,1)S(1)}, u32[]{:S(2)}, u32[]{:S(2)}) collective-permute-start(bf16[192,128]{1,0:T(8,128)(2,1)S(1)} %get-tuple-element.45), channel_id=1, source_target_pairs={{0,12},{4,8},{8,4},{12,0},{1,13},{5,9},{9,5},{13,1},{2,14},{6,10},... | collective-permute-start | bytes 147464 | tf_op jit(solution)/shard_map/ppermute | solution.py:17
  23.5 4.6 %collective-permute-start.11 = (bf16[192,128]{1,0:T(8,128)(2,1)S(1)}, bf16[192,128]{1,0:T(8,128)(2,1)S(1)}, u32[]{:S(2)}, u32[]{:S(2)}) collective-permute-start(bf16[192,128]{1,0:T(8,128)(2,1)S(1)} %get-tuple-element.44), channel_id=1, source_target_pairs={{0,4},{4,0},{8,12},{12,8},{1,5},{5,1},{9,13},{13,9},{2,6},{6,2},{1... | collective-permute-start | bytes 147464 | tf_op jit(solution)/shard_map/ppermute | solution.py:17
  23.6 5.0 %collective-permute-start.12 = (bf16[192,128]{1,0:T(8,128)(2,1)S(1)}, bf16[192,128]{1,0:T(8,128)(2,1)S(1)}, u32[]{:S(2)}, u32[]{:S(2)}) collective-permute-start(bf16[192,128]{1,0:T(8,128)(2,1)S(1)} %get-tuple-element.43), channel_id=1, source_target_pairs={{0,8},{4,12},{8,0},{12,4},{1,9},{5,13},{9,1},{13,5},{2,10},{6,14},... | collective-permute-start | bytes 147464 | tf_op jit(solution)/shard_map/ppermute | solution.py:17
  28.6 4.5 %collective-permute-start.14 = (bf16[320,128]{1,0:T(8,128)(2,1)S(1)}, bf16[320,128]{1,0:T(8,128)(2,1)S(1)}, u32[]{:S(2)}, u32[]{:S(2)}) collective-permute-start(bf16[320,128]{1,0:T(8,128)(2,1)S(1)} %get-tuple-element.36.unread.both_ref), channel_id=1, source_target_pairs={{0,2},{2,0},{1,3},{3,1},{4,6},{6,4},{5,7},{7,5},{8,10},{10,8},{9,1... | collective-permute-start | bytes 245768 | tf_op jit(solution)/shard_map/ppermute | solution.py:17
  30.3 2.9 %collective-permute-start.13 = (bf16[128,128]{1,0:T(8,128)(2,1)S(1)}, bf16[128,128]{1,0:T(8,128)(2,1)S(1)}, u32[]{:S(2)}, u32[]{:S(2)}) collective-permute-start(bf16[128,128]{1,0:T(8,128)(2,1)S(1)} %fusion), channel_id=1, source_target_pairs={{0,1},{1,0},{2,3},{3,2},{4,5},{5,4},{6,7},{7,6},{8,9},{9,8},{10,11... | collective-permute-start | bytes 98312 | tf_op jit(solution)/shard_map/ppermute | solution.py:17
  33.2 1.4 %collective-permute-start.15 = (bf16[512,128]{1,0:T(8,128)(2,1)S(1)}, bf16[512,128]{1,0:T(8,128)(2,1)S(1)}, u32[]{:S(2)}, u32[]{:S(2)}) collective-permute-start(bf16[512,128]{1,0:T(8,128)(2,1)S(1)} %shard_map.111), channel_id=1, source_target_pairs={{0,1},{1,0},{2,3},{3,2},{4,5},{5,4},{6,7},{7,6},{8,9},{9,8},{10,11... | collective-permute-start | bytes 393224 | tf_op jit(solution)/shard_map/ppermute | solution.py:17
